TPU v7x, 32 devices: a whole 2x2x4 slice. The times are simulated.
32 devices in a mesh: band: 4 (over z), dev: 8 (over y, x, core).
Axes of the slice: x: 2, y: 2, z: 4, core: 2. Of those that a mesh axis runs over, the one named last changes fastest.
Arguments:
- anomaly: float32 [256, 131072], P('dev', 'band'), may hold values from -6 to 6
- ocean_mask: int32 [131072], P('band'), may hold values 0 or 1
- area_weight: float32 [131072], P('band'), may hold values from 0.02 to 1
Outputs:
- factor: float32 [256, 256], replicated
- scores: float32 [256, 131072], P(None, ('band', 'dev'))
All inputs are finite; a program needn't handle non-finite values. No bound on the sum of `ocean_mask` on one device may be relied on, other than what follows from the above.
Results may differ from a plain program's by a relative error of at most 0.000075.
Values sent between devices are 32-bit elements; how exact they have to be, the bound alone decides.
No kernel may reach another device: no remote copies, remote signals or barrier semaphores. Data moves between devices by JAX's collectives and lax.ppermute only.
A program may use at most 64 MiB of HBM per device.

v0:
```python
import jax
import jax.numpy as jnp
from jax import lax
from jax.sharding import PartitionSpec as P


def on_device(anomaly, ocean_mask, area_weight):
    weights = area_weight * ocean_mask.astype(jnp.float32)
    local_scaled = anomaly * jnp.sqrt(weights)[None, :]
    group_size = lax.axis_size("dev")
    own_cells = weights.shape[0] // group_size
    own_weights = lax.dynamic_slice_in_dim(weights, lax.axis_index("dev") * own_cells, own_cells, 0)
    partial_total = jnp.sum(own_weights)
    scaled = lax.all_to_all(local_scaled, "dev", split_axis=1, concat_axis=0, tiled=True)
    partial_gram = jnp.dot(scaled, scaled.T, precision=lax.Precision.HIGHEST)
    band_gram, band_total = lax.psum((partial_gram, partial_total), "dev")
    gram, total = lax.psum((band_gram, band_total), "band")
    lower = jnp.linalg.cholesky(gram / total)
    scores = lax.linalg.triangular_solve(lower, scaled, left_side=True, lower=True)
    return (lower.T, scores)


def solution(mesh):
    return jax.shard_map(
        on_device,
        mesh=mesh,
        in_specs=(P("dev", "band"), P("band"), P("band")),
        out_specs=(P(), P(None, ("band", "dev"))),
        check_vma=False,
    )
```

profile of v0, /device:TPU:0, one launch (start us, length us, event | category | flops | bytes accessed | tf_op | source)
XLA Modules:
  0.0 242.3 jit_solution(10001902621968987980)
XLA Ops:
  7.2 1.0 fusion.9
  8.2 2.5 %broadcast_multiply_fusion = f32[32,32768]{1,0:T(8,128)S(1)} fusion(f32[32,32768]{1,0:T(8,128)} %param.3, f32[32768]{0:T(1024)S(1)} %get-tuple-element.26), kind=kLoop, calls=%fused_computation.5 | loop fusion | flops 1048576 | bytes 8519680 | tf_op jit(solution)/shard_map/mul | solution.py:9
  11.2 54.0 %all_to_all.19 = f32[32,8,4096]{2,0,1:T(8,128)S(1)} all-to-all(f32[32,8,4096]{2,0,1:T(8,128)S(1)} %bitcast.48), channel_id=1, replica_groups=mesh['band'=4,'dev'=8] {'dev'}, dimensions={1} | all-to-all | bytes 8388608 | tf_op jit(solution)/shard_map/all_to_all | solution.py:14
  65.2 2.0 copy-done
  67.2 4.2 %fusion.12 = f32[256,256]{0,1:T(8,128)} fusion(f32[256,4096]{1,0:T(8,128)S(1)} %bitcast.45), kind=kOutput, calls=%fused_computation.37 | convolution fusion | flops 3221225472 | bytes 4456448 | tf_op jit(solution)/shard_map/dot_general | solution.py:15
  72.2 12.6 %psum.30 = f32[]{:T(128)} all-reduce(f32[]{:T(128)} %dynamic-slice_reduce_fusion), channel_id=1, replica_groups=mesh['band'=4,'dev'=8] {'dev'}, use_global_device_ids=true, to_apply=%region_3.0 | all-reduce | flops 1 | bytes 8 | tf_op jit(solution)/shard_map/psum | solution.py:16
  84.8 12.8 %psum.31 = f32[]{:T(128)} all-reduce(f32[]{:T(128)} %psum.30), channel_id=1, replica_groups=mesh['band'=4,'dev'=8] {'band'}, use_global_device_ids=true, to_apply=%region_4.0 | all-reduce | flops 1 | bytes 8 | tf_op jit(solution)/shard_map/psum | solution.py:17
  97.6 26.9 %all-reduce.4.cloned.1.call-done = f32[256,256]{0,1:T(8,128)} async-done(((f32[256,256]{0,1:T(8,128)}), f32[256,256]{0,1:T(8,128)}) %all-reduce.4.cloned.1.call-update) | async-done | bytes 262160 | tf_op jit(solution)/shard_map/psum | solution.py:16
  124.5 4.0 %fusion.11 = (f32[4,32,4096]{2,1,0:T(8,128)}, f32[4,32,4096]{2,1,0:T(8,128)S(1)}) fusion(f32[8,32,4096]{2,1,0:T(8,128)} %bitcast.46), kind=kLoop, calls=%fused_computation.36 | loop fusion | bytes 8388608 | tf_op jit(solution)/shard_map/triangular_solve | solution.py:19
  128.6 33.1 %all-reduce.6.cloned.1.call-done = f32[256,256]{0,1:T(8,128)} async-done(((f32[256,256]{0,1:T(8,128)}), f32[256,256]{0,1:T(8,128)}) %all-reduce.6.cloned.1.call-update) | async-done | bytes 262160 | tf_op jit(solution)/shard_map/psum | solution.py:17
  161.7 1.6 broadcast_divide_fusion
  163.4 1.6 fusion
  165.0 11.7 %cholesky.50 = f32[128,128]{1,0:T(8,128)S(1)} custom-call(f32[128,128]{1,0:T(8,128)S(1)} %cholesky.118), custom_call_target="Cholesky" | custom-call | tf_op jit(solution)/shard_map/jit(cholesky)/cholesky | solution.py:18
  176.8 9.8 %custom-call.14 = f32[1,128,128]{1,2,0:T(8,128)S(1)} custom-call(f32[1,128,128]{2,1,0:T(8,128)S(1)} %get-tuple-element.37), custom_call_target="InvertDiagBlocksLowerTriangular" | custom-call | tf_op jit(solution)/shard_map/jit(cholesky)/cholesky | solution.py:18
  187.1 11.7 %cholesky.105 = f32[128,128]{1,0:T(8,128)S(1)} custom-call(f32[128,128]{1,0:T(8,128)S(1)} %convolution_subtract_fusion.1), custom_call_target="Cholesky" | custom-call | tf_op jit(solution)/shard_map/jit(cholesky)/cholesky | solution.py:18
  200.9 0.8 copy.20
  201.8 3.9 %while.1 = (s32[]{:T(128)}, f32[256,256]{1,0:T(8,128)S(1)}, s32[2,2]{1,0:T(2,128)S(1)}, f32[2,128,128]{2,1,0:T(8,128)S(1)}, s32[]{:T(128)}) while((s32[]{:T(128)}, f32[256,256]{1,0:T(8,128)S(1)}, s32[2,2]{1,0:T(2,128)S(1)}, f32[2,128,128]{2,1,0:T(8,128)S(1)}, s32[]{:T(128)}) %tuple.34), condition=%wide.while_cond, body=%wide.while_body.sunk | while | flops 2 | bytes 131189 | solution.py:19
  202.4 1.4 bitcast_dynamic-update-slice_fusion.2
  204.3 1.4 bitcast_dynamic-update-slice_fusion.2
  205.7 19.9 %custom-call.15 = f32[2,128,128]{1,2,0:T(8,128)S(1)} custom-call(f32[2,128,128]{2,1,0:T(8,128)S(1)} %get-tuple-element.9), custom_call_target="InvertDiagBlocksLowerTriangular" | custom-call | tf_op jit(solution)/shard_map/triangular_solve | solution.py:19
  225.6 3.5 %fusion.5 = f32[128,4096]{1,0:T(8,128)S(1)} fusion(f32[128,4096]{1,0:T(8,128)} %bitcast.50, f32[2,128,128]{1,2,0:T(8,128)S(1)} %custom-call.15), kind=kOutput, calls=%fused_computation.19 | convolution fusion | flops 805306368 | bytes 4259840 | tf_op jit(solution)/shard_map/triangular_solve | solution.py:19
  229.1 2.0 convolution_subtract_fusion
  231.1 1.9 fusion.4
  233.0 2.5 %pad_maximum_fusion = f32[256,4096]{1,0:T(8,128)} fusion(f32[128,4096]{1,0:T(8,128)S(1)} %fusion.4, f32[128,4096]{1,0:T(8,128)S(1)} %fusion.5), kind=kLoop, calls=%fused_computation.4 | loop fusion | flops 1048576 | bytes 8388608 | tf_op jit(solution)/shard_map/triangular_solve | solution.py:19
  (23 shorter events, 3.9 us)
Async XLA Ops:
  7.2 117.3 %all-reduce.4.cloned.1.call-start = ((), (), s32[]{:S(2)}) async-start(), calls=%async_computation.1 | async-start | bytes 524288 | tf_op jit(solution)/shard_map/psum | solution.py:16
  65.2 2.0 copy-start
  71.5 90.2 %all-reduce.6.cloned.1.call-start = ((), (), s32[]{:S(2)}) async-start(), calls=%async_computation.2 | async-start | bytes 524288 | tf_op jit(solution)/shard_map/psum | solution.py:17
Sparse Core Ops, SparseCore 0:
  71.6 52.8 all-reduce.3
  126.9 34.6 all-reduce.5
where the time goes:
time: 243 us; the launch traced here: 242 us
  blocking collectives  79.4 us (33%)
  other arithmetic  63.8 us (26%)
  waiting for transfers between devices  60 us (25%)
  between operations  15.5 us (6%)
  matrix products  12.1 us (5%)
  local copies, waits for them, and re-layouts  11.4 us (5%)
    all_to_all x1, blocking collectives, on_device(): lax.all_to_all(local_scaled, 'dev', split_axis=1, concat_axis=0, tiled=True)  54 us
    another operation x6, other arithmetic, on_device(): lower = jnp.linalg.cholesky(gram / total)  33.9 us
    psum x1, waiting for transfers between devices, on_device(): gram, total = lax.psum((band_gram, band_total), 'band')  33.1 us
    psum x1, waiting for transfers between devices, on_device(): band_gram, band_total = lax.psum((partial_gram, partial_total), 'dev')  26.9 us
    another operation x4, other arithmetic, on_device(): lax.linalg.triangular_solve(lower, scaled, left_side=True, lower=True)  22.4 us
    psum x1, blocking collectives, on_device(): gram, total = lax.psum((band_gram, band_total), 'band')  12.8 us
    psum x1, blocking collectives, on_device(): band_gram, band_total = lax.psum((partial_gram, partial_total), 'dev')  12.6 us
    another operation x3, matrix products, on_device(): lax.linalg.triangular_solve(lower, scaled, left_side=True, lower=True)  7.4 us
  transfers between devices with their start and end apart: 2, of which 2 were waited for; matrix products, arithmetic and copies ran while one was open for 2% of the time, Pallas kernels for 0%

commit v1 on v0

v1 whole, which is shorter than its diff:
```python
import functools
import jax
import jax.numpy as jnp
from jax import lax
from jax.experimental import pallas as pl
from jax.experimental.pallas import tpu as pltpu
from jax.sharding import PartitionSpec as P

F32, BF16 = jnp.float32, jnp.bfloat16
SUB, LANE = 8, 128
PANEL = 64
NN = (((1,), (0,)), ((), ()))
NT = (((1,), (1,)), ((), ()))
VMEM_LIMIT = 32 * 1024 * 1024


def split2(x):
    high = x.astype(BF16)
    return high, (x - high.astype(F32)).astype(BF16)


def split3(x):
    high = x.astype(BF16)
    rest = x - high.astype(F32)
    middle = rest.astype(BF16)
    return high, middle, (rest - middle.astype(F32)).astype(BF16)


def dot(a, b, dims):
    return lax.dot_general(a, b, dims, preferred_element_type=F32)


def product(a, b, dims):
    a1, a2, a3 = a
    b1, b2, b3 = b
    small = (dot(a1, b3, dims) + dot(a3, b1, dims)) + dot(a2, b2, dims)
    return dot(a1, b1, dims) + ((dot(a1, b2, dims) + dot(a2, b1, dims)) + small)


def tree_sum(terms):
    while len(terms) > 1:
        terms = [sum(terms[i : i + 2][1:], terms[i]) for i in range(0, len(terms), 2)]
    return terms[0]


def row_of(x, k):
    return jnp.broadcast_to(x[k : k + 1, :], (SUB, LANE))


def column_of(x, k):
    return jnp.broadcast_to(x[:, k : k + 1], (SUB, LANE))


def factor_panel(tiles, start):
    tiles = list(tiles)
    count = len(tiles)
    sub = lax.broadcasted_iota(jnp.int32, (SUB, LANE), 0)
    diag = [column_of(tiles[0], start + k) for k in range(SUB)]
    for b in range(count):
        rest = range(b + 1, count)
        cols = {t: [column_of(tiles[t], start + SUB * b + k) for k in range(SUB)] for t in rest}
        ahead = [column_of(tiles[b + 1], start + SUB * (b + 1) + k) for k in range(SUB)] if b + 1 < count else None
        rows = []
        for j in range(SUB):
            inverse = lax.rsqrt(row_of(diag[j], j))
            own = diag[j] * inverse
            spread = {k: row_of(own, k) for k in range(j + 1, SUB)}
            for k in range(j + 1, SUB):
                diag[k] = diag[k] - own * spread[k]
            for t in rest:
                cols[t][j] = cols[t][j] * inverse
                for k in range(j + 1, SUB):
                    cols[t][k] = cols[t][k] - cols[t][j] * spread[k]
            row = row_of(tiles[b], j) * inverse
            tiles[b] = jnp.where(sub == j, row, jnp.where(sub > j, tiles[b] - own * row, tiles[b]))
            rows.append(row)
        if ahead is not None:
            below = cols[b + 1]
            diag = [ahead[k] - tree_sum([below[j] * row_of(below[j], k) for j in range(SUB)]) for k in range(SUB)]
        for t in rest:
            tiles[t] = tiles[t] - tree_sum([cols[t][j] * rows[j] for j in range(SUB)])
    return tiles


def cholesky_and_inverse(a_ref, inverse_ref, upper_ref):
    order = a_ref.shape[0]
    inverse_ref[...] = jnp.zeros((order, order), F32)
    upper_ref[...] = jnp.zeros((order, order), F32)
    lane = lax.broadcasted_iota(jnp.int32, (SUB, LANE), 1)
    sub = lax.broadcasted_iota(jnp.int32, (SUB, LANE), 0)
    block_row = lax.broadcasted_iota(jnp.int32, (PANEL, PANEL), 0)
    block_col = lax.broadcasted_iota(jnp.int32, (PANEL, PANEL), 1)
    for first in range(0, order, PANEL):
        end = first + PANEL
        start = first % LANE
        other = PANEL - start
        tiles = []
        for t in range(PANEL // SUB):
            at = first + SUB * t
            eye = jnp.where(lane - other == sub + SUB * t, 1.0, 0.0)
            inside = (lane >= start) & (lane < start + PANEL)
            tiles.append(jnp.where(inside, a_ref[at : at + SUB, first - start : first - start + LANE], eye))
        both = jnp.concatenate(factor_panel(tiles, start), 0)
        upper_ref[first:end, first:end] = jnp.where(block_col >= block_row, both[:, start : start + PANEL], 0.0)
        own = both[:, other : other + PANEL]
        own_terms = split3(own)
        if first:
            inverse_ref[first:end, :first] = product(own_terms, split3(inverse_ref[first:end, :first]), NN)
        inverse_ref[first:end, first:end] = own
        if end < order:
            lower = product(split3(a_ref[end:, first:end]), own_terms, NT)
            lower_terms = split3(lower)
            a_ref[end:, end:] = a_ref[end:, end:] - product(lower_terms, lower_terms, NT)
            inverse_ref[end:, :end] = inverse_ref[end:, :end] - product(lower_terms, split3(inverse_ref[first:end, :end]), NN)
            upper_ref[first:end, end:] = lower.T


def slice_kernel(index_ref, x_ref, out_ref):
    out_ref[...] = x_ref[...]


def take_cells(anomaly, index, cells):
    rows = anomaly.shape[0]
    return pl.pallas_call(
        slice_kernel,
        grid_spec=pltpu.PrefetchScalarGridSpec(
            num_scalar_prefetch=1,
            grid=(1,),
            in_specs=[pl.BlockSpec((rows, cells), lambda i, at: (0, at[0]))],
            out_specs=pl.BlockSpec((rows, cells), lambda i, at: (0, 0)),
        ),
        out_shape=jax.ShapeDtypeStruct((rows, cells), F32),
        compiler_params=pltpu.CompilerParams(vmem_limit_bytes=VMEM_LIMIT),
    )(index[None], anomaly)


def gram_kernel(pieces, me_ref, own_ref, *refs):
    piece_refs, (root_ref, total_ref) = refs[: pieces - 1], refs[pieces - 1 : pieces + 1]
    high_ref, low_ref, keep_ref, send_ref, scaled_ref, main_ref, cross_ref = refs[pieces + 1 :]
    step = pl.program_id(0)
    me = me_ref[0]
    rows = own_ref.shape[0]
    root = root_ref[...]
    for k, ref in enumerate((own_ref, *piece_refs)):
        at = pl.multiple_of((me ^ k) * rows, rows)
        scaled_ref[pl.ds(at, rows), :] = ref[...] * root
    high, low = split2(scaled_ref[...])
    high_ref[...] = high
    low_ref[...] = low

    @pl.when(step == 0)
    def _():
        main_ref[...] = jnp.zeros_like(main_ref)
        cross_ref[...] = jnp.zeros_like(cross_ref)

    main_ref[...] += dot(high, high, NT)
    cross_ref[...] += dot(high, low, NT)

    @pl.when(step == pl.num_programs(0) - 1)
    def _():
        cross = cross_ref[...]
        main_ref[...] = main_ref[...] + (cross + cross.T)
        half = main_ref.shape[0] // 2
        row = lax.broadcasted_iota(jnp.int32, (half, half), 0)
        col = lax.broadcasted_iota(jnp.int32, (half, half), 1)
        last = main_ref[half:, half:]
        both = jnp.where(row >= col, main_ref[:half, :half], last)
        corner = jnp.sum(jnp.where(row == col, last, 0.0), axis=0, keepdims=True)
        extra_row = lax.broadcasted_iota(jnp.int32, (SUB, half), 0)
        extra = jnp.where(extra_row == 0, jnp.broadcast_to(corner, (SUB, half)), jnp.broadcast_to(total_ref[...], (SUB, half)))
        off = main_ref[half:, :half]
        first_core = (me & 1) == 0
        for ref, is_off in ((keep_ref, first_core), (send_ref, jnp.logical_not(first_core))):
            ref[:half, :] = jnp.where(is_off, off, both)
            ref[half:, :] = extra


def form_gram(me, anomaly, pieces, root, total, cells):
    rows = anomaly.shape[0]
    count = len(pieces) + 1
    order = rows * count
    step = min(cells, 1024)
    packed = (order // 2 + SUB, order // 2)
    steps = cells // step
    return pl.pallas_call(
        functools.partial(gram_kernel, count),
        grid_spec=pltpu.PrefetchScalarGridSpec(
            num_scalar_prefetch=1,
            grid=(steps,),
            in_specs=[pl.BlockSpec((rows, step), lambda i, me: (0, me[0] * steps + i))]
            + [pl.BlockSpec((rows, step), lambda i, me: (0, i))] * (count - 1)
            + [pl.BlockSpec((1, step), lambda i, me: (0, i)), pl.BlockSpec((1, 1), lambda i, me: (0, 0))],
            out_specs=[pl.BlockSpec((order, step), lambda i, me: (0, i))] * 2
            + [pl.BlockSpec(packed, lambda i, me: (0, 0))] * 2,
            scratch_shapes=[pltpu.VMEM((order, step), F32), pltpu.VMEM((order, order), F32), pltpu.VMEM((order, order), F32)],
        ),
        out_shape=[jax.ShapeDtypeStruct((order, cells), BF16)] * 2 + [jax.ShapeDtypeStruct(packed, F32)] * 2,
        compiler_params=pltpu.CompilerParams(vmem_limit_bytes=VMEM_LIMIT),
        cost_estimate=pl.CostEstimate(flops=4 * order * order * cells, bytes_accessed=8 * order * cells, transcendentals=0),
    )(me[None], anomaly, *pieces, root, total)


def solve_kernel(me_ref, mine_ref, other_ref, high_ref, low_ref, upper_ref, scores_ref, a_ref, inverse_ref, high_inv_ref, low_inv_ref):
    @pl.when(pl.program_id(0) == 0)
    def _():
        half = mine_ref.shape[1]
        first_core = (me_ref[0] & 1) == 0
        mine, other = mine_ref[...], other_ref[...]
        off = jnp.where(first_core, mine[:half], other[:half])
        both = jnp.where(first_core, other[:half], mine[:half])
        scale = 1.0 / mine[half + 1 : half + 2, :]
        row = lax.broadcasted_iota(jnp.int32, (half, half), 0)
        col = lax.broadcasted_iota(jnp.int32, (half, half), 1)
        turned = both.T
        corner = jnp.broadcast_to(mine[half : half + 1, :], (half, half))
        a_ref[:half, :half] = jnp.where(row >= col, both, turned) * scale
        a_ref[half:, half:] = jnp.where(row < col, both, jnp.where(row > col, turned, corner)) * scale
        a_ref[half:, :half] = off * scale
        cholesky_and_inverse(a_ref, inverse_ref, upper_ref)
        high, low = split2(inverse_ref[...])
        high_inv_ref[...] = high
        low_inv_ref[...] = low

    high = high_inv_ref[...]
    scores_ref[...] = dot(high, high_ref[...], NN) + (dot(high, low_ref[...], NN) + dot(low_inv_ref[...], high_ref[...], NN))


def solve(me, mine, other, high, low):
    order, cells = high.shape
    step = min(cells, 512)
    whole = lambda i, me: (0, 0)
    chunk = lambda i, me: (0, i)
    return pl.pallas_call(
        solve_kernel,
        grid_spec=pltpu.PrefetchScalarGridSpec(
            num_scalar_prefetch=1,
            grid=(cells // step,),
            in_specs=[pl.BlockSpec(mine.shape, whole)] * 2 + [pl.BlockSpec((order, step), chunk)] * 2,
            out_specs=[pl.BlockSpec((order, order), whole), pl.BlockSpec((order, step), chunk)],
            scratch_shapes=[pltpu.VMEM((order, order), F32)] * 2 + [pltpu.VMEM((order, order), BF16)] * 2,
        ),
        out_shape=[jax.ShapeDtypeStruct((order, order), F32), jax.ShapeDtypeStruct((order, cells), F32)],
        compiler_params=pltpu.CompilerParams(vmem_limit_bytes=VMEM_LIMIT),
        cost_estimate=pl.CostEstimate(flops=6 * order * order * cells, bytes_accessed=8 * order * cells, transcendentals=0),
    )(me[None], mine, other, high, low)


def swap(x, axis, mask):
    return lax.ppermute(x, axis, [(i, i ^ mask) for i in range(lax.axis_size(axis))])


def sum_over(x, axis, first):
    size = lax.axis_size(axis)
    while first < size:
        if 2 * first < size:
            near, far, both = swap(x, axis, first), swap(x, axis, 2 * first), swap(x, axis, 3 * first)
            x = (x + near) + (far + both)
        else:
            x = x + swap(x, axis, first)
        first *= 4
    return x


def on_device(anomaly, ocean_mask, area_weight):
    size = lax.axis_size("dev")
    me = lax.axis_index("dev")
    cells = anomaly.shape[1] // size
    order = sorted(range(1, size), key=lambda k: (-(k >> 1).bit_count(), k & 1))
    pieces = {k: swap(take_cells(anomaly, me ^ k, cells), "dev", k) for k in order}
    own = lambda x: lax.dynamic_slice_in_dim(x, me * cells, cells, 0)
    weights = own(area_weight) * own(ocean_mask).astype(F32)
    root = jnp.sqrt(weights)[None, :]
    total = jnp.sum(weights)[None, None]
    high, low, keep, send = form_gram(me, anomaly, [pieces[k] for k in range(1, size)], root, total, cells)
    mine = keep + swap(send, "dev", 1)
    mine = sum_over(mine, "dev", 2)
    mine = sum_over(mine, "band", 1)
    other = swap(mine, "dev", 1)
    return tuple(solve(me, mine, other, high, low))


def solution(mesh):
    return jax.shard_map(
        on_device,
        mesh=mesh,
        in_specs=(P("dev", "band"), P("band"), P("band")),
        out_specs=(P(), P(None, ("band", "dev"))),
        check_vma=False,
    )
```

time: 243 us -> 96.1 us (0.40)
  blocking collectives: 79.4 us -> 0 us
  other arithmetic: 63.8 us -> 1.39 us
  Pallas kernels: 0 us -> 22.8 us
  waiting for transfers between devices: 60 us -> 39.4 us
  starting transfers between devices: 0.08 us -> 16.1 us
  between operations: 15.5 us -> 0.7 us
  matrix products: 12.1 us -> 0 us
  local copies, waits for them, and re-layouts: 11.4 us -> 15.3 us
    psum x2 -> x0, waiting for transfers between devices: 60 us -> none  [the longest x1 33.1 us: on_device(): gram, total = lax.psum((band_gram, band_total), 'band')]
    another operation x10 -> x0, other arithmetic: 56.4 us -> none  [the longest x6 33.9 us: on_device(): lower = jnp.linalg.cholesky(gram / total)]
    all_to_all x1 -> x0, blocking collectives: 54 us -> none  [on_device(): lax.all_to_all(local_scaled, 'dev', split_axis=1, concat_axis=0, tiled=True)]
    ppermute x0 -> x15, waiting for transfers between devices: none -> 39.4 us  [swap(): lax.ppermute(x, axis, [(i, i ^ mask) for i in range(lax.axis_size(axis))])]
    psum x2 -> x0, blocking collectives: 25.4 us -> none  [the longest x1 12.8 us: on_device(): gram, total = lax.psum((band_gram, band_total), 'band')]
    pallas_call x0 -> x9, Pallas kernels: none -> 22.8 us  [the longest x1 12 us: solve(): pl.pallas_call(solve_kernel, grid_spec=pltpu.PrefetchScalarGridSpec(num_s...]
    ppermute x0 -> x15, starting transfers between devices: none -> 16.1 us  [swap(): lax.ppermute(x, axis, [(i, i ^ mask) for i in range(lax.axis_size(axis))])]
    unnamed x3 -> x14, local copies, waits for them, and re-layouts: 2.85 us -> 15.3 us
  transfers between devices with their start and end apart: 2 -> 15, of which waited for: 2 -> 9; matrix products, arithmetic and copies ran while one was open for 2% -> 1% of each run, Pallas kernels for 0% -> 4%
where the time goes in v1:
time: 96.1 us; the launch traced here: 95.6 us
  waiting for transfers between devices  39.4 us (41%)
  Pallas kernels  22.8 us (24%)
  starting transfers between devices  16.1 us (17%)
  local copies, waits for them, and re-layouts  15.3 us (16%)
  other arithmetic  1.39 us (1%)
    ppermute x15, waiting for transfers between devices, swap(): lax.ppermute(x, axis, [(i, i ^ mask) for i in range(lax.axis_size(axis))])  39.4 us
    ppermute x15, starting transfers between devices, swap(): lax.ppermute(x, axis, [(i, i ^ mask) for i in range(lax.axis_size(axis))])  16.1 us
    unnamed x14, local copies, waits for them, and re-layouts  15.3 us
    pallas_call x1, Pallas kernels, solve(): pl.pallas_call(solve_kernel, grid_spec=pltpu.PrefetchScalarGridSpec(num_s...  12 us
    pallas_call x1, Pallas kernels, form_gram(): pl.pallas_call(functools.partial(gram_kernel, count), grid_spec=pltpu.Pre...  5.7 us
    pallas_call x7, Pallas kernels, take_cells(): pl.pallas_call(slice_kernel, grid_spec=pltpu.PrefetchScalarGridSpec(num_s...  5.03 us
  transfers between devices with their start and end apart: 15, of which 9 were waited for; matrix products, arithmetic and copies ran while one was open for 1% of the time, Pallas kernels for 4%

profile of v1, /device:TPU:0, one launch (start us, length us, event | category | flops | bytes accessed | tf_op | source)
XLA Modules:
  0.0 95.6 jit_solution(7548140861327512872)
XLA Ops:
  0.6 2.2 %copy-done = f32[32,32768]{1,0:T(8,128)S(1)} copy-done((f32[32,32768]{1,0:T(8,128)S(1)}, f32[32,32768]{1,0:T(8,128)}, u32[]{:S(2)}) %copy-start) | copy-done | bytes 4194328
  2.8 0.9 shard_map.56
  3.7 3.3 %collective-permute-start.6 = (f32[32,4096]{1,0:T(8,128)}, f32[32,4096]{1,0:T(8,128)S(1)}, u32[]{:S(2)}, u32[]{:S(2)}) collective-permute-start(f32[32,4096]{1,0:T(8,128)} %shard_map.56), channel_id=1, source_target_pairs={{0,7},{1,6},{2,5},{3,4},{4,3},{5,2},{6,1},{7,0},{8,15},{9,14},{10,... | collective-permute-start | bytes 1572872 | tf_op jit(solution)/shard_map/ppermute | solution.py:249
  7.0 2.2 %copy-done.1 = f32[32,32768]{1,0:T(8,128)S(1)} copy-done((f32[32,32768]{1,0:T(8,128)S(1)}, f32[32,32768]{1,0:T(8,128)}, u32[]{:S(2)}) %copy-start.1) | copy-done | bytes 4194328
  10.7 2.2 %copy-done.2 = f32[32,32768]{1,0:T(8,128)S(1)} copy-done((f32[32,32768]{1,0:T(8,128)S(1)}, f32[32,32768]{1,0:T(8,128)}, u32[]{:S(2)}) %copy-start.2) | copy-done | bytes 4194328
  13.5 2.2 %copy-done.3 = f32[32,32768]{1,0:T(8,128)S(1)} copy-done((f32[32,32768]{1,0:T(8,128)S(1)}, f32[32,32768]{1,0:T(8,128)}, u32[]{:S(2)}) %copy-start.3) | copy-done | bytes 4194328
  17.4 2.2 %copy-done.4 = f32[32,32768]{1,0:T(8,128)S(1)} copy-done((f32[32,32768]{1,0:T(8,128)S(1)}, f32[32,32768]{1,0:T(8,128)}, u32[]{:S(2)}) %copy-start.4) | copy-done | bytes 4194328
  20.9 2.2 %copy-done.5 = f32[32,32768]{1,0:T(8,128)S(1)} copy-done((f32[32,32768]{1,0:T(8,128)S(1)}, f32[32,32768]{1,0:T(8,128)}, u32[]{:S(2)}) %copy-start.5) | copy-done | bytes 4194328
  24.7 1.6 %collective-permute-start.4 = (f32[32,4096]{1,0:T(8,128)}, f32[32,4096]{1,0:T(8,128)}, u32[]{:S(2)}, u32[]{:S(2)}) collective-permute-start(f32[32,4096]{1,0:T(8,128)} %shard_map.54), channel_id=1, source_target_pairs={{0,5},{1,4},{2,7},{3,6},{4,1},{5,0},{6,3},{7,2},{8,13},{9,12},{10,... | collective-permute-start | bytes 1572872 | tf_op jit(solution)/shard_map/ppermute | solution.py:249
  26.6 1.3 %fusion = (f32[]{:T(128)}, f32[4096]{0:T(1024)S(1)}) fusion(s32[32768]{0:T(1024)} %param.4, s32[]{:T(128)S(6)} %select_n.4, f32[32768]{0:T(1024)} %param.5), kind=kLoop, calls=%fused_computation.3 | loop fusion | flops 12287 | bytes 49160 | tf_op jit(solution)/shard_map/reduce_sum | solution.py:273
  28.0 3.8 %collective-permute-done.1.refs_1_ = f32[32,4096]{1,0:T(8,128)S(1)} collective-permute-done((f32[32,4096]{1,0:T(8,128)S(1)}, f32[32,4096]{1,0:T(8,128)S(1)}, u32[]{:S(2)}, u32[]{:S(2)}) %collective-permute-start.1) | collective-permute-done | bytes 524320 | tf_op jit(solution)/shard_map/ppermute | solution.py:249
  31.8 11.2 %collective-permute-done.2.refs_2_ = f32[32,4096]{1,0:T(8,128)S(1)} collective-permute-done((f32[32,4096]{1,0:T(8,128)}, f32[32,4096]{1,0:T(8,128)S(1)}, u32[]{:S(2)}, u32[]{:S(2)}) %collective-permute-start.2) | collective-permute-done | bytes 524320 | tf_op jit(solution)/shard_map/ppermute | solution.py:249
  43.0 14.6 %collective-permute-done.4.refs_4_ = f32[32,4096]{1,0:T(8,128)} collective-permute-done((f32[32,4096]{1,0:T(8,128)}, f32[32,4096]{1,0:T(8,128)}, u32[]{:S(2)}, u32[]{:S(2)}) %collective-permute-start.4) | collective-permute-done | bytes 524320 | tf_op jit(solution)/shard_map/ppermute | solution.py:249
  57.6 2.2 %copy-done.6 = f32[32,32768]{1,0:T(8,128)S(1)} copy-done((f32[32,32768]{1,0:T(8,128)S(1)}, f32[32,32768]{1,0:T(8,128)}, u32[]{:S(2)}) %copy-start.6) | copy-done | bytes 4194328
  59.8 5.7 %shard_map.57 = (bf16[256,4096]{1,0:T(8,128)(2,1)S(1)}, bf16[256,4096]{1,0:T(8,128)(2,1)S(1)}, f32[136,128]{1,0:T(8,128)S(1)}, f32[136,128]{1,0:T(8,128)S(1)}) custom-call(s32[1]{0:T(128)} %bitcast.me_ref, f32[32,32768]{1,0:T(8,128)S(1)} %copy-done.6, f32[32,4096]{1,0:T(8,128)S(1)} %collective-permute-done.refs_0_, ...), custom_call_target="tpu_custom_call" | custom-call | flops 1073741824 | bytes 8388608 | tf_op jit(solution)/shard_map/pallas_call | solution.py:185
  65.7 1.1 %collective-permute-done.7 = f32[136,128]{1,0:T(8,128)S(1)} collective-permute-done((f32[136,128]{1,0:T(8,128)S(1)}, f32[136,128]{1,0:T(8,128)S(1)}, u32[]{:S(2)}, u32[]{:S(2)}) %collective-permute-start.7) | collective-permute-done | bytes 69664 | tf_op jit(solution)/shard_map/ppermute | solution.py:249
  66.9 1.8 %collective-permute-start.9 = (f32[136,128]{1,0:T(8,128)S(1)}, f32[136,128]{1,0:T(8,128)S(1)}, u32[]{:S(2)}, u32[]{:S(2)}) collective-permute-start(f32[136,128]{1,0:T(8,128)S(1)} %add.26), channel_id=1, source_target_pairs={{0,4},{1,5},{2,6},{3,7},{4,0},{5,1},{6,2},{7,3},{8,12},{9,13},{10,... | collective-permute-start | bytes 208904 | tf_op jit(solution)/shard_map/ppermute | solution.py:249
  68.8 1.6 %collective-permute-start.8 = (f32[136,128]{1,0:T(8,128)S(1)}, f32[136,128]{1,0:T(8,128)S(1)}, u32[]{:S(2)}, u32[]{:S(2)}) collective-permute-start(f32[136,128]{1,0:T(8,128)S(1)} %add.26), channel_id=1, source_target_pairs={{0,2},{1,3},{2,0},{3,1},{4,6},{5,7},{6,4},{7,5},{8,10},{9,11},{10,... | collective-permute-start | bytes 208904 | tf_op jit(solution)/shard_map/ppermute | solution.py:249
  70.4 2.4 %collective-permute-done.10 = f32[136,128]{1,0:T(8,128)S(1)} collective-permute-done((f32[136,128]{1,0:T(8,128)S(1)}, f32[136,128]{1,0:T(8,128)S(1)}, u32[]{:S(2)}, u32[]{:S(2)}) %collective-permute-start.10) | collective-permute-done | bytes 69664 | tf_op jit(solution)/shard_map/ppermute | solution.py:249
  73.1 3.7 %collective-permute-start.13 = (f32[136,128]{1,0:T(8,128)S(1)}, f32[136,128]{1,0:T(8,128)S(1)}, u32[]{:S(2)}, u32[]{:S(2)}) collective-permute-start(f32[136,128]{1,0:T(8,128)S(1)} %add_add_fusion.1), channel_id=1, source_target_pairs={{0,24},{8,16},{16,8},{24,0},{1,25},{9,17},{17,9},{25,1},{2,26},{10... | collective-permute-start | bytes 208904 | tf_op jit(solution)/shard_map/ppermute | solution.py:249
  77.6 2.0 %collective-permute-done.13 = f32[136,128]{1,0:T(8,128)S(1)} collective-permute-done((f32[136,128]{1,0:T(8,128)S(1)}, f32[136,128]{1,0:T(8,128)S(1)}, u32[]{:S(2)}, u32[]{:S(2)}) %collective-permute-start.13) | collective-permute-done | bytes 69664 | tf_op jit(solution)/shard_map/ppermute | solution.py:249
  79.5 2.7 %collective-permute-done.12 = f32[136,128]{1,0:T(8,128)S(1)} collective-permute-done((f32[136,128]{1,0:T(8,128)S(1)}, f32[136,128]{1,0:T(8,128)S(1)}, u32[]{:S(2)}, u32[]{:S(2)}) %collective-permute-start.12) | collective-permute-done | bytes 69664 | tf_op jit(solution)/shard_map/ppermute | solution.py:249
  82.3 1.2 %collective-permute-done.14.other_ref = f32[136,128]{1,0:T(8,128)S(1)} collective-permute-done((f32[136,128]{1,0:T(8,128)S(1)}, f32[136,128]{1,0:T(8,128)S(1)}, u32[]{:S(2)}, u32[]{:S(2)}) %collective-permute-start.14) | collective-permute-done | bytes 69664 | tf_op jit(solution)/shard_map/ppermute | solution.py:249
  83.6 12.0 %shard_map.58 = (f32[256,256]{1,0:T(8,128)}, f32[256,4096]{1,0:T(8,128)}) custom-call(s32[1]{0:T(128)} %bitcast.me_ref, f32[136,128]{1,0:T(8,128)S(1)} %add_add_fusion.mine_ref, f32[136,128]{1,0:T(8,128)S(1)} %collective-permute-done.14.other_ref, bf16[256,4096]{1,0:T(8,128)(2,1)S(1)} %get-tuple-element.8.high_ref, ...), custom_call_target="tpu_custom_call" | custom-call | flops 1610612736 | bytes 8388608 | tf_op jit(solution)/shard_map/pallas_call | solution.py:233
  (33 shorter events, 8.5 us)
Async XLA Ops:
  0.6 2.2 %copy-start = (f32[32,32768]{1,0:T(8,128)S(1)}, f32[32,32768]{1,0:T(8,128)}, u32[]{:S(2)}) copy-start(f32[32,32768]{1,0:T(8,128)} %own_ref.1) | copy-start | bytes 12582916
  3.7 21.1 %collective-permute-start.6 = (f32[32,4096]{1,0:T(8,128)}, f32[32,4096]{1,0:T(8,128)S(1)}, u32[]{:S(2)}, u32[]{:S(2)}) collective-permute-start(f32[32,4096]{1,0:T(8,128)} %shard_map.56), channel_id=1, source_target_pairs={{0,7},{1,6},{2,5},{3,4},{4,3},{5,2},{6,1},{7,0},{8,15},{9,14},{10,... | collective-permute-start | bytes 1572872 | tf_op jit(solution)/shard_map/ppermute | solution.py:249
  7.0 2.2 %copy-start.1 = (f32[32,32768]{1,0:T(8,128)S(1)}, f32[32,32768]{1,0:T(8,128)}, u32[]{:S(2)}) copy-start(f32[32,32768]{1,0:T(8,128)} %own_ref.1) | copy-start | bytes 12582916
  10.0 16.4 %collective-permute-start = (f32[32,4096]{1,0:T(8,128)}, f32[32,4096]{1,0:T(8,128)S(1)}, u32[]{:S(2)}, u32[]{:S(2)}) collective-permute-start(f32[32,4096]{1,0:T(8,128)} %shard_map.50), channel_id=1, source_target_pairs={{0,1},{1,0},{2,3},{3,2},{4,5},{5,4},{6,7},{7,6},{8,9},{9,8},{10,11... | collective-permute-start | bytes 1572872 | tf_op jit(solution)/shard_map/ppermute | solution.py:249
  10.7 2.2 %copy-start.2 = (f32[32,32768]{1,0:T(8,128)S(1)}, f32[32,32768]{1,0:T(8,128)}, u32[]{:S(2)}) copy-start(f32[32,32768]{1,0:T(8,128)} %own_ref.1) | copy-start | bytes 12582916
  12.9 18.8 %collective-permute-start.1 = (f32[32,4096]{1,0:T(8,128)S(1)}, f32[32,4096]{1,0:T(8,128)S(1)}, u32[]{:S(2)}, u32[]{:S(2)}) collective-permute-start(f32[32,4096]{1,0:T(8,128)S(1)} %shard_map.51), channel_id=1, source_target_pairs={{0,2},{1,3},{2,0},{3,1},{4,6},{5,7},{6,4},{7,5},{8,10},{9,11},{10,... | collective-permute-start | bytes 1572872 | tf_op jit(solution)/shard_map/ppermute | solution.py:249
  13.5 2.2 %copy-start.3 = (f32[32,32768]{1,0:T(8,128)S(1)}, f32[32,32768]{1,0:T(8,128)}, u32[]{:S(2)}) copy-start(f32[32,32768]{1,0:T(8,128)} %own_ref.1) | copy-start | bytes 12582916
  16.6 26.4 %collective-permute-start.2 = (f32[32,4096]{1,0:T(8,128)}, f32[32,4096]{1,0:T(8,128)S(1)}, u32[]{:S(2)}, u32[]{:S(2)}) collective-permute-start(f32[32,4096]{1,0:T(8,128)} %shard_map.52), channel_id=1, source_target_pairs={{0,3},{1,2},{2,1},{3,0},{4,7},{5,6},{6,5},{7,4},{8,11},{9,10},{10,... | collective-permute-start | bytes 1572872 | tf_op jit(solution)/shard_map/ppermute | solution.py:249
  17.4 2.2 %copy-start.4 = (f32[32,32768]{1,0:T(8,128)S(1)}, f32[32,32768]{1,0:T(8,128)}, u32[]{:S(2)}) copy-start(f32[32,32768]{1,0:T(8,128)} %own_ref.1) | copy-start | bytes 12582916
  20.4 22.6 %collective-permute-start.3 = (f32[32,4096]{1,0:T(8,128)}, f32[32,4096]{1,0:T(8,128)S(1)}, u32[]{:S(2)}, u32[]{:S(2)}) collective-permute-start(f32[32,4096]{1,0:T(8,128)} %shard_map.53), channel_id=1, source_target_pairs={{0,4},{1,5},{2,6},{3,7},{4,0},{5,1},{6,2},{7,3},{8,12},{9,13},{10,... | collective-permute-start | bytes 1572872 | tf_op jit(solution)/shard_map/ppermute | solution.py:249
  20.9 2.2 %copy-start.5 = (f32[32,32768]{1,0:T(8,128)S(1)}, f32[32,32768]{1,0:T(8,128)}, u32[]{:S(2)}) copy-start(f32[32,32768]{1,0:T(8,128)} %own_ref.1) | copy-start | bytes 12582916
  24.7 32.9 %collective-permute-start.4 = (f32[32,4096]{1,0:T(8,128)}, f32[32,4096]{1,0:T(8,128)}, u32[]{:S(2)}, u32[]{:S(2)}) collective-permute-start(f32[32,4096]{1,0:T(8,128)} %shard_map.54), channel_id=1, source_target_pairs={{0,5},{1,4},{2,7},{3,6},{4,1},{5,0},{6,3},{7,2},{8,13},{9,12},{10,... | collective-permute-start | bytes 1572872 | tf_op jit(solution)/shard_map/ppermute | solution.py:249
  26.4 31.2 %collective-permute-start.5 = (f32[32,4096]{1,0:T(8,128)}, f32[32,4096]{1,0:T(8,128)}, u32[]{:S(2)}, u32[]{:S(2)}) collective-permute-start(f32[32,4096]{1,0:T(8,128)} %shard_map.55), channel_id=1, source_target_pairs={{0,6},{1,7},{2,4},{3,5},{4,2},{5,3},{6,0},{7,1},{8,14},{9,15},{10,... | collective-permute-start | bytes 1572872 | tf_op jit(solution)/shard_map/ppermute | solution.py:249
  57.6 2.2 %copy-start.6 = (f32[32,32768]{1,0:T(8,128)S(1)}, f32[32,32768]{1,0:T(8,128)}, u32[]{:S(2)}) copy-start(f32[32,32768]{1,0:T(8,128)} %own_ref.1) | copy-start | bytes 12582916
  65.5 1.3 %collective-permute-start.7 = (f32[136,128]{1,0:T(8,128)S(1)}, f32[136,128]{1,0:T(8,128)S(1)}, u32[]{:S(2)}, u32[]{:S(2)}) collective-permute-start(f32[136,128]{1,0:T(8,128)S(1)} %get-tuple-element.7), channel_id=1, source_target_pairs={{0,1},{1,0},{2,3},{3,2},{4,5},{5,4},{6,7},{7,6},{8,9},{9,8},{10,11... | collective-permute-start | bytes 208904 | tf_op jit(solution)/shard_map/ppermute | solution.py:249
  66.8 6.0 %collective-permute-start.10 = (f32[136,128]{1,0:T(8,128)S(1)}, f32[136,128]{1,0:T(8,128)S(1)}, u32[]{:S(2)}, u32[]{:S(2)}) collective-permute-start(f32[136,128]{1,0:T(8,128)S(1)} %add.26), channel_id=1, source_target_pairs={{0,6},{1,7},{2,4},{3,5},{4,2},{5,3},{6,0},{7,1},{8,14},{9,15},{10,... | collective-permute-start | bytes 208904 | tf_op jit(solution)/shard_map/ppermute | solution.py:249
  66.9 5.9 %collective-permute-start.9 = (f32[136,128]{1,0:T(8,128)S(1)}, f32[136,128]{1,0:T(8,128)S(1)}, u32[]{:S(2)}, u32[]{:S(2)}) collective-permute-start(f32[136,128]{1,0:T(8,128)S(1)} %add.26), channel_id=1, source_target_pairs={{0,4},{1,5},{2,6},{3,7},{4,0},{5,1},{6,2},{7,3},{8,12},{9,13},{10,... | collective-permute-start | bytes 208904 | tf_op jit(solution)/shard_map/ppermute | solution.py:249
  68.8 4.3 %collective-permute-start.8 = (f32[136,128]{1,0:T(8,128)S(1)}, f32[136,128]{1,0:T(8,128)S(1)}, u32[]{:S(2)}, u32[]{:S(2)}) collective-permute-start(f32[136,128]{1,0:T(8,128)S(1)} %add.26), channel_id=1, source_target_pairs={{0,2},{1,3},{2,0},{3,1},{4,6},{5,7},{6,4},{7,5},{8,10},{9,11},{10,... | collective-permute-start | bytes 208904 | tf_op jit(solution)/shard_map/ppermute | solution.py:249
  73.1 6.4 %collective-permute-start.13 = (f32[136,128]{1,0:T(8,128)S(1)}, f32[136,128]{1,0:T(8,128)S(1)}, u32[]{:S(2)}, u32[]{:S(2)}) collective-permute-start(f32[136,128]{1,0:T(8,128)S(1)} %add_add_fusion.1), channel_id=1, source_target_pairs={{0,24},{8,16},{16,8},{24,0},{1,25},{9,17},{17,9},{25,1},{2,26},{10... | collective-permute-start | bytes 208904 | tf_op jit(solution)/shard_map/ppermute | solution.py:249
  76.8 5.5 %collective-permute-start.12 = (f32[136,128]{1,0:T(8,128)S(1)}, f32[136,128]{1,0:T(8,128)S(1)}, u32[]{:S(2)}, u32[]{:S(2)}) collective-permute-start(f32[136,128]{1,0:T(8,128)S(1)} %add_add_fusion.1), channel_id=1, source_target_pairs={{0,16},{8,24},{16,0},{24,8},{1,17},{9,25},{17,1},{25,9},{2,18},{10... | collective-permute-start | bytes 208904 | tf_op jit(solution)/shard_map/ppermute | solution.py:249
  76.8 5.5 %collective-permute-start.11 = (f32[136,128]{1,0:T(8,128)S(1)}, f32[136,128]{1,0:T(8,128)S(1)}, u32[]{:S(2)}, u32[]{:S(2)}) collective-permute-start(f32[136,128]{1,0:T(8,128)S(1)} %add_add_fusion.1), channel_id=1, source_target_pairs={{0,8},{8,0},{16,24},{24,16},{1,9},{9,1},{17,25},{25,17},{2,10},{10... | collective-permute-start | bytes 208904 | tf_op jit(solution)/shard_map/ppermute | solution.py:249
  82.2 1.3 %collective-permute-start.14 = (f32[136,128]{1,0:T(8,128)S(1)}, f32[136,128]{1,0:T(8,128)S(1)}, u32[]{:S(2)}, u32[]{:S(2)}) collective-permute-start(f32[136,128]{1,0:T(8,128)S(1)} %add_add_fusion.mine_ref), channel_id=1, source_target_pairs={{0,1},{1,0},{2,3},{3,2},{4,5},{5,4},{6,7},{7,6},{8,9},{9,8},{10,11... | collective-permute-start | bytes 208904 | tf_op jit(solution)/shard_map/ppermute | solution.py:249

commit v2 on v0

v2 whole, which is shorter than its diff:
```python
import functools
import jax
import jax.numpy as jnp
from jax import lax
from jax.experimental import pallas as pl
from jax.experimental.pallas import tpu as pltpu
from jax.sharding import PartitionSpec as P

F32, BF16 = jnp.float32, jnp.bfloat16
SUB, LANE = 8, 128
PANEL = 64
NN = (((1,), (0,)), ((), ()))
NT = (((1,), (1,)), ((), ()))
VMEM_LIMIT = 24 * 1024 * 1024
STEP = 512


def split2(x):
    high = x.astype(BF16)
    return high, (x - high.astype(F32)).astype(BF16)


def split3(x):
    high = x.astype(BF16)
    rest = x - high.astype(F32)
    middle = rest.astype(BF16)
    return high, middle, (rest - middle.astype(F32)).astype(BF16)


def dot(a, b, dims):
    return lax.dot_general(a, b, dims, preferred_element_type=F32)


def product(a, b, dims):
    a1, a2, a3 = a
    b1, b2, b3 = b
    small = (dot(a1, b3, dims) + dot(a3, b1, dims)) + dot(a2, b2, dims)
    return dot(a1, b1, dims) + ((dot(a1, b2, dims) + dot(a2, b1, dims)) + small)


def tree_sum(terms):
    while len(terms) > 1:
        terms = [sum(terms[i : i + 2][1:], terms[i]) for i in range(0, len(terms), 2)]
    return terms[0]


def row_of(x, k):
    return jnp.broadcast_to(x[k : k + 1, :], (SUB, LANE))


def column_of(x, k):
    return jnp.broadcast_to(x[:, k : k + 1], (SUB, LANE))


def factor_panel(tiles, start):
    tiles = list(tiles)
    count = len(tiles)
    sub = lax.broadcasted_iota(jnp.int32, (SUB, LANE), 0)
    diag = [column_of(tiles[0], start + k) for k in range(SUB)]
    for b in range(count):
        rest = range(b + 1, count)
        cols = {t: [column_of(tiles[t], start + SUB * b + k) for k in range(SUB)] for t in rest}
        ahead = [column_of(tiles[b + 1], start + SUB * (b + 1) + k) for k in range(SUB)] if b + 1 < count else None
        rows = []
        for j in range(SUB):
            inverse = lax.rsqrt(row_of(diag[j], j))
            own = diag[j] * inverse
            spread = {k: row_of(own, k) for k in range(j + 1, SUB)}
            for k in range(j + 1, SUB):
                diag[k] = diag[k] - own * spread[k]
            for t in rest:
                cols[t][j] = cols[t][j] * inverse
                for k in range(j + 1, SUB):
                    cols[t][k] = cols[t][k] - cols[t][j] * spread[k]
            row = row_of(tiles[b], j) * inverse
            tiles[b] = jnp.where(sub == j, row, jnp.where(sub > j, tiles[b] - own * row, tiles[b]))
            rows.append(row)
        if ahead is not None:
            below = cols[b + 1]
            diag = [ahead[k] - tree_sum([below[j] * row_of(below[j], k) for j in range(SUB)]) for k in range(SUB)]
        for t in rest:
            tiles[t] = tiles[t] - tree_sum([cols[t][j] * rows[j] for j in range(SUB)])
    return tiles


def cholesky_and_inverse(a_ref, inverse_ref, upper_ref, lower_ref):
    order = a_ref.shape[0]
    inverse_ref[...] = jnp.zeros((order, order), F32)
    upper_ref[...] = jnp.zeros((order, order), F32)
    lane = lax.broadcasted_iota(jnp.int32, (SUB, PANEL), 1)
    sub = lax.broadcasted_iota(jnp.int32, (SUB, PANEL), 0)
    block_row = lax.broadcasted_iota(jnp.int32, (PANEL, PANEL), 0)
    block_col = lax.broadcasted_iota(jnp.int32, (PANEL, PANEL), 1)
    for first in range(0, order, PANEL):
        end = first + PANEL
        column = a_ref[first:, first:end]
        if first:
            done = split3(lower_ref[first:, :first])
            column = column - product(done, tuple(term[:PANEL] for term in done), NT)
        tiles = []
        for t in range(PANEL // SUB):
            eye = jnp.where(lane == sub + SUB * t, 1.0, 0.0)
            tiles.append(jnp.concatenate([column[SUB * t : SUB * t + SUB], eye], 1))
        both = jnp.concatenate(factor_panel(tiles, 0), 0)
        upper_ref[first:end, first:end] = jnp.where(block_col >= block_row, both[:, :PANEL], 0.0)
        own = both[:, PANEL:]
        own_terms = split3(own)
        if end < order:
            lower = product(split3(column[PANEL:]), own_terms, NT)
            lower_ref[end:, first:end] = lower
            upper_ref[first:end, end:] = lower.T
        if first:
            behind = product(tuple(term[:PANEL] for term in done), split3(inverse_ref[:first, :first]), NN)
            inverse_ref[first:end, :first] = -product(own_terms, split3(behind), NN)
        inverse_ref[first:end, first:end] = own


def gram_kernel(pieces, me_ref, own_ref, *refs):
    piece_refs, (root_ref, total_ref) = refs[: pieces - 1], refs[pieces - 1 : pieces + 1]
    high_ref, low_ref, keep_ref, send_ref, scaled_ref, sum_ref = refs[pieces + 1 :]
    me = me_ref[0]
    rows, cells = own_ref.shape
    main = cross = None
    for first in range(0, cells, STEP):
        at = slice(first, min(first + STEP, cells))
        root = root_ref[:, at]
        for k, ref in enumerate((own_ref, *piece_refs)):
            scaled_ref[pl.ds(pl.multiple_of((me ^ k) * rows, rows), rows), at] = ref[:, at] * root
        high, low = split2(scaled_ref[:, at])
        high_ref[:, at] = high
        low_ref[:, at] = low
        more_main, more_cross = dot(high, high, NT), dot(high, low, NT)
        main, cross = (main + more_main, cross + more_cross) if first else (more_main, more_cross)
    sum_ref[...] = main + (cross + cross.T)
    half = sum_ref.shape[0] // 2
    row = lax.broadcasted_iota(jnp.int32, (half, half), 0)
    col = lax.broadcasted_iota(jnp.int32, (half, half), 1)
    last = sum_ref[half:, half:]
    both = jnp.where(row >= col, sum_ref[:half, :half], last)
    corner = jnp.sum(jnp.where(row == col, last, 0.0), axis=0, keepdims=True)
    extra_row = lax.broadcasted_iota(jnp.int32, (SUB, half), 0)
    extra = jnp.where(extra_row == 0, jnp.broadcast_to(corner, (SUB, half)), jnp.broadcast_to(total_ref[...], (SUB, half)))
    off = sum_ref[half:, :half]
    first_core = (me & 1) == 0
    for ref, is_off in ((keep_ref, first_core), (send_ref, jnp.logical_not(first_core))):
        ref[:half, :] = jnp.where(is_off, off, both)
        ref[half:, :] = extra


def form_gram(me, own, pieces, root, total):
    rows, cells = own.shape
    count = len(pieces) + 1
    order = rows * count
    packed = (order // 2 + SUB, order // 2)
    here = pl.BlockSpec(memory_space=pltpu.VMEM)
    return pl.pallas_call(
        functools.partial(gram_kernel, count),
        in_specs=[pl.BlockSpec(memory_space=pltpu.SMEM)] + [here] * (count + 2),
        out_specs=[here] * 4,
        out_shape=[jax.ShapeDtypeStruct((order, cells), BF16)] * 2 + [jax.ShapeDtypeStruct(packed, F32)] * 2,
        scratch_shapes=[pltpu.VMEM((order, cells), F32), pltpu.VMEM((order, order), F32)],
        compiler_params=pltpu.CompilerParams(vmem_limit_bytes=VMEM_LIMIT),
    )(me[None], own, *pieces, root, total)


def solve_kernel(me_ref, mine_ref, other_ref, *refs):
    term_refs, (upper_ref, scores_ref, out_ref, a_ref, inverse_ref, lower_ref, sems) = refs[:-7], refs[-7:]
    half = mine_ref.shape[1]
    first_core = (me_ref[0] & 1) == 0
    mine, other = mine_ref[...], other_ref[...]
    off = jnp.where(first_core, mine[:half], other[:half])
    both = jnp.where(first_core, other[:half], mine[:half])
    scale = 1.0 / mine[half + 1 : half + 2, :]
    row = lax.broadcasted_iota(jnp.int32, (half, half), 0)
    col = lax.broadcasted_iota(jnp.int32, (half, half), 1)
    turned = both.T
    corner = jnp.broadcast_to(mine[half : half + 1, :], (half, half))
    a_ref[:half, :half] = jnp.where(row >= col, both, turned) * scale
    a_ref[half:, half:] = jnp.where(row < col, both, jnp.where(row > col, turned, corner)) * scale
    a_ref[half:, :half] = off * scale
    cholesky_and_inverse(a_ref, inverse_ref, upper_ref, lower_ref)
    high, low = split2(inverse_ref[...])
    copies, at = [], 0
    for high_ref, low_ref in zip(term_refs[::2], term_refs[1::2]):
        for first in range(0, high_ref.shape[1], STEP):
            here = slice(first, min(first + STEP, high_ref.shape[1]))
            there = slice(at + here.start, at + here.stop)
            high_term = high_ref[:, here]
            out_ref[:, there] = dot(high, high_term, NN) + (dot(high, low_ref[:, here], NN) + dot(low, high_term, NN))
            copies.append(pltpu.make_async_copy(out_ref.at[:, there], scores_ref.at[:, there], sems.at[len(copies)]))
            copies[-1].start()
        at += high_ref.shape[1]
    for copy in copies:
        copy.wait()


def solve(me, mine, other, terms):
    order = terms[0].shape[0]
    cells = [term.shape[1] for term in terms[::2]]
    here, square = pl.BlockSpec(memory_space=pltpu.VMEM), (order, order)
    return pl.pallas_call(
        solve_kernel,
        in_specs=[pl.BlockSpec(memory_space=pltpu.SMEM)] + [here] * (2 + len(terms)),
        out_specs=[here, pl.BlockSpec(memory_space=pl.ANY)],
        out_shape=[jax.ShapeDtypeStruct(square, F32), jax.ShapeDtypeStruct((order, sum(cells)), F32)],
        scratch_shapes=[pltpu.VMEM((order, sum(cells)), F32)]
        + [pltpu.VMEM(square, F32)] * 3
        + [pltpu.SemaphoreType.DMA((sum(-(-c // STEP) for c in cells),))],
        compiler_params=pltpu.CompilerParams(vmem_limit_bytes=VMEM_LIMIT),
    )(me[None], mine, other, *terms)


def swap(x, axis, mask):
    return lax.ppermute(x, axis, [(i, i ^ mask) for i in range(lax.axis_size(axis))])


def sum_over(x, axis, first):
    size = lax.axis_size(axis)
    while first < size:
        if 2 * first < size:
            near, far, both = swap(x, axis, first), swap(x, axis, 2 * first), swap(x, axis, 3 * first)
            x = (x + near) + (far + both)
        else:
            x = x + swap(x, axis, first)
        first *= 4
    return x


def on_device(anomaly, ocean_mask, area_weight):
    size = lax.axis_size("dev")
    me = lax.axis_index("dev")
    cells = anomaly.shape[1] // size
    order = sorted(range(1, size), key=lambda k: (-(k >> 1).bit_count(), k & 1))
    sizes = (cells - cells // 4, cells // 4)
    part = lambda k: lax.dynamic_slice_in_dim(anomaly, (me ^ k) * cells, cells, 1)
    pieces = {k: swap(part(k), "dev", k) for k in (order[0], 1)}
    anomaly, pieces[1] = lax.optimization_barrier((anomaly, pieces[1]))
    pieces |= {k: swap(part(k), "dev", k) for k in order if k not in pieces}
    own = lambda x: lax.dynamic_slice_in_dim(x, me * cells, cells, 0)
    weights = own(area_weight) * own(ocean_mask).astype(F32)
    root = jnp.sqrt(weights)[None, :]
    total = jnp.sum(weights)[None, None]
    high, low, keep, send = form_gram(me, part(0), [pieces[k] for k in range(1, size)], root, total)
    mine = keep + swap(send, "dev", 1)
    mine = sum_over(mine, "dev", 2)
    mine = sum_over(mine, "band", 1)
    other = swap(mine, "dev", 1)
    return tuple(solve(me, mine, other, [high, low]))


def solution(mesh):
    return jax.shard_map(
        on_device,
        mesh=mesh,
        in_specs=(P("dev", "band"), P("band"), P("band")),
        out_specs=(P(), P(None, ("band", "dev"))),
        check_vma=False,
    )
```

time: 243 us -> 84.8 us (0.35)
  blocking collectives: 79.4 us -> 0 us
  other arithmetic: 63.8 us -> 1.39 us
  starting transfers between devices: 0.08 us -> 17.7 us
  between operations: 15.5 us -> 0.7 us
  Pallas kernels: 0 us -> 12.8 us
  matrix products: 12.1 us -> 0 us
  waiting for transfers between devices: 60 us -> 48.5 us
  local copies, waits for them, and re-layouts: 11.4 us -> 3.31 us
    psum x2 -> x0, waiting for transfers between devices: 60 us -> none  [the longest x1 33.1 us: on_device(): gram, total = lax.psum((band_gram, band_total), 'band')]
    another operation x10 -> x0, other arithmetic: 56.4 us -> none  [the longest x6 33.9 us: on_device(): lower = jnp.linalg.cholesky(gram / total)]
    all_to_all x1 -> x0, blocking collectives: 54 us -> none  [on_device(): lax.all_to_all(local_scaled, 'dev', split_axis=1, concat_axis=0, tiled=True)]
    ppermute x0 -> x15, waiting for transfers between devices: none -> 48.5 us  [swap(): lax.ppermute(x, axis, [(i, i ^ mask) for i in range(lax.axis_size(axis))])]
    psum x2 -> x0, blocking collectives: 25.4 us -> none  [the longest x1 12.8 us: on_device(): gram, total = lax.psum((band_gram, band_total), 'band')]
    ppermute x0 -> x15, starting transfers between devices: none -> 17.7 us  [swap(): lax.ppermute(x, axis, [(i, i ^ mask) for i in range(lax.axis_size(axis))])]
    pallas_call x0 -> x2, Pallas kernels: none -> 12.8 us  [the longest x1 10.3 us: solve(): pl.pallas_call(solve_kernel, in_specs=[pl.BlockSpec(memory_space=pltpu.SM...]
    another operation x10 -> x0, local copies, waits for them, and re-layouts: 8.02 us -> none  [the longest x2 4.1 us: on_device(): lax.linalg.triangular_solve(lower, scaled, left_side=True, lower=True)]
  transfers between devices with their start and end apart: 2 -> 15, of which waited for: 2 -> 12; matrix products, arithmetic and copies ran while one was open for 2% -> 4% of each run, Pallas kernels for 0% -> 0%
where the time goes in v2:
time: 84.8 us; the launch traced here: 84.4 us
  waiting for transfers between devices  48.5 us (57%)
  starting transfers between devices  17.7 us (21%)
  Pallas kernels  12.8 us (15%)
  local copies, waits for them, and re-layouts  3.31 us (4%)
  other arithmetic  1.39 us (2%)
    ppermute x15, waiting for transfers between devices, swap(): lax.ppermute(x, axis, [(i, i ^ mask) for i in range(lax.axis_size(axis))])  48.5 us
    ppermute x15, starting transfers between devices, swap(): lax.ppermute(x, axis, [(i, i ^ mask) for i in range(lax.axis_size(axis))])  17.7 us
    pallas_call x1, Pallas kernels, solve(): pl.pallas_call(solve_kernel, in_specs=[pl.BlockSpec(memory_space=pltpu.SM...  10.3 us
    dynamic_slice x2, local copies, waits for them, and re-layouts, on_device(): lax.dynamic_slice_in_dim(anomaly, (me ^ k) * cells, cells, 1)  3.31 us
    pallas_call x1, Pallas kernels, form_gram(): pl.pallas_call(functools.partial(gram_kernel, count), in_specs=[pl.BlockS...  2.52 us
  transfers between devices with their start and end apart: 15, of which 12 were waited for; matrix products, arithmetic and copies ran while one was open for 4% of the time, Pallas kernels for 0%

profile of v2, /device:TPU:0, one launch (start us, length us, event | category | flops | bytes accessed | tf_op | source)
XLA Modules:
  0.0 84.4 jit_solution(7397186467180185905)
XLA Ops:
  0.6 1.3 %constant_dynamic-slice_fusion.1 = (f32[32,4096]{1,0:T(8,128)S(1)}, f32[32,4096]{1,0:T(8,128)S(1)}) fusion(f32[32,32768]{1,0:T(8,128)} %param.3, s32[]{:T(128)S(6)} %select_n.32, s32[]{:T(128)S(6)} %select_n.26), kind=kLoop, calls=%fused_computation.6 | loop fusion | bytes 2097160 | tf_op jit(solution)/shard_map/dynamic_slice | solution.py:235
  2.4 3.5 %collective-permute-start.5 = (f32[32,4096]{1,0:T(8,128)S(1)}, f32[32,4096]{1,0:T(8,128)S(1)}, u32[]{:S(2)}, u32[]{:S(2)}) collective-permute-start(f32[32,4096]{1,0:T(8,128)S(1)} %get-tuple-element.20), channel_id=1, source_target_pairs={{0,6},{1,7},{2,4},{3,5},{4,2},{5,3},{6,0},{7,1},{8,14},{9,15},{10,... | collective-permute-start | bytes 1572872 | tf_op jit(solution)/shard_map/ppermute | solution.py:214
  6.0 2.0 %constant_dynamic-slice_fusion = (f32[32,4096]{1,0:T(8,128)S(1)}, f32[32,4096]{1,0:T(8,128)S(1)}, f32[32,4096]{1,0:T(8,128)S(1)}, f32[32,4096]{1,0:T(8,128)S(1)}...) fusion(f32[32,32768]{1,0:T(8,128)} %param.3, s32[]{:T(128)S(6)} %select_n.33, s32[]{:T(128)S(6)} %select_n.31, ...), kind=kLoop, calls=%fused_computation.5 | loop fusion | bytes 6291480 | tf_op jit(solution)/shard_map/dynamic_slice | solution.py:235
  8.0 1.6 %collective-permute-start.6 = (f32[32,4096]{1,0:T(8,128)S(1)}, f32[32,4096]{1,0:T(8,128)S(1)}, u32[]{:S(2)}, u32[]{:S(2)}) collective-permute-start(f32[32,4096]{1,0:T(8,128)S(1)} %get-tuple-element.14), channel_id=1, source_target_pairs={{0,7},{1,6},{2,5},{3,4},{4,3},{5,2},{6,1},{7,0},{8,15},{9,14},{10,... | collective-permute-start | bytes 1572872 | tf_op jit(solution)/shard_map/ppermute | solution.py:214
  10.1 1.5 %collective-permute-start.3 = (f32[32,4096]{1,0:T(8,128)S(1)}, f32[32,4096]{1,0:T(8,128)S(1)}, u32[]{:S(2)}, u32[]{:S(2)}) collective-permute-start(f32[32,4096]{1,0:T(8,128)S(1)} %get-tuple-element.16), channel_id=1, source_target_pairs={{0,4},{1,5},{2,6},{3,7},{4,0},{5,1},{6,2},{7,3},{8,12},{9,13},{10,... | collective-permute-start | bytes 1572872 | tf_op jit(solution)/shard_map/ppermute | solution.py:214
  11.7 7.2 %collective-permute-done.5.refs_5_ = f32[32,4096]{1,0:T(8,128)S(1)} collective-permute-done((f32[32,4096]{1,0:T(8,128)S(1)}, f32[32,4096]{1,0:T(8,128)S(1)}, u32[]{:S(2)}, u32[]{:S(2)}) %collective-permute-start.5) | collective-permute-done | bytes 524320 | tf_op jit(solution)/shard_map/ppermute | solution.py:214
  18.8 1.9 %collective-permute-start.1 = (f32[32,4096]{1,0:T(8,128)S(1)}, f32[32,4096]{1,0:T(8,128)S(1)}, u32[]{:S(2)}, u32[]{:S(2)}) collective-permute-start(f32[32,4096]{1,0:T(8,128)S(1)} %get-tuple-element.18), channel_id=1, source_target_pairs={{0,2},{1,3},{2,0},{3,1},{4,6},{5,7},{6,4},{7,5},{8,10},{9,11},{10,... | collective-permute-start | bytes 1572872 | tf_op jit(solution)/shard_map/ppermute | solution.py:214
  20.7 1.3 %fusion = (f32[]{:T(128)}, f32[4096]{0:T(1024)S(1)}) fusion(s32[32768]{0:T(1024)} %param.4, s32[]{:T(128)S(6)} %select_n.27, f32[32768]{0:T(1024)} %param.5), kind=kLoop, calls=%fused_computation.3 | loop fusion | flops 12287 | bytes 49160 | tf_op jit(solution)/shard_map/reduce_sum | solution.py:242
  22.1 7.5 %collective-permute-done.6.refs_6_ = f32[32,4096]{1,0:T(8,128)S(1)} collective-permute-done((f32[32,4096]{1,0:T(8,128)S(1)}, f32[32,4096]{1,0:T(8,128)S(1)}, u32[]{:S(2)}, u32[]{:S(2)}) %collective-permute-start.6) | collective-permute-done | bytes 524320 | tf_op jit(solution)/shard_map/ppermute | solution.py:214
  29.6 11.3 %collective-permute-done.4.refs_4_ = f32[32,4096]{1,0:T(8,128)S(1)} collective-permute-done((f32[32,4096]{1,0:T(8,128)S(1)}, f32[32,4096]{1,0:T(8,128)S(1)}, u32[]{:S(2)}, u32[]{:S(2)}) %collective-permute-start.4) | collective-permute-done | bytes 524320 | tf_op jit(solution)/shard_map/ppermute | solution.py:214
  40.9 11.3 %collective-permute-done.3.refs_3_ = f32[32,4096]{1,0:T(8,128)S(1)} collective-permute-done((f32[32,4096]{1,0:T(8,128)S(1)}, f32[32,4096]{1,0:T(8,128)S(1)}, u32[]{:S(2)}, u32[]{:S(2)}) %collective-permute-start.3) | collective-permute-done | bytes 524320 | tf_op jit(solution)/shard_map/ppermute | solution.py:214
  52.5 2.5 %shard_map.50 = (bf16[256,4096]{1,0:T(8,128)(2,1)S(1)}, bf16[256,4096]{1,0:T(8,128)(2,1)S(1)}, f32[136,128]{1,0:T(8,128)S(1)}, f32[136,128]{1,0:T(8,128)S(1)}) custom-call(s32[1]{0:T(128)} %bitcast.me_ref, f32[32,4096]{1,0:T(8,128)S(1)} %get-tuple-element.19.own_ref, f32[32,4096]{1,0:T(8,128)S(1)} %collective-permute-done.refs_0_, ...), custom_call_target="tpu_custom_call" | custom-call | tf_op jit(solution)/shard_map/pallas_call | solution.py:156
  55.1 1.2 %collective-permute-done.7 = f32[136,128]{1,0:T(8,128)S(1)} collective-permute-done((f32[136,128]{1,0:T(8,128)S(1)}, f32[136,128]{1,0:T(8,128)S(1)}, u32[]{:S(2)}, u32[]{:S(2)}) %collective-permute-start.7) | collective-permute-done | bytes 69664 | tf_op jit(solution)/shard_map/ppermute | solution.py:214
  56.4 2.4 %collective-permute-start.10 = (f32[136,128]{1,0:T(8,128)S(1)}, f32[136,128]{1,0:T(8,128)S(1)}, u32[]{:S(2)}, u32[]{:S(2)}) collective-permute-start(f32[136,128]{1,0:T(8,128)S(1)} %add.55), channel_id=1, source_target_pairs={{0,6},{1,7},{2,4},{3,5},{4,2},{5,3},{6,0},{7,1},{8,14},{9,15},{10,... | collective-permute-start | bytes 208904 | tf_op jit(solution)/shard_map/ppermute | solution.py:214
  58.8 0.6 collective-permute-start.9
  59.9 1.8 %collective-permute-done.10 = f32[136,128]{1,0:T(8,128)S(1)} collective-permute-done((f32[136,128]{1,0:T(8,128)S(1)}, f32[136,128]{1,0:T(8,128)S(1)}, u32[]{:S(2)}, u32[]{:S(2)}) %collective-permute-start.10) | collective-permute-done | bytes 69664 | tf_op jit(solution)/shard_map/ppermute | solution.py:214
  61.7 1.5 %collective-permute-done.9 = f32[136,128]{1,0:T(8,128)S(1)} collective-permute-done((f32[136,128]{1,0:T(8,128)S(1)}, f32[136,128]{1,0:T(8,128)S(1)}, u32[]{:S(2)}, u32[]{:S(2)}) %collective-permute-start.9) | collective-permute-done | bytes 69664 | tf_op jit(solution)/shard_map/ppermute | solution.py:214
  63.1 0.6 collective-permute-done.8
  63.7 3.7 %collective-permute-start.13 = (f32[136,128]{1,0:T(8,128)S(1)}, f32[136,128]{1,0:T(8,128)S(1)}, u32[]{:S(2)}, u32[]{:S(2)}) collective-permute-start(f32[136,128]{1,0:T(8,128)S(1)} %add_add_fusion.1), channel_id=1, source_target_pairs={{0,24},{8,16},{16,8},{24,0},{1,25},{9,17},{17,9},{25,1},{2,26},{10... | collective-permute-start | bytes 208904 | tf_op jit(solution)/shard_map/ppermute | solution.py:214
  67.4 0.8 collective-permute-start.11
  68.2 1.9 %collective-permute-done.13 = f32[136,128]{1,0:T(8,128)S(1)} collective-permute-done((f32[136,128]{1,0:T(8,128)S(1)}, f32[136,128]{1,0:T(8,128)S(1)}, u32[]{:S(2)}, u32[]{:S(2)}) %collective-permute-start.13) | collective-permute-done | bytes 69664 | tf_op jit(solution)/shard_map/ppermute | solution.py:214
  70.0 2.8 %collective-permute-done.12 = f32[136,128]{1,0:T(8,128)S(1)} collective-permute-done((f32[136,128]{1,0:T(8,128)S(1)}, f32[136,128]{1,0:T(8,128)S(1)}, u32[]{:S(2)}, u32[]{:S(2)}) %collective-permute-start.12) | collective-permute-done | bytes 69664 | tf_op jit(solution)/shard_map/ppermute | solution.py:214
  72.9 1.2 %collective-permute-done.14.other_ref = f32[136,128]{1,0:T(8,128)S(1)} collective-permute-done((f32[136,128]{1,0:T(8,128)S(1)}, f32[136,128]{1,0:T(8,128)S(1)}, u32[]{:S(2)}, u32[]{:S(2)}) %collective-permute-start.14) | collective-permute-done | bytes 69664 | tf_op jit(solution)/shard_map/ppermute | solution.py:214
  74.2 10.3 %shard_map.51 = (f32[256,256]{1,0:T(8,128)}, f32[256,4096]{1,0:T(8,128)}) custom-call(s32[1]{0:T(128)} %bitcast.me_ref, f32[136,128]{1,0:T(8,128)S(1)} %add_add_fusion.mine_ref, f32[136,128]{1,0:T(8,128)S(1)} %collective-permute-done.14.other_ref, bf16[256,4096]{1,0:T(8,128)(2,1)S(1)} %get-tuple-element.12.refs_0_, ...), custom_call_target="tpu_custom_call" | custom-call | tf_op jit(solution)/shard_map/pallas_call | solution.py:201
  (14 shorter events, 2.1 us)
Async XLA Ops:
  1.9 4.0 %collective-permute-start = (f32[32,4096]{1,0:T(8,128)S(1)}, f32[32,4096]{1,0:T(8,128)S(1)}, u32[]{:S(2)}, u32[]{:S(2)}) collective-permute-start(f32[32,4096]{1,0:T(8,128)S(1)} %get-tuple-element.21), channel_id=1, source_target_pairs={{0,1},{1,0},{2,3},{3,2},{4,5},{5,4},{6,7},{7,6},{8,9},{9,8},{10,11... | collective-permute-start | bytes 1572872 | tf_op jit(solution)/shard_map/ppermute | solution.py:214
  2.4 16.4 %collective-permute-start.5 = (f32[32,4096]{1,0:T(8,128)S(1)}, f32[32,4096]{1,0:T(8,128)S(1)}, u32[]{:S(2)}, u32[]{:S(2)}) collective-permute-start(f32[32,4096]{1,0:T(8,128)S(1)} %get-tuple-element.20), channel_id=1, source_target_pairs={{0,6},{1,7},{2,4},{3,5},{4,2},{5,3},{6,0},{7,1},{8,14},{9,15},{10,... | collective-permute-start | bytes 1572872 | tf_op jit(solution)/shard_map/ppermute | solution.py:214
  8.0 21.5 %collective-permute-start.6 = (f32[32,4096]{1,0:T(8,128)S(1)}, f32[32,4096]{1,0:T(8,128)S(1)}, u32[]{:S(2)}, u32[]{:S(2)}) collective-permute-start(f32[32,4096]{1,0:T(8,128)S(1)} %get-tuple-element.14), channel_id=1, source_target_pairs={{0,7},{1,6},{2,5},{3,4},{4,3},{5,2},{6,1},{7,0},{8,15},{9,14},{10,... | collective-permute-start | bytes 1572872 | tf_op jit(solution)/shard_map/ppermute | solution.py:214
  9.6 31.3 %collective-permute-start.4 = (f32[32,4096]{1,0:T(8,128)S(1)}, f32[32,4096]{1,0:T(8,128)S(1)}, u32[]{:S(2)}, u32[]{:S(2)}) collective-permute-start(f32[32,4096]{1,0:T(8,128)S(1)} %get-tuple-element.15), channel_id=1, source_target_pairs={{0,5},{1,4},{2,7},{3,6},{4,1},{5,0},{6,3},{7,2},{8,13},{9,12},{10,... | collective-permute-start | bytes 1572872 | tf_op jit(solution)/shard_map/ppermute | solution.py:214
  10.1 42.1 %collective-permute-start.3 = (f32[32,4096]{1,0:T(8,128)S(1)}, f32[32,4096]{1,0:T(8,128)S(1)}, u32[]{:S(2)}, u32[]{:S(2)}) collective-permute-start(f32[32,4096]{1,0:T(8,128)S(1)} %get-tuple-element.16), channel_id=1, source_target_pairs={{0,4},{1,5},{2,6},{3,7},{4,0},{5,1},{6,2},{7,3},{8,12},{9,13},{10,... | collective-permute-start | bytes 1572872 | tf_op jit(solution)/shard_map/ppermute | solution.py:214
  11.7 40.5 %collective-permute-start.2 = (f32[32,4096]{1,0:T(8,128)S(1)}, f32[32,4096]{1,0:T(8,128)S(1)}, u32[]{:S(2)}, u32[]{:S(2)}) collective-permute-start(f32[32,4096]{1,0:T(8,128)S(1)} %get-tuple-element.17), channel_id=1, source_target_pairs={{0,3},{1,2},{2,1},{3,0},{4,7},{5,6},{6,5},{7,4},{8,11},{9,10},{10,... | collective-permute-start | bytes 1572872 | tf_op jit(solution)/shard_map/ppermute | solution.py:214
  18.8 33.7 %collective-permute-start.1 = (f32[32,4096]{1,0:T(8,128)S(1)}, f32[32,4096]{1,0:T(8,128)S(1)}, u32[]{:S(2)}, u32[]{:S(2)}) collective-permute-start(f32[32,4096]{1,0:T(8,128)S(1)} %get-tuple-element.18), channel_id=1, source_target_pairs={{0,2},{1,3},{2,0},{3,1},{4,6},{5,7},{6,4},{7,5},{8,10},{9,11},{10,... | collective-permute-start | bytes 1572872 | tf_op jit(solution)/shard_map/ppermute | solution.py:214
  55.0 1.3 %collective-permute-start.7 = (f32[136,128]{1,0:T(8,128)S(1)}, f32[136,128]{1,0:T(8,128)S(1)}, u32[]{:S(2)}, u32[]{:S(2)}) collective-permute-start(f32[136,128]{1,0:T(8,128)S(1)} %get-tuple-element.11), channel_id=1, source_target_pairs={{0,1},{1,0},{2,3},{3,2},{4,5},{5,4},{6,7},{7,6},{8,9},{9,8},{10,11... | collective-permute-start | bytes 208904 | tf_op jit(solution)/shard_map/ppermute | solution.py:214
  56.4 5.3 %collective-permute-start.10 = (f32[136,128]{1,0:T(8,128)S(1)}, f32[136,128]{1,0:T(8,128)S(1)}, u32[]{:S(2)}, u32[]{:S(2)}) collective-permute-start(f32[136,128]{1,0:T(8,128)S(1)} %add.55), channel_id=1, source_target_pairs={{0,6},{1,7},{2,4},{3,5},{4,2},{5,3},{6,0},{7,1},{8,14},{9,15},{10,... | collective-permute-start | bytes 208904 | tf_op jit(solution)/shard_map/ppermute | solution.py:214
  58.8 4.3 %collective-permute-start.9 = (f32[136,128]{1,0:T(8,128)S(1)}, f32[136,128]{1,0:T(8,128)S(1)}, u32[]{:S(2)}, u32[]{:S(2)}) collective-permute-start(f32[136,128]{1,0:T(8,128)S(1)} %add.55), channel_id=1, source_target_pairs={{0,4},{1,5},{2,6},{3,7},{4,0},{5,1},{6,2},{7,3},{8,12},{9,13},{10,... | collective-permute-start | bytes 208904 | tf_op jit(solution)/shard_map/ppermute | solution.py:214
  59.4 4.3 %collective-permute-start.8 = (f32[136,128]{1,0:T(8,128)S(1)}, f32[136,128]{1,0:T(8,128)S(1)}, u32[]{:S(2)}, u32[]{:S(2)}) collective-permute-start(f32[136,128]{1,0:T(8,128)S(1)} %add.55), channel_id=1, source_target_pairs={{0,2},{1,3},{2,0},{3,1},{4,6},{5,7},{6,4},{7,5},{8,10},{9,11},{10,... | collective-permute-start | bytes 208904 | tf_op jit(solution)/shard_map/ppermute | solution.py:214
  63.7 6.3 %collective-permute-start.13 = (f32[136,128]{1,0:T(8,128)S(1)}, f32[136,128]{1,0:T(8,128)S(1)}, u32[]{:S(2)}, u32[]{:S(2)}) collective-permute-start(f32[136,128]{1,0:T(8,128)S(1)} %add_add_fusion.1), channel_id=1, source_target_pairs={{0,24},{8,16},{16,8},{24,0},{1,25},{9,17},{17,9},{25,1},{2,26},{10... | collective-permute-start | bytes 208904 | tf_op jit(solution)/shard_map/ppermute | solution.py:214
  67.4 5.4 %collective-permute-start.12 = (f32[136,128]{1,0:T(8,128)S(1)}, f32[136,128]{1,0:T(8,128)S(1)}, u32[]{:S(2)}, u32[]{:S(2)}) collective-permute-start(f32[136,128]{1,0:T(8,128)S(1)} %add_add_fusion.1), channel_id=1, source_target_pairs={{0,16},{8,24},{16,0},{24,8},{1,17},{9,25},{17,1},{25,9},{2,18},{10... | collective-permute-start | bytes 208904 | tf_op jit(solution)/shard_map/ppermute | solution.py:214
  67.4 5.4 %collective-permute-start.11 = (f32[136,128]{1,0:T(8,128)S(1)}, f32[136,128]{1,0:T(8,128)S(1)}, u32[]{:S(2)}, u32[]{:S(2)}) collective-permute-start(f32[136,128]{1,0:T(8,128)S(1)} %add_add_fusion.1), channel_id=1, source_target_pairs={{0,8},{8,0},{16,24},{24,16},{1,9},{9,1},{17,25},{25,17},{2,10},{10... | collective-permute-start | bytes 208904 | tf_op jit(solution)/shard_map/ppermute | solution.py:214
  72.8 1.3 %collective-permute-start.14 = (f32[136,128]{1,0:T(8,128)S(1)}, f32[136,128]{1,0:T(8,128)S(1)}, u32[]{:S(2)}, u32[]{:S(2)}) collective-permute-start(f32[136,128]{1,0:T(8,128)S(1)} %add_add_fusion.mine_ref), channel_id=1, source_target_pairs={{0,1},{1,0},{2,3},{3,2},{4,5},{5,4},{6,7},{7,6},{8,9},{9,8},{10,11... | collective-permute-start | bytes 208904 | tf_op jit(solution)/shard_map/ppermute | solution.py:214

commit v3 on v2

--- a/solution.py
+++ b/solution.py
@@ -13,6 +13,11 @@
 NT = (((1,), (1,)), ((), ()))
 VMEM_LIMIT = 24 * 1024 * 1024
 STEP = 512
+RUN = 1024
+PARTS = RUN // LANE
+KEPT = 3 * RUN // 4
+STEPS = (RUN - 1).bit_length()
+ALL_VMEM = 62 * 1024 * 1024
 
 
 def split2(x):
@@ -115,23 +120,216 @@
         inverse_ref[first:end, first:end] = own
 
 
-def gram_kernel(pieces, me_ref, own_ref, *refs):
-    piece_refs, (root_ref, total_ref) = refs[: pieces - 1], refs[pieces - 1 : pieces + 1]
-    high_ref, low_ref, keep_ref, send_ref, scaled_ref, sum_ref = refs[pieces + 1 :]
+HERE = pl.BlockSpec(memory_space=pltpu.VMEM)
+SCALARS = pl.BlockSpec(memory_space=pltpu.SMEM)
+
+
+def call(kernel, operands, outs, scratch=(), scalars=1, us=1):
+    return pl.pallas_call(
+        kernel,
+        in_specs=[SCALARS] * scalars + [HERE] * (len(operands) - scalars),
+        out_specs=[HERE] * len(outs),
+        out_shape=outs,
+        scratch_shapes=scratch,
+        compiler_params=pltpu.CompilerParams(vmem_limit_bytes=VMEM_LIMIT),
+        cost_estimate=pl.CostEstimate(flops=us * 1_000_000_000, bytes_accessed=us * 3_600_000, transcendentals=0),
+    )(*operands)
+
+
+def shift_left(parts, by):
+    if by >= LANE:
+        return parts[by // LANE :] + [jnp.zeros_like(parts[0])] * (by // LANE)
+    lane = lax.broadcasted_iota(jnp.int32, parts[0].shape, 1)
+    turned = [pltpu.roll(part, LANE - by, 1) for part in parts] + [jnp.zeros_like(parts[0])]
+    return [jnp.where(lane < LANE - by, here, after) for here, after in zip(turned, turned[1:])]
+
+
+def plan(mask_ref, source_ref, rank_ref, over_ref, gap_ref):
+    groups = mask_ref.shape[0]
+    runs = groups // PARTS
+    chunk = min(groups, 2 * LANE)
+    bit = lambda keep: jnp.where(keep, 1.0, 0.0).astype(BF16)
+    iota = lambda shape, axis: lax.broadcasted_iota(jnp.int32, shape, axis)
+    before = bit(iota((LANE, LANE), 0) < iota((LANE, LANE), 1))
+    row, col = iota((chunk, chunk), 0), iota((chunk, chunk), 1)
+    earlier = bit((row // PARTS == col // PARTS) & (col < row))
+    for first in range(0, groups, chunk):
+        mask = mask_ref[first : first + chunk, :]
+        land = (1 - mask).astype(F32).astype(BF16)
+        carried = dot(dot(earlier, land, NN).astype(BF16), jnp.ones((LANE, LANE), BF16), NN)
+        gap_ref[first : first + chunk, :] = (dot(land, before, NN) + carried).astype(jnp.int32)
+    mask = [mask_ref[pl.ds(p, runs, stride=PARTS), :] for p in range(PARTS)]
+    gap = [gap_ref[pl.ds(p, runs, stride=PARTS), :] for p in range(PARTS)]
+    last = gap[-1] + (1 - mask[-1])
+    count = RUN - jnp.broadcast_to(last[:, LANE - 1 :], (runs, LANE))
+    over_ref[...] = jnp.broadcast_to(jnp.max(jnp.where(count > KEPT, 1.0, 0.0), axis=0, keepdims=True), (SUB, LANE))
+    lane = iota((runs, LANE), 1)
+    for p in range(PARTS):
+        rank_ref[p] = jnp.where(mask[p] != 0, lane + p * LANE - gap[p], -1)
+    gap = [g * m for g, m in zip(gap, mask)]
+    for step in range(STEPS):
+        moved = [jnp.where((g & (1 << step)) != 0, g, 0) for g in gap]
+        gap = [g - m + a for g, m, a in zip(gap, moved, shift_left(moved, 1 << step))]
+    for p in range(PARTS):
+        at = lane + p * LANE
+        source_ref[p] = jnp.where(at < count, at + gap[p], -1)
+
+
+def across(ref, at, run):
+    return jnp.broadcast_to(ref[at, pl.ds(run, 1), :], (SUB, LANE))
+
+
+def gathered(parts, index):
+    lane, part = index & (LANE - 1), index >> (LANE.bit_length() - 1)
+    out = jnp.zeros((SUB, LANE), F32)
+    for p, x in parts.items():
+        out = jnp.where(part == p, jnp.take_along_axis(x, lane, axis=1, mode="promise_in_bounds"), out)
+    return out
+
+
+def pack(to, x_ref, root_ref, source_ref, out_ref, first):
+    rows, cells = x_ref.shape
+    runs = cells // RUN
+    width = out_ref.shape[1] // runs
+    for run in range(runs):
+        places = range(first // LANE, (first + width) // LANE)
+        index = {p: across(source_ref, p, to * runs + run) for p in places}
+        for t in range(0, rows, SUB):
+            parts = []
+            for group in range(run * PARTS, (run + 1) * PARTS):
+                root = jnp.broadcast_to(root_ref[group : group + 1, :], (SUB, LANE))
+                parts.append(x_ref[t : t + SUB, group * LANE : (group + 1) * LANE] * root)
+            for p in places:
+                at = run * width + p * LANE - first
+                out_ref[t : t + SUB, at : at + LANE] = gathered({i: parts[i] for i in range(p, PARTS)}, index[p])
+
+
+def slice_copies(to, x_ref, area_ref, own_ref, own_area_ref, sems):
+    cells = own_ref.shape[1]
+    groups = cells // LANE
+    return [
+        pltpu.make_async_copy(area_ref.at[pl.ds(pl.multiple_of(to * groups, groups), groups), :], own_area_ref, sems.at[0]),
+        pltpu.make_async_copy(x_ref.at[:, pl.ds(pl.multiple_of(to * cells, cells), cells)], own_ref, sems.at[1]),
+    ]
+
+
+def first_kernel(to_ref, x_ref, mask_ref, area_ref, source_ref, rank_ref, over_ref, kept_ref, *scratch):
+    own_ref, own_area_ref, root_ref, whole_mask_ref, gap_ref, sems = scratch
+    groups = own_area_ref.shape[0]
+    to = to_ref[0]
+    mask_copy = pltpu.make_async_copy(mask_ref, whole_mask_ref, sems.at[2])
+    mask_copy.start()
+    copies = slice_copies(to, x_ref, area_ref, own_ref, own_area_ref, sems)
+    for copy in copies:
+        copy.start()
+    mask_copy.wait()
+    plan(whole_mask_ref, source_ref, rank_ref, over_ref, gap_ref)
+    for copy in copies:
+        copy.wait()
+    mask = whole_mask_ref[pl.ds(pl.multiple_of(to * groups, groups), groups), :]
+    root_ref[...] = jnp.sqrt(own_area_ref[...] * mask.astype(F32))
+    pack(to, own_ref, root_ref, source_ref, kept_ref, 0)
+
+
+def second_kernel(to_ref, x_ref, mask_ref, area_ref, source_ref, gate_ref, kept_ref, *scratch):
+    own_ref, own_area_ref, root_ref, own_mask_ref, sems = scratch
+    groups = own_area_ref.shape[0]
+    to = to_ref[0]
+    at = pl.ds(pl.multiple_of(to * groups, groups), groups)
+    copies = slice_copies(to, x_ref, area_ref, own_ref, own_area_ref, sems)
+    copies.append(pltpu.make_async_copy(mask_ref.at[at, :], own_mask_ref, sems.at[2]))
+    for copy in copies:
+        copy.start()
+    for copy in copies:
+        copy.wait()
+    root_ref[...] = jnp.sqrt(own_area_ref[...] * own_mask_ref[...].astype(F32))
+    pack(to, own_ref, root_ref, source_ref, kept_ref, 0)
+
+
+def pack_early(to, anomaly, mask, area, cells, source=None, gate=None):
+    rows, groups, own_groups = anomaly.shape[0], mask.shape[0], cells // LANE
+    moves = jax.ShapeDtypeStruct((PARTS, groups // PARTS, LANE), jnp.int32)
+    outs = [jax.ShapeDtypeStruct((rows, cells // RUN * KEPT), F32)]
+    scratch = [pltpu.VMEM((rows, cells), F32)] + [pltpu.VMEM((own_groups, LANE), F32)] * 2
+    operands, specs = [to[None], anomaly, mask, area], [SCALARS] + [pl.BlockSpec(memory_space=pl.ANY)] * 3
+    if source is None:
+        kernel = first_kernel
+        outs = [moves, moves, jax.ShapeDtypeStruct((SUB, LANE), F32)] + outs
+        scratch += [pltpu.VMEM((groups, LANE), jnp.int32)] * 2
+    else:
+        kernel = second_kernel
+        operands, specs = operands + [source, gate], specs + [HERE] * 2
+        scratch += [pltpu.VMEM((own_groups, LANE), jnp.int32)]
+    return pl.pallas_call(
+        kernel,
+        in_specs=specs,
+        out_specs=[HERE] * len(outs),
+        out_shape=outs,
+        scratch_shapes=scratch + [pltpu.SemaphoreType.DMA((3,))],
+        compiler_params=pltpu.CompilerParams(vmem_limit_bytes=ALL_VMEM),
+        cost_estimate=pl.CostEstimate(flops=2_000_000_000, bytes_accessed=7_200_000, transcendentals=0),
+    )(*operands)
+
+
+def pack_kernel(first, to_ref, x_ref, mask_ref, area_ref, source_ref, out_ref, root_ref):
+    groups = x_ref.shape[1] // LANE
+    to = to_ref[0]
+    at = pl.ds(pl.multiple_of(to * groups, groups), groups)
+    root_ref[...] = jnp.sqrt(area_ref[at, :] * mask_ref[at, :].astype(F32))
+    pack(to, x_ref, root_ref, source_ref, out_ref, first)
+
+
+def pack_cells(to, x, mask, area, source, rest=False):
+    rows, cells = x.shape
+    out = jax.ShapeDtypeStruct((rows, cells // RUN * (RUN - KEPT if rest else KEPT)), F32)
+    kernel = functools.partial(pack_kernel, KEPT if rest else 0)
+    return call(kernel, [to[None], x, mask, area, source], [out], [pltpu.VMEM((cells // LANE, LANE), F32)])[0]
+
+
+def spread_kernel(me_ref, rank_ref, kept_ref, *refs):
+    out_ref = refs[-1]
+    rows, cells = out_ref.shape
+    runs = cells // RUN
     me = me_ref[0]
-    rows, cells = own_ref.shape
+    for run in range(runs):
+        index = [across(rank_ref, p, me * runs + run) for p in range(PARTS)]
+        for t in range(0, rows, SUB):
+            parts = [kept_ref[t : t + SUB, first : first + LANE] for first in range(run * KEPT, (run + 1) * KEPT, LANE)]
+            for ref in refs[:-1]:
+                width = RUN - KEPT
+                parts += [ref[t : t + SUB, first : first + LANE] for first in range(run * width, (run + 1) * width, LANE)]
+            for p in range(PARTS):
+                first = run * RUN + p * LANE
+                out_ref[t : t + SUB, first : first + LANE] = gathered({i: parts[i] for i in range(min(p + 1, len(parts)))}, index[p])
+
+
+def spread(me, rank, kept, *rest):
+    out = jax.ShapeDtypeStruct((kept.shape[0], kept.shape[1] // KEPT * RUN), F32)
+    return call(spread_kernel, [me[None], rank, kept, *rest], [out])[0]
+
+
+def place(me, refs, at, whole_ref):
+    rows = refs[0].shape[0]
+    for k, ref in enumerate(refs):
+        whole_ref[pl.ds(pl.multiple_of((me ^ k) * rows, rows), rows), at] = ref[:, at]
+
+
+def products(me, piece_refs, whole_ref):
     main = cross = None
+    cells = piece_refs[0].shape[1]
     for first in range(0, cells, STEP):
         at = slice(first, min(first + STEP, cells))
-        root = root_ref[:, at]
-        for k, ref in enumerate((own_ref, *piece_refs)):
-            scaled_ref[pl.ds(pl.multiple_of((me ^ k) * rows, rows), rows), at] = ref[:, at] * root
-        high, low = split2(scaled_ref[:, at])
-        high_ref[:, at] = high
-        low_ref[:, at] = low
+        place(me, piece_refs, at, whole_ref)
+        high, low = split2(whole_ref[:, at])
         more_main, more_cross = dot(high, high, NT), dot(high, low, NT)
         main, cross = (main + more_main, cross + more_cross) if first else (more_main, more_cross)
-    sum_ref[...] = main + (cross + cross.T)
+    return main + (cross + cross.T)
+
+
+def gram_kernel(pieces, me_ref, *refs):
+    piece_refs, (total_ref, over_ref, keep_ref, send_ref, whole_ref, sum_ref) = refs[:pieces], refs[pieces:]
+    me = me_ref[0]
+    sum_ref[...] = products(me, piece_refs, whole_ref)
     half = sum_ref.shape[0] // 2
     row = lax.broadcasted_iota(jnp.int32, (half, half), 0)
     col = lax.broadcasted_iota(jnp.int32, (half, half), 1)
@@ -140,6 +338,7 @@
     corner = jnp.sum(jnp.where(row == col, last, 0.0), axis=0, keepdims=True)
     extra_row = lax.broadcasted_iota(jnp.int32, (SUB, half), 0)
     extra = jnp.where(extra_row == 0, jnp.broadcast_to(corner, (SUB, half)), jnp.broadcast_to(total_ref[...], (SUB, half)))
+    extra = jnp.where(extra_row == SUB - 1, jnp.broadcast_to(over_ref[:1, :1], (SUB, half)), extra)
     off = sum_ref[half:, :half]
     first_core = (me & 1) == 0
     for ref, is_off in ((keep_ref, first_core), (send_ref, jnp.logical_not(first_core))):
@@ -147,20 +346,25 @@
         ref[half:, :] = extra
 
 
-def form_gram(me, own, pieces, root, total):
-    rows, cells = own.shape
-    count = len(pieces) + 1
-    order = rows * count
-    packed = (order // 2 + SUB, order // 2)
-    here = pl.BlockSpec(memory_space=pltpu.VMEM)
-    return pl.pallas_call(
-        functools.partial(gram_kernel, count),
-        in_specs=[pl.BlockSpec(memory_space=pltpu.SMEM)] + [here] * (count + 2),
-        out_specs=[here] * 4,
-        out_shape=[jax.ShapeDtypeStruct((order, cells), BF16)] * 2 + [jax.ShapeDtypeStruct(packed, F32)] * 2,
-        scratch_shapes=[pltpu.VMEM((order, cells), F32), pltpu.VMEM((order, order), F32)],
-        compiler_params=pltpu.CompilerParams(vmem_limit_bytes=VMEM_LIMIT),
-    )(me[None], own, *pieces, root, total)
+def form_gram(me, pieces, total, over):
+    rows, cells = pieces[0].shape
+    order = rows * len(pieces)
+    packed = jax.ShapeDtypeStruct((order // 2 + SUB, order // 2), F32)
+    scratch = [pltpu.VMEM((order, cells), F32), pltpu.VMEM((order, order), F32)]
+    return call(functools.partial(gram_kernel, len(pieces)), [me[None], *pieces, total, over], [packed] * 2, scratch, us=2)
+
+
+def terms_kernel(pieces, me_ref, *refs):
+    piece_refs, (high_ref, low_ref, whole_ref) = refs[:pieces], refs[pieces:]
+    place(me_ref[0], piece_refs, slice(None), whole_ref)
+    high_ref[...], low_ref[...] = split2(whole_ref[...])
+
+
+def form_terms(me, pieces):
+    rows, cells = pieces[0].shape
+    out = jax.ShapeDtypeStruct((rows * len(pieces), cells), BF16)
+    scratch = [pltpu.VMEM(out.shape, F32)]
+    return call(functools.partial(terms_kernel, len(pieces)), [me[None], *pieces], [out] * 2, scratch)
 
 
 def solve_kernel(me_ref, mine_ref, other_ref, *refs):
@@ -214,16 +418,23 @@
     return lax.ppermute(x, axis, [(i, i ^ mask) for i in range(lax.axis_size(axis))])
 
 
-def sum_over(x, axis, first):
+def reduce_over(op, x, axis, first):
     size = lax.axis_size(axis)
     while first < size:
         if 2 * first < size:
             near, far, both = swap(x, axis, first), swap(x, axis, 2 * first), swap(x, axis, 3 * first)
-            x = (x + near) + (far + both)
+            x = op(op(x, near), op(far, both))
         else:
-            x = x + swap(x, axis, first)
+            x = op(x, swap(x, axis, first))
         first *= 4
     return x
+
+
+def sum_all(keep, send):
+    mine = keep + swap(send, "dev", 1)
+    mine = reduce_over(jnp.add, mine, "dev", 2)
+    mine = reduce_over(jnp.add, mine, "band", 1)
+    return mine, swap(mine, "dev", 1)
 
 
 def on_device(anomaly, ocean_mask, area_weight):
@@ -231,21 +442,53 @@
     me = lax.axis_index("dev")
     cells = anomaly.shape[1] // size
     order = sorted(range(1, size), key=lambda k: (-(k >> 1).bit_count(), k & 1))
-    sizes = (cells - cells // 4, cells // 4)
+    mask, area = ocean_mask.reshape(-1, LANE), area_weight.reshape(-1, LANE)
+    others, every = range(1, size), range(size)
     part = lambda k: lax.dynamic_slice_in_dim(anomaly, (me ^ k) * cells, cells, 1)
-    pieces = {k: swap(part(k), "dev", k) for k in (order[0], 1)}
-    anomaly, pieces[1] = lax.optimization_barrier((anomaly, pieces[1]))
-    pieces |= {k: swap(part(k), "dev", k) for k in order if k not in pieces}
-    own = lambda x: lax.dynamic_slice_in_dim(x, me * cells, cells, 0)
-    weights = own(area_weight) * own(ocean_mask).astype(F32)
-    root = jnp.sqrt(weights)[None, :]
+    kept = {}
+    source, rank, over, packed = pack_early(me ^ order[0], anomaly, mask, area, cells)
+    kept[order[0]] = swap(packed, "dev", order[0])
+    if size > 2:
+        packed = pack_early(me ^ order[1], anomaly, mask, area, cells, source, swap(over, "dev", 1))[0]
+        kept[order[1]] = swap(packed, "dev", order[1])
+        anomaly, source, packed = lax.optimization_barrier((anomaly, source, packed))
+    for k in (*order[2:], 0):
+        packed = pack_cells(me ^ k, part(k), mask, area, source)
+        kept[k] = swap(packed, "dev", k) if k else packed
+    cut = lambda x: lax.dynamic_slice_in_dim(x, me * cells, cells, 0)
+    weights = cut(area_weight) * cut(ocean_mask).astype(F32)
     total = jnp.sum(weights)[None, None]
-    high, low, keep, send = form_gram(me, part(0), [pieces[k] for k in range(1, size)], root, total)
+    scaled = part(0) * jnp.sqrt(weights)[None, :]
+    late = order[-3:-1]
+    pieces = {k: spread(me, rank, kept[k]) for k in others if k not in late}
+    pieces[0] = scaled
+    last = kept[late[-1]] if late else kept[1]
+    last, pieces = lax.optimization_barrier((last, pieces))
+    if late:
+        kept[late[-1]] = last
+    kept = [kept[k] for k in every]
+    keep, send = form_gram(me, kept, total, over)
     mine = keep + swap(send, "dev", 1)
-    mine = sum_over(mine, "dev", 2)
-    mine = sum_over(mine, "band", 1)
+    for k, axis, first in zip(late, ("dev", "band"), (2, 1)):
+        mine, rank = lax.optimization_barrier((mine, rank))
+        pieces[k] = spread(me, rank, kept[k])
+        mine = reduce_over(jnp.add, mine, axis, first)
+    terms = form_terms(me, [pieces[k] for k in every])
+    mine, terms = lax.optimization_barrier((mine, terms))
     other = swap(mine, "dev", 1)
-    return tuple(solve(me, mine, other, [high, low]))
+    flag = mine[-1, 0] > 0
+
+    def all_sent(mine, other):
+        return solve(me, mine, other, terms)
+
+    def send_rest(mine, other):
+        rest = [pack_cells(me ^ k, part(k), mask, area, source, True) for k in every]
+        rest = rest[:1] + [swap(x, "dev", k) for k, x in zip(others, rest[1:])]
+        more_mine, more_other = sum_all(*form_gram(me, rest, jnp.zeros_like(total), over))
+        pieces = [scaled] + [spread(me, rank, kept[k], rest[k]) for k in others]
+        return solve(me, mine + more_mine, other + more_other, form_terms(me, pieces))
+
+    return tuple(lax.cond(flag, send_rest, all_sent, mine, other))
 
 
 def solution(mesh):

time: 84.8 us -> 75.5 us (0.89)
  waiting for transfers between devices: 48.5 us -> 17.8 us
  Pallas kernels: 12.8 us -> 33.4 us
  local copies, waits for them, and re-layouts: 3.31 us -> 1.12 us
  other arithmetic: 1.39 us -> 2.9 us
  between operations: 0.7 us -> 1.61 us
    ppermute x15 -> x16, waiting for transfers between devices: 48.5 us -> 17.8 us  [swap(): lax.ppermute(x, axis, [(i, i ^ mask) for i in range(lax.axis_size(axis))])]
    pallas_call x1 -> x17, Pallas kernels: 2.52 us -> 23.1 us  [the longest x15 16 us: call(): pl.pallas_call(kernel, in_specs=[SCALARS] * scalars + [HERE] * (len(opera...]
    dynamic_slice x2 -> x0, local copies, waits for them, and re-layouts: 3.31 us -> none  [on_device(): lax.dynamic_slice_in_dim(anomaly, (me ^ k) * cells, cells, 1)]
    dynamic_slice x0 -> x1, other arithmetic: none -> 2.23 us  [on_device(): lax.dynamic_slice_in_dim(anomaly, (me ^ k) * cells, cells, 1)]
    ppermute x15 -> x16, starting transfers between devices: 17.7 us -> 18.1 us  [swap(): lax.ppermute(x, axis, [(i, i ^ mask) for i in range(lax.axis_size(axis))])]
  transfers between devices with their start and end apart: 15 -> 16, of which waited for: 12 -> 9; matrix products, arithmetic and copies ran while one was open for 4% -> 4% of each run, Pallas kernels for 0% -> 23%
where the time goes in v3:
time: 75.5 us; the launch traced here: 75.2 us
  Pallas kernels  33.4 us (44%)
  starting transfers between devices  18.1 us (24%)
  waiting for transfers between devices  17.8 us (24%)
  other arithmetic  2.9 us (4%)
  between operations  1.61 us (2%)
  local copies, waits for them, and re-layouts  1.12 us (1%)
    ppermute x16, starting transfers between devices, swap(): lax.ppermute(x, axis, [(i, i ^ mask) for i in range(lax.axis_size(axis))])  18.1 us
    ppermute x16, waiting for transfers between devices, swap(): lax.ppermute(x, axis, [(i, i ^ mask) for i in range(lax.axis_size(axis))])  17.8 us
    pallas_call x15, Pallas kernels, call(): pl.pallas_call(kernel, in_specs=[SCALARS] * scalars + [HERE] * (len(opera...  16 us
    pallas_call x1, Pallas kernels, solve(): pl.pallas_call(solve_kernel, in_specs=[pl.BlockSpec(memory_space=pltpu.SM...  10.3 us
    pallas_call x2, Pallas kernels, pack_early(): pl.pallas_call(kernel, in_specs=specs, out_specs=[HERE] * len(outs), out_...  7.12 us
    dynamic_slice x1, other arithmetic, on_device(): lax.dynamic_slice_in_dim(anomaly, (me ^ k) * cells, cells, 1)  2.23 us
  transfers between devices with their start and end apart: 16, of which 9 were waited for; matrix products, arithmetic and copies ran while one was open for 4% of the time, Pallas kernels for 23%

profile of v3, /device:TPU:0, one launch (start us, length us, event | category | flops | bytes accessed | tf_op | source)
XLA Modules:
  0.0 75.2 jit_solution(5209052012081597000)
XLA Ops:
  0.7 3.7 %shard_map.54 = (s32[8,32,128]{2,1,0:T(8,128)S(1)}, s32[8,32,128]{2,1,0:T(8,128)}, f32[8,128]{1,0:T(8,128)S(1)}, f32[32,3072]{1,0:T(8,128)}) custom-call(s32[1]{0:T(128)} %bitcast.10.to_ref, f32[32,32768]{1,0:T(8,128)} %x_ref.3, s32[256,128]{1,0:T(8,128)} %bitcast.21, f32[256,128]{1,0:T(8,128)} %bitcast.30), custom_call_target="tpu_custom_call" | custom-call | flops 2000000000 | bytes 7200000 | tf_op jit(solution)/shard_map/pallas_call | solution.py:263
  4.8 3.5 %collective-permute-start.21 = (f32[32,3072]{1,0:T(8,128)}, f32[32,3072]{1,0:T(8,128)S(1)}, u32[]{:S(2)}, u32[]{:S(2)}) collective-permute-start(f32[32,3072]{1,0:T(8,128)} %get-tuple-element.101), channel_id=1, source_target_pairs={{0,6},{1,7},{2,4},{3,5},{4,2},{5,3},{6,0},{7,1},{8,14},{9,15},{10,... | collective-permute-start | bytes 1179656 | tf_op jit(solution)/shard_map/ppermute | solution.py:418
  9.6 3.5 %shard_map.55 = f32[32,3072]{1,0:T(8,128)} custom-call(s32[1]{0:T(128)} %bitcast.13.to_ref, f32[32,32768]{1,0:T(8,128)} %x_ref.3, s32[256,128]{1,0:T(8,128)S(1)} %bitcast.22, f32[256,128]{1,0:T(8,128)S(1)} %bitcast.31, s32[8,32,128]{2,1,0:T(8,128)S(1)} %get-tuple-element.99.source_ref, f32[8,128]{1,0:T(8,128)} %copy-done.4), custom_call_target="tpu_custom_call" | custom-call | flops 2000000000 | bytes 7200000 | tf_op jit(solution)/shard_map/pallas_call | solution.py:263
  13.3 2.2 %constant_dynamic-slice_fusion.8 = (f32[32,4096]{1,0:T(8,128)S(1)}, f32[32,4096]{1,0:T(8,128)S(1)}, f32[32,4096]{1,0:T(8,128)S(1)}, f32[32,4096]{1,0:T(8,128)S(1...) fusion(f32[32,32768]{1,0:T(8,128)} %x_ref.3, s32[]{:T(128)S(6)} %select_n.50, ...), kind=kLoop, calls=%fused_computation.16 | loop fusion | flops 131072 | bytes 6832152 | tf_op jit(solution)/shard_map/dynamic_slice | solution.py:447
  17.9 1.6 %collective-permute-start.17 = (f32[32,3072]{1,0:T(8,128)S(1)}, f32[32,3072]{1,0:T(8,128)S(1)}, u32[]{:S(2)}, u32[]{:S(2)}) collective-permute-start(f32[32,3072]{1,0:T(8,128)S(1)} %shard_map.58), channel_id=1, source_target_pairs={{0,2},{1,3},{2,0},{3,1},{4,6},{5,7},{6,4},{7,5},{8,10},{9,11},{10,... | collective-permute-start | bytes 1179656 | tf_op jit(solution)/shard_map/ppermute | solution.py:418
  20.4 1.6 %collective-permute-start.19 = (f32[32,3072]{1,0:T(8,128)S(1)}, f32[32,3072]{1,0:T(8,128)S(1)}, u32[]{:S(2)}, u32[]{:S(2)}) collective-permute-start(f32[32,3072]{1,0:T(8,128)S(1)} %shard_map.60), channel_id=1, source_target_pairs={{0,4},{1,5},{2,6},{3,7},{4,0},{5,1},{6,2},{7,3},{8,12},{9,13},{10,... | collective-permute-start | bytes 1179656 | tf_op jit(solution)/shard_map/ppermute | solution.py:418
  25.0 1.6 %collective-permute-done.22.kept_ref.refs_7_ = f32[32,3072]{1,0:T(8,128)S(1)} collective-permute-done((f32[32,3072]{1,0:T(8,128)}, f32[32,3072]{1,0:T(8,128)S(1)}, u32[]{:S(2)}, u32[]{:S(2)}) %collective-permute-start.22) | collective-permute-done | bytes 393248 | tf_op jit(solution)/shard_map/ppermute | solution.py:418
  26.6 1.8 %collective-permute-start.20 = (f32[32,3072]{1,0:T(8,128)S(1)}, f32[32,3072]{1,0:T(8,128)S(1)}, u32[]{:S(2)}, u32[]{:S(2)}) collective-permute-start(f32[32,3072]{1,0:T(8,128)S(1)} %shard_map.61), channel_id=1, source_target_pairs={{0,5},{1,4},{2,7},{3,6},{4,1},{5,0},{6,3},{7,2},{8,13},{9,12},{10,... | collective-permute-start | bytes 1179656 | tf_op jit(solution)/shard_map/ppermute | solution.py:418
  29.3 1.0 %shard_map.66.refs_7_ = f32[32,4096]{1,0:T(8,128)S(1)} custom-call(s32[1]{0:T(128)} %bitcast.9.to_ref.me_ref, s32[8,32,128]{2,1,0:T(8,128)S(1)} %copy-done.5, f32[32,3072]{1,0:T(8,128)S(1)} %collective-permute-done.22.kept_ref.refs_7_), custom_call_target="tpu_custom_call" | custom-call | flops 1000000000 | bytes 3600000 | tf_op jit(solution)/shard_map/pallas_call | solution.py:128
  30.3 4.9 %collective-permute-done.19.kept_ref.refs_4_ = f32[32,3072]{1,0:T(8,128)S(1)} collective-permute-done((f32[32,3072]{1,0:T(8,128)S(1)}, f32[32,3072]{1,0:T(8,128)S(1)}, u32[]{:S(2)}, u32[]{:S(2)}) %collective-permute-start.19) | collective-permute-done | bytes 393248 | tf_op jit(solution)/shard_map/ppermute | solution.py:418
  35.2 1.0 %shard_map.64.refs_4_ = f32[32,4096]{1,0:T(8,128)S(1)} custom-call(s32[1]{0:T(128)} %bitcast.9.to_ref.me_ref, s32[8,32,128]{2,1,0:T(8,128)S(1)} %copy-done.5, f32[32,3072]{1,0:T(8,128)S(1)} %collective-permute-done.19.kept_ref.refs_4_), custom_call_target="tpu_custom_call" | custom-call | flops 1000000000 | bytes 3600000 | tf_op jit(solution)/shard_map/pallas_call | solution.py:128
  36.2 1.0 %shard_map.63.refs_2_ = f32[32,4096]{1,0:T(8,128)S(1)} custom-call(s32[1]{0:T(128)} %bitcast.9.to_ref.me_ref, s32[8,32,128]{2,1,0:T(8,128)S(1)} %copy-done.5, f32[32,3072]{1,0:T(8,128)S(1)} %collective-permute-done.17.kept_ref.refs_2_), custom_call_target="tpu_custom_call" | custom-call | flops 1000000000 | bytes 3600000 | tf_op jit(solution)/shard_map/pallas_call | solution.py:128
  37.2 1.0 %shard_map.62.refs_1_ = f32[32,4096]{1,0:T(8,128)S(1)} custom-call(s32[1]{0:T(128)} %bitcast.9.to_ref.me_ref, s32[8,32,128]{2,1,0:T(8,128)S(1)} %copy-done.5, f32[32,3072]{1,0:T(8,128)S(1)} %collective-permute-done.16.kept_ref.refs_1_), custom_call_target="tpu_custom_call" | custom-call | flops 1000000000 | bytes 3600000 | tf_op jit(solution)/shard_map/pallas_call | solution.py:128
  38.2 5.2 %collective-permute-done.20.refs_5_.kept_ref = f32[32,3072]{1,0:T(8,128)S(1)} collective-permute-done((f32[32,3072]{1,0:T(8,128)S(1)}, f32[32,3072]{1,0:T(8,128)S(1)}, u32[]{:S(2)}, u32[]{:S(2)}) %collective-permute-start.20) | collective-permute-done | bytes 393248 | tf_op jit(solution)/shard_map/ppermute | solution.py:418
  43.5 1.9 %shard_map.67 = (f32[136,128]{1,0:T(8,128)S(1)}, f32[136,128]{1,0:T(8,128)S(1)}) custom-call(s32[1]{0:T(128)} %bitcast.9.to_ref.me_ref, f32[32,3072]{1,0:T(8,128)S(1)} %shard_map.56.refs_0_, f32[32,3072]{1,0:T(8,128)S(1)} %collective-permute-done.16.kept_ref.refs_1_, f32[32,3072]{1,0:T(8,128)S(1)} %collective-permute-done.17.kept_ref.refs_2_, ...), custom_call_target="tpu_custom_call" | custom-call | flops 2000000000 | bytes 7200000 | tf_op jit(solution)/shard_map/pallas_call | solution.py:128
  45.6 1.0 %collective-permute-done.23 = f32[136,128]{1,0:T(8,128)S(1)} collective-permute-done((f32[136,128]{1,0:T(8,128)S(1)}, f32[136,128]{1,0:T(8,128)S(1)}, u32[]{:S(2)}, u32[]{:S(2)}) %collective-permute-start.23) | collective-permute-done | bytes 69664 | tf_op jit(solution)/shard_map/ppermute | solution.py:418
  46.7 2.7 %collective-permute-start.26 = (f32[136,128]{1,0:T(8,128)S(1)}, f32[136,128]{1,0:T(8,128)S(1)}, u32[]{:S(2)}, u32[]{:S(2)}) collective-permute-start(f32[136,128]{1,0:T(8,128)S(1)} %add.99), channel_id=1, source_target_pairs={{0,6},{1,7},{2,4},{3,5},{4,2},{5,3},{6,0},{7,1},{8,14},{9,15},{10,... | collective-permute-start | bytes 208904 | tf_op jit(solution)/shard_map/ppermute | solution.py:418
  52.0 1.7 %collective-permute-done.25 = f32[136,128]{1,0:T(8,128)S(1)} collective-permute-done((f32[136,128]{1,0:T(8,128)S(1)}, f32[136,128]{1,0:T(8,128)S(1)}, u32[]{:S(2)}, u32[]{:S(2)}) %collective-permute-start.25) | collective-permute-done | bytes 69664 | tf_op jit(solution)/shard_map/ppermute | solution.py:418
  54.2 3.7 %collective-permute-start.29 = (f32[136,128]{1,0:T(8,128)S(1)}, f32[136,128]{1,0:T(8,128)S(1)}, u32[]{:S(2)}, u32[]{:S(2)}) collective-permute-start(f32[136,128]{1,0:T(8,128)S(1)} %add_add_fusion.3), channel_id=1, source_target_pairs={{0,24},{8,16},{16,8},{24,0},{1,25},{9,17},{17,9},{25,1},{2,26},{10... | collective-permute-start | bytes 208904 | tf_op jit(solution)/shard_map/ppermute | solution.py:418
  58.7 1.2 %shard_map.69.refs_5_ = f32[32,4096]{1,0:T(8,128)S(1)} custom-call(s32[1]{0:T(128)} %bitcast.9.to_ref.me_ref, s32[8,32,128]{2,1,0:T(8,128)S(1)} %copy-done.5, f32[32,3072]{1,0:T(8,128)S(1)} %collective-permute-done.20.refs_5_.kept_ref), custom_call_target="tpu_custom_call" | custom-call | flops 1000000000 | bytes 3600000 | tf_op jit(solution)/shard_map/pallas_call | solution.py:128
  59.9 1.3 %shard_map.70 = (bf16[256,4096]{1,0:T(8,128)(2,1)S(1)}, bf16[256,4096]{1,0:T(8,128)(2,1)S(1)}) custom-call(s32[1]{0:T(128)} %bitcast.9.to_ref.me_ref, f32[32,4096]{1,0:T(8,128)S(1)} %get-tuple-element.108.refs_0_, f32[32,4096]{1,0:T(8,128)S(1)} %shard_map.62.refs_1_, f32[32,4096]{1,0:T(8,128)S(1)} %shard_map.63.refs_2_, f32[32,4096]{1,0:T(8,128)S(1)} %shard_map.68.refs_3_, ...), custom_call_target="tpu_custom_call" | custom-call | flops 1000000000 | bytes 3600000 | tf_op jit(solution)/shard_map/pallas_call | solution.py:128
  61.2 2.0 %collective-permute-done.28 = f32[136,128]{1,0:T(8,128)S(1)} collective-permute-done((f32[136,128]{1,0:T(8,128)S(1)}, f32[136,128]{1,0:T(8,128)S(1)}, u32[]{:S(2)}, u32[]{:S(2)}) %collective-permute-start.28) | collective-permute-done | bytes 69664 | tf_op jit(solution)/shard_map/ppermute | solution.py:418
  64.5 10.5 %conditional.1 = ((f32[256,256]{1,0:T(8,128)}, f32[256,4096]{1,0:T(8,128)})) conditional(s32[]{:T(128)} %bitcast.20, (s32[]{:T(128)}, f32[136,128]{1,0:T(8,128)S(1)}, f32[136,128]{1,0:T(8,128)S(1)}, bf16[256,4096]{1,0:T(8,128)(2,1)S(1)}, bf16[256,4096]{1,0:T(8,128)(2,1)S(1)}) %tuple.23, (s32[]{:T(128)}, f32[32,32768]{1,0:T(8,128)}, ...), branch_computations={%region_1.0_spmd, %region_2.0_spmd} | conditional | flops 18000152576 | bytes 82438528 | solution.py:491
  64.5 10.3 %branch_0_fun.1 = (f32[256,256]{1,0:T(8,128)}, f32[256,4096]{1,0:T(8,128)}) custom-call(s32[1]{0:T(128)} %bitcast.me_ref, f32[136,128]{1,0:T(8,128)S(1)} %get-tuple-element.45.mine_ref, f32[136,128]{1,0:T(8,128)S(1)} %get-tuple-element.46.other_ref, bf16[256,4096]{1,0:T(8,128)(2,1)S(1)} %get-tuple-element.47.refs_0_, ...), custom_call_target="tpu_custom_call" | custom-call | tf_op jit(solution)/shard_map/cond/branch_0_fun/pallas_call | solution.py:405
  (43 shorter events, 14.2 us)
Async XLA Ops:
  0.6 7.7 %copy-start.1 = (f32[32768]{0:T(1024)S(1)}, f32[32768]{0:T(1024)}, u32[]{:S(2)}) copy-start(f32[32768]{0:T(1024)} %param.7) | copy-start | bytes 393220
  0.6 7.7 %copy-start = (s32[32768]{0:T(1024)S(1)}, s32[32768]{0:T(1024)}, u32[]{:S(2)}) copy-start(s32[32768]{0:T(1024)} %param.6) | copy-start | bytes 393220
  4.3 4.7 %collective-permute-start.15 = (f32[8,128]{1,0:T(8,128)S(1)}, f32[8,128]{1,0:T(8,128)S(1)}, u32[]{:S(2)}, u32[]{:S(2)}) collective-permute-start(f32[8,128]{1,0:T(8,128)S(1)} %get-tuple-element.97.refs_9_), channel_id=1, source_target_pairs={{0,1},{1,0},{2,3},{3,2},{4,5},{5,4},{6,7},{7,6},{8,9},{9,8},{10,11... | collective-permute-start | bytes 12296 | tf_op jit(solution)/shard_map/ppermute | solution.py:418
  4.8 20.1 %collective-permute-start.21 = (f32[32,3072]{1,0:T(8,128)}, f32[32,3072]{1,0:T(8,128)S(1)}, u32[]{:S(2)}, u32[]{:S(2)}) collective-permute-start(f32[32,3072]{1,0:T(8,128)} %get-tuple-element.101), channel_id=1, source_target_pairs={{0,6},{1,7},{2,4},{3,5},{4,2},{5,3},{6,0},{7,1},{8,14},{9,15},{10,... | collective-permute-start | bytes 1179656 | tf_op jit(solution)/shard_map/ppermute | solution.py:418
  9.0 0.6 copy-start.4
  13.0 13.5 %collective-permute-start.22 = (f32[32,3072]{1,0:T(8,128)}, f32[32,3072]{1,0:T(8,128)S(1)}, u32[]{:S(2)}, u32[]{:S(2)}) collective-permute-start(f32[32,3072]{1,0:T(8,128)} %shard_map.55), channel_id=1, source_target_pairs={{0,7},{1,6},{2,5},{3,4},{4,3},{5,2},{6,1},{7,0},{8,15},{9,14},{10,... | collective-permute-start | bytes 1179656 | tf_op jit(solution)/shard_map/ppermute | solution.py:418
  16.5 20.7 %collective-permute-start.16 = (f32[32,3072]{1,0:T(8,128)S(1)}, f32[32,3072]{1,0:T(8,128)S(1)}, u32[]{:S(2)}, u32[]{:S(2)}) collective-permute-start(f32[32,3072]{1,0:T(8,128)S(1)} %shard_map.57), channel_id=1, source_target_pairs={{0,1},{1,0},{2,3},{3,2},{4,5},{5,4},{6,7},{7,6},{8,9},{9,8},{10,11... | collective-permute-start | bytes 1179656 | tf_op jit(solution)/shard_map/ppermute | solution.py:418
  17.9 18.3 %collective-permute-start.17 = (f32[32,3072]{1,0:T(8,128)S(1)}, f32[32,3072]{1,0:T(8,128)S(1)}, u32[]{:S(2)}, u32[]{:S(2)}) collective-permute-start(f32[32,3072]{1,0:T(8,128)S(1)} %shard_map.58), channel_id=1, source_target_pairs={{0,2},{1,3},{2,0},{3,1},{4,6},{5,7},{6,4},{7,5},{8,10},{9,11},{10,... | collective-permute-start | bytes 1179656 | tf_op jit(solution)/shard_map/ppermute | solution.py:418
  20.4 14.8 %collective-permute-start.19 = (f32[32,3072]{1,0:T(8,128)S(1)}, f32[32,3072]{1,0:T(8,128)S(1)}, u32[]{:S(2)}, u32[]{:S(2)}) collective-permute-start(f32[32,3072]{1,0:T(8,128)S(1)} %shard_map.60), channel_id=1, source_target_pairs={{0,4},{1,5},{2,6},{3,7},{4,0},{5,1},{6,2},{7,3},{8,12},{9,13},{10,... | collective-permute-start | bytes 1179656 | tf_op jit(solution)/shard_map/ppermute | solution.py:418
  23.0 5.4 %copy-start.5 = (s32[8,32,128]{2,1,0:T(8,128)S(1)}, s32[8,32,128]{2,1,0:T(8,128)}, u32[]{:S(2)}) copy-start(s32[8,32,128]{2,1,0:T(8,128)} %get-tuple-element.112.rank_ref) | copy-start | bytes 393220
  24.9 18.6 %collective-permute-start.18 = (f32[32,3072]{1,0:T(8,128)S(1)}, f32[32,3072]{1,0:T(8,128)S(1)}, u32[]{:S(2)}, u32[]{:S(2)}) collective-permute-start(f32[32,3072]{1,0:T(8,128)S(1)} %shard_map.59), channel_id=1, source_target_pairs={{0,3},{1,2},{2,1},{3,0},{4,7},{5,6},{6,5},{7,4},{8,11},{9,10},{10,... | collective-permute-start | bytes 1179656 | tf_op jit(solution)/shard_map/ppermute | solution.py:418
  26.6 16.9 %collective-permute-start.20 = (f32[32,3072]{1,0:T(8,128)S(1)}, f32[32,3072]{1,0:T(8,128)S(1)}, u32[]{:S(2)}, u32[]{:S(2)}) collective-permute-start(f32[32,3072]{1,0:T(8,128)S(1)} %shard_map.61), channel_id=1, source_target_pairs={{0,5},{1,4},{2,7},{3,6},{4,1},{5,0},{6,3},{7,2},{8,13},{9,12},{10,... | collective-permute-start | bytes 1179656 | tf_op jit(solution)/shard_map/ppermute | solution.py:418
  43.5 15.2 %copy-start.2 = (f32[32,3072]{1,0:T(8,128)}, f32[32,3072]{1,0:T(8,128)S(1)}, u32[]{:S(2)}) copy-start(f32[32,3072]{1,0:T(8,128)S(1)} %collective-permute-done.20.refs_5_.kept_ref) | copy-start | bytes 1179652
  45.3 1.3 %collective-permute-start.23 = (f32[136,128]{1,0:T(8,128)S(1)}, f32[136,128]{1,0:T(8,128)S(1)}, u32[]{:S(2)}, u32[]{:S(2)}) collective-permute-start(f32[136,128]{1,0:T(8,128)S(1)} %get-tuple-element.104), channel_id=1, source_target_pairs={{0,1},{1,0},{2,3},{3,2},{4,5},{5,4},{6,7},{7,6},{8,9},{9,8},{10,11... | collective-permute-start | bytes 208904 | tf_op jit(solution)/shard_map/ppermute | solution.py:418
  46.7 5.3 %collective-permute-start.26 = (f32[136,128]{1,0:T(8,128)S(1)}, f32[136,128]{1,0:T(8,128)S(1)}, u32[]{:S(2)}, u32[]{:S(2)}) collective-permute-start(f32[136,128]{1,0:T(8,128)S(1)} %add.99), channel_id=1, source_target_pairs={{0,6},{1,7},{2,4},{3,5},{4,2},{5,3},{6,0},{7,1},{8,14},{9,15},{10,... | collective-permute-start | bytes 208904 | tf_op jit(solution)/shard_map/ppermute | solution.py:418
  49.4 4.3 %collective-permute-start.25 = (f32[136,128]{1,0:T(8,128)S(1)}, f32[136,128]{1,0:T(8,128)S(1)}, u32[]{:S(2)}, u32[]{:S(2)}) collective-permute-start(f32[136,128]{1,0:T(8,128)S(1)} %add.99), channel_id=1, source_target_pairs={{0,4},{1,5},{2,6},{3,7},{4,0},{5,1},{6,2},{7,3},{8,12},{9,13},{10,... | collective-permute-start | bytes 208904 | tf_op jit(solution)/shard_map/ppermute | solution.py:418
  49.9 4.3 %collective-permute-start.24 = (f32[136,128]{1,0:T(8,128)S(1)}, f32[136,128]{1,0:T(8,128)S(1)}, u32[]{:S(2)}, u32[]{:S(2)}) collective-permute-start(f32[136,128]{1,0:T(8,128)S(1)} %add.99), channel_id=1, source_target_pairs={{0,2},{1,3},{2,0},{3,1},{4,6},{5,7},{6,4},{7,5},{8,10},{9,11},{10,... | collective-permute-start | bytes 208904 | tf_op jit(solution)/shard_map/ppermute | solution.py:418
  54.2 6.9 %collective-permute-start.29 = (f32[136,128]{1,0:T(8,128)S(1)}, f32[136,128]{1,0:T(8,128)S(1)}, u32[]{:S(2)}, u32[]{:S(2)}) collective-permute-start(f32[136,128]{1,0:T(8,128)S(1)} %add_add_fusion.3), channel_id=1, source_target_pairs={{0,24},{8,16},{16,8},{24,0},{1,25},{9,17},{17,9},{25,1},{2,26},{10... | collective-permute-start | bytes 208904 | tf_op jit(solution)/shard_map/ppermute | solution.py:418
  57.9 5.3 %collective-permute-start.28 = (f32[136,128]{1,0:T(8,128)S(1)}, f32[136,128]{1,0:T(8,128)S(1)}, u32[]{:S(2)}, u32[]{:S(2)}) collective-permute-start(f32[136,128]{1,0:T(8,128)S(1)} %add_add_fusion.3), channel_id=1, source_target_pairs={{0,16},{8,24},{16,0},{24,8},{1,17},{9,25},{17,1},{25,9},{2,18},{10... | collective-permute-start | bytes 208904 | tf_op jit(solution)/shard_map/ppermute | solution.py:418
  57.9 5.3 %collective-permute-start.27 = (f32[136,128]{1,0:T(8,128)S(1)}, f32[136,128]{1,0:T(8,128)S(1)}, u32[]{:S(2)}, u32[]{:S(2)}) collective-permute-start(f32[136,128]{1,0:T(8,128)S(1)} %add_add_fusion.3), channel_id=1, source_target_pairs={{0,8},{8,0},{16,24},{24,16},{1,9},{9,1},{17,25},{25,17},{2,10},{10... | collective-permute-start | bytes 208904 | tf_op jit(solution)/shard_map/ppermute | solution.py:418
  63.2 1.3 %collective-permute-start.30 = (f32[136,128]{1,0:T(8,128)S(1)}, f32[136,128]{1,0:T(8,128)S(1)}, u32[]{:S(2)}, u32[]{:S(2)}) collective-permute-start(f32[136,128]{1,0:T(8,128)S(1)} %add_add_fusion.2), channel_id=1, source_target_pairs={{0,1},{1,0},{2,3},{3,2},{4,5},{5,4},{6,7},{7,6},{8,9},{9,8},{10,11... | collective-permute-start | bytes 208904 | tf_op jit(solution)/shard_map/ppermute | solution.py:418

commit v4 on v3

--- a/solution.py
+++ b/solution.py
@@ -17,7 +17,6 @@
 PARTS = RUN // LANE
 KEPT = 3 * RUN // 4
 STEPS = (RUN - 1).bit_length()
-ALL_VMEM = 62 * 1024 * 1024
 
 
 def split2(x):
@@ -187,125 +186,70 @@
     return out
 
 
-def pack(to, x_ref, root_ref, source_ref, out_ref, first):
+def pack(base, x_ref, root_ref, source_ref, out_ref):
     rows, cells = x_ref.shape
-    runs = cells // RUN
-    width = out_ref.shape[1] // runs
-    for run in range(runs):
-        places = range(first // LANE, (first + width) // LANE)
-        index = {p: across(source_ref, p, to * runs + run) for p in places}
+    for run in range(cells // RUN):
+        index = [across(source_ref, p, base + run) for p in range(KEPT // LANE)]
         for t in range(0, rows, SUB):
             parts = []
             for group in range(run * PARTS, (run + 1) * PARTS):
                 root = jnp.broadcast_to(root_ref[group : group + 1, :], (SUB, LANE))
                 parts.append(x_ref[t : t + SUB, group * LANE : (group + 1) * LANE] * root)
-            for p in places:
-                at = run * width + p * LANE - first
-                out_ref[t : t + SUB, at : at + LANE] = gathered({i: parts[i] for i in range(p, PARTS)}, index[p])
-
-
-def slice_copies(to, x_ref, area_ref, own_ref, own_area_ref, sems):
-    cells = own_ref.shape[1]
-    groups = cells // LANE
-    return [
-        pltpu.make_async_copy(area_ref.at[pl.ds(pl.multiple_of(to * groups, groups), groups), :], own_area_ref, sems.at[0]),
-        pltpu.make_async_copy(x_ref.at[:, pl.ds(pl.multiple_of(to * cells, cells), cells)], own_ref, sems.at[1]),
-    ]
-
-
-def first_kernel(to_ref, x_ref, mask_ref, area_ref, source_ref, rank_ref, over_ref, kept_ref, *scratch):
-    own_ref, own_area_ref, root_ref, whole_mask_ref, gap_ref, sems = scratch
-    groups = own_area_ref.shape[0]
-    to = to_ref[0]
-    mask_copy = pltpu.make_async_copy(mask_ref, whole_mask_ref, sems.at[2])
-    mask_copy.start()
-    copies = slice_copies(to, x_ref, area_ref, own_ref, own_area_ref, sems)
-    for copy in copies:
-        copy.start()
-    mask_copy.wait()
-    plan(whole_mask_ref, source_ref, rank_ref, over_ref, gap_ref)
-    for copy in copies:
-        copy.wait()
-    mask = whole_mask_ref[pl.ds(pl.multiple_of(to * groups, groups), groups), :]
-    root_ref[...] = jnp.sqrt(own_area_ref[...] * mask.astype(F32))
-    pack(to, own_ref, root_ref, source_ref, kept_ref, 0)
-
-
-def second_kernel(to_ref, x_ref, mask_ref, area_ref, source_ref, gate_ref, kept_ref, *scratch):
-    own_ref, own_area_ref, root_ref, own_mask_ref, sems = scratch
-    groups = own_area_ref.shape[0]
-    to = to_ref[0]
-    at = pl.ds(pl.multiple_of(to * groups, groups), groups)
-    copies = slice_copies(to, x_ref, area_ref, own_ref, own_area_ref, sems)
-    copies.append(pltpu.make_async_copy(mask_ref.at[at, :], own_mask_ref, sems.at[2]))
-    for copy in copies:
-        copy.start()
-    for copy in copies:
-        copy.wait()
-    root_ref[...] = jnp.sqrt(own_area_ref[...] * own_mask_ref[...].astype(F32))
-    pack(to, own_ref, root_ref, source_ref, kept_ref, 0)
-
-
-def pack_early(to, anomaly, mask, area, cells, source=None, gate=None):
-    rows, groups, own_groups = anomaly.shape[0], mask.shape[0], cells // LANE
+            for p, lanes in enumerate(index):
+                at = run * KEPT + p * LANE
+                out_ref[t : t + SUB, at : at + LANE] = gathered({i: parts[i] for i in range(p, PARTS)}, lanes)
+
+
+def groups_from(base, groups):
+    return pl.ds(pl.multiple_of(base * PARTS, PARTS), groups)
+
+
+def first_kernel(base_ref, x_ref, mask_ref, area_ref, gate_ref, source_ref, rank_ref, over_ref, out_ref, root_ref, gap_ref):
+    base = base_ref[0]
+    plan(mask_ref, source_ref, rank_ref, over_ref, gap_ref)
+    at = groups_from(base, root_ref.shape[0])
+    root_ref[...] = jnp.sqrt(area_ref[at, :] * mask_ref[at, :].astype(F32))
+    pack(base, x_ref, root_ref, source_ref, out_ref)
+
+
+def plan_and_pack(base, x, mask, area, gate):
+    rows, cells = x.shape
+    groups = mask.shape[0]
     moves = jax.ShapeDtypeStruct((PARTS, groups // PARTS, LANE), jnp.int32)
-    outs = [jax.ShapeDtypeStruct((rows, cells // RUN * KEPT), F32)]
-    scratch = [pltpu.VMEM((rows, cells), F32)] + [pltpu.VMEM((own_groups, LANE), F32)] * 2
-    operands, specs = [to[None], anomaly, mask, area], [SCALARS] + [pl.BlockSpec(memory_space=pl.ANY)] * 3
-    if source is None:
-        kernel = first_kernel
-        outs = [moves, moves, jax.ShapeDtypeStruct((SUB, LANE), F32)] + outs
-        scratch += [pltpu.VMEM((groups, LANE), jnp.int32)] * 2
-    else:
-        kernel = second_kernel
-        operands, specs = operands + [source, gate], specs + [HERE] * 2
-        scratch += [pltpu.VMEM((own_groups, LANE), jnp.int32)]
-    return pl.pallas_call(
-        kernel,
-        in_specs=specs,
-        out_specs=[HERE] * len(outs),
-        out_shape=outs,
-        scratch_shapes=scratch + [pltpu.SemaphoreType.DMA((3,))],
-        compiler_params=pltpu.CompilerParams(vmem_limit_bytes=ALL_VMEM),
-        cost_estimate=pl.CostEstimate(flops=2_000_000_000, bytes_accessed=7_200_000, transcendentals=0),
-    )(*operands)
-
-
-def pack_kernel(first, to_ref, x_ref, mask_ref, area_ref, source_ref, out_ref, root_ref):
-    groups = x_ref.shape[1] // LANE
-    to = to_ref[0]
-    at = pl.ds(pl.multiple_of(to * groups, groups), groups)
+    outs = [moves, moves, jax.ShapeDtypeStruct((SUB, LANE), F32), jax.ShapeDtypeStruct((rows, cells // RUN * KEPT), F32)]
+    scratch = [pltpu.VMEM((cells // LANE, LANE), F32), pltpu.VMEM((groups, LANE), jnp.int32)]
+    return call(first_kernel, [base[None], x, mask, area, gate], outs, scratch, us=2)
+
+
+def pack_kernel(base_ref, x_ref, mask_ref, area_ref, source_ref, *refs):
+    out_ref, root_ref = refs[-2:]
+    base = base_ref[0]
+    at = groups_from(base, root_ref.shape[0])
     root_ref[...] = jnp.sqrt(area_ref[at, :] * mask_ref[at, :].astype(F32))
-    pack(to, x_ref, root_ref, source_ref, out_ref, first)
-
-
-def pack_cells(to, x, mask, area, source, rest=False):
+    pack(base, x_ref, root_ref, source_ref, out_ref)
+
+
+def pack_cells(base, x, mask, area, source, *gate):
     rows, cells = x.shape
-    out = jax.ShapeDtypeStruct((rows, cells // RUN * (RUN - KEPT if rest else KEPT)), F32)
-    kernel = functools.partial(pack_kernel, KEPT if rest else 0)
-    return call(kernel, [to[None], x, mask, area, source], [out], [pltpu.VMEM((cells // LANE, LANE), F32)])[0]
-
-
-def spread_kernel(me_ref, rank_ref, kept_ref, *refs):
-    out_ref = refs[-1]
+    out = jax.ShapeDtypeStruct((rows, cells // RUN * KEPT), F32)
+    return call(pack_kernel, [base[None], x, mask, area, source, *gate], [out], [pltpu.VMEM((cells // LANE, LANE), F32)])[0]
+
+
+def spread_kernel(me_ref, rank_ref, kept_ref, out_ref):
     rows, cells = out_ref.shape
     runs = cells // RUN
-    me = me_ref[0]
     for run in range(runs):
-        index = [across(rank_ref, p, me * runs + run) for p in range(PARTS)]
+        index = [across(rank_ref, p, me_ref[0] * runs + run) for p in range(PARTS)]
         for t in range(0, rows, SUB):
             parts = [kept_ref[t : t + SUB, first : first + LANE] for first in range(run * KEPT, (run + 1) * KEPT, LANE)]
-            for ref in refs[:-1]:
-                width = RUN - KEPT
-                parts += [ref[t : t + SUB, first : first + LANE] for first in range(run * width, (run + 1) * width, LANE)]
             for p in range(PARTS):
                 first = run * RUN + p * LANE
                 out_ref[t : t + SUB, first : first + LANE] = gathered({i: parts[i] for i in range(min(p + 1, len(parts)))}, index[p])
 
 
-def spread(me, rank, kept, *rest):
+def spread(me, rank, kept):
     out = jax.ShapeDtypeStruct((kept.shape[0], kept.shape[1] // KEPT * RUN), F32)
-    return call(spread_kernel, [me[None], rank, kept, *rest], [out])[0]
+    return call(spread_kernel, [me[None], rank, kept], [out])[0]
 
 
 def place(me, refs, at, whole_ref):
@@ -441,33 +385,40 @@
     size = lax.axis_size("dev")
     me = lax.axis_index("dev")
     cells = anomaly.shape[1] // size
-    order = sorted(range(1, size), key=lambda k: (-(k >> 1).bit_count(), k & 1))
+    runs = cells // RUN
+    early = runs // 2 * RUN
+    others, every = range(1, size), range(size)
+    order = sorted(others, key=lambda k: (-(k >> 1).bit_count(), k & 1))
+    far, late = order[0], order[-3:-1]
     mask, area = ocean_mask.reshape(-1, LANE), area_weight.reshape(-1, LANE)
-    others, every = range(1, size), range(size)
-    part = lambda k: lax.dynamic_slice_in_dim(anomaly, (me ^ k) * cells, cells, 1)
-    kept = {}
-    source, rank, over, packed = pack_early(me ^ order[0], anomaly, mask, area, cells)
-    kept[order[0]] = swap(packed, "dev", order[0])
-    if size > 2:
-        packed = pack_early(me ^ order[1], anomaly, mask, area, cells, source, swap(over, "dev", 1))[0]
-        kept[order[1]] = swap(packed, "dev", order[1])
-        anomaly, source, packed = lax.optimization_barrier((anomaly, source, packed))
-    for k in (*order[2:], 0):
-        packed = pack_cells(me ^ k, part(k), mask, area, source)
-        kept[k] = swap(packed, "dev", k) if k else packed
-    cut = lambda x: lax.dynamic_slice_in_dim(x, me * cells, cells, 0)
-    weights = cut(area_weight) * cut(ocean_mask).astype(F32)
+    inputs = anomaly, ocean_mask, area_weight
+    start_of = lambda k: (me ^ k) * runs
+    part = lambda x, k, count=cells: lax.dynamic_slice_in_dim(x, (me ^ k) * cells, count, x.ndim - 1)
+
+    half = lambda k, at: lax.dynamic_slice_in_dim(anomaly, (me ^ k) * cells + at, early, 1)
+    raw = swap(half(far, 0), "dev", far)
+    source, rank, over, packed = plan_and_pack(start_of(far) + early // RUN, half(far, early), mask, area, swap(area, "dev", 1))
+    kept = {far: swap(packed, "dev", far)}
+    anomaly, source = lax.optimization_barrier((anomaly, source))
+    near = swap(part(anomaly, 1), "dev", 1)
+    gate = [swap(over, "dev", 1)]
+    for k in order[1:-1]:
+        packed = pack_cells(start_of(k), part(anomaly, k), mask, area, source, *gate)
+        kept[k] = swap(packed, "dev", k)
+        if gate:
+            anomaly, ocean_mask, area_weight, source, packed = lax.optimization_barrier((anomaly, ocean_mask, area_weight, source, packed))
+            gate = []
+    weights = part(area_weight, 0) * part(ocean_mask, 0).astype(F32)
     total = jnp.sum(weights)[None, None]
-    scaled = part(0) * jnp.sqrt(weights)[None, :]
-    late = order[-3:-1]
-    pieces = {k: spread(me, rank, kept[k]) for k in others if k not in late}
-    pieces[0] = scaled
-    last = kept[late[-1]] if late else kept[1]
-    last, pieces = lax.optimization_barrier((last, pieces))
-    if late:
-        kept[late[-1]] = last
-    kept = [kept[k] for k in every]
-    keep, send = form_gram(me, kept, total, over)
+    root = jnp.sqrt(weights)[None, :]
+    own = part(anomaly, 0)
+    kept[0] = pack_cells(start_of(0), own, mask, area, source)
+    kept[1] = pack_cells(start_of(0), near, mask, area, source)
+    kept[far] = jnp.concatenate([pack_cells(start_of(0), raw, mask, area, source), kept[far]], 1)
+    pieces = {0: own * root, 1: near * root}
+    pieces |= {k: spread(me, rank, kept[k]) for k in others if k not in late and k not in pieces}
+    kept[late[-1]], pieces = lax.optimization_barrier((kept[late[-1]], pieces))
+    keep, send = form_gram(me, [kept[k] for k in every], total, over)
     mine = keep + swap(send, "dev", 1)
     for k, axis, first in zip(late, ("dev", "band"), (2, 1)):
         mine, rank = lax.optimization_barrier((mine, rank))
@@ -476,19 +427,18 @@
     terms = form_terms(me, [pieces[k] for k in every])
     mine, terms = lax.optimization_barrier((mine, terms))
     other = swap(mine, "dev", 1)
-    flag = mine[-1, 0] > 0
-
-    def all_sent(mine, other):
+
+    def packed_ones(mine, other, terms, inputs):
         return solve(me, mine, other, terms)
 
-    def send_rest(mine, other):
-        rest = [pack_cells(me ^ k, part(k), mask, area, source, True) for k in every]
-        rest = rest[:1] + [swap(x, "dev", k) for k, x in zip(others, rest[1:])]
-        more_mine, more_other = sum_all(*form_gram(me, rest, jnp.zeros_like(total), over))
-        pieces = [scaled] + [spread(me, rank, kept[k], rest[k]) for k in others]
-        return solve(me, mine + more_mine, other + more_other, form_terms(me, pieces))
-
-    return tuple(lax.cond(flag, send_rest, all_sent, mine, other))
+    def whole_ones(mine, other, terms, inputs):
+        anomaly, ocean_mask, area_weight = inputs
+        root = jnp.sqrt(part(area_weight, 0) * part(ocean_mask, 0).astype(F32))[None, :]
+        pieces = [part(anomaly, 0)] + [swap(part(anomaly, k), "dev", k) for k in others]
+        pieces = [piece * root for piece in pieces]
+        return solve(me, *sum_all(*form_gram(me, pieces, total, over)), form_terms(me, pieces))
+
+    return tuple(lax.cond(mine[-1, 0] > 0, whole_ones, packed_ones, mine, other, terms, inputs))
 
 
 def solution(mesh):

time: 75.5 us -> 73.9 us (0.979)
  Pallas kernels: 33.4 us -> 29.3 us
  waiting for transfers between devices: 17.8 us -> 20.4 us
  other arithmetic: 2.9 us -> 1.08 us
  starting transfers between devices: 18.1 us -> 19.5 us
    pallas_call x2 -> x0, Pallas kernels: 7.12 us -> none  [pack_early(): pl.pallas_call(kernel, in_specs=specs, out_specs=[HERE] * len(outs), out_...]
    pallas_call x15 -> x17, Pallas kernels: 16 us -> 19.1 us  [call(): pl.pallas_call(kernel, in_specs=[SCALARS] * scalars + [HERE] * (len(opera...]
    ppermute x16 -> x18, waiting for transfers between devices: 17.8 us -> 20.4 us  [swap(): lax.ppermute(x, axis, [(i, i ^ mask) for i in range(lax.axis_size(axis))])]
    dynamic_slice x1, other arithmetic: 2.23 us -> 0.38 us  [on_device(): lax.dynamic_slice_in_dim(x, (me ^ k) * cells, count, x.ndim - 1)]
    ppermute x16 -> x18, starting transfers between devices: 18.1 us -> 19.5 us  [swap(): lax.ppermute(x, axis, [(i, i ^ mask) for i in range(lax.axis_size(axis))])]
    dynamic_slice x0 -> x2, local copies, waits for them, and re-layouts: none -> 1.13 us  [the longest x1 1.06 us: on_device(): lax.dynamic_slice_in_dim(anomaly, (me ^ k) * cells + at, early, 1)]
  transfers between devices with their start and end apart: 16 -> 18, of which waited for: 9 -> 11; matrix products, arithmetic and copies ran while one was open for 4% -> 4% of each run, Pallas kernels for 23% -> 23%
where the time goes in v4:
time: 73.9 us; the launch traced here: 73.8 us
  Pallas kernels  29.3 us (40%)
  waiting for transfers between devices  20.4 us (28%)
  starting transfers between devices  19.5 us (26%)
  local copies, waits for them, and re-layouts  1.66 us (2%)
  between operations  1.57 us (2%)
  other arithmetic  1.08 us (1%)
    ppermute x18, waiting for transfers between devices, swap(): lax.ppermute(x, axis, [(i, i ^ mask) for i in range(lax.axis_size(axis))])  20.4 us
    ppermute x18, starting transfers between devices, swap(): lax.ppermute(x, axis, [(i, i ^ mask) for i in range(lax.axis_size(axis))])  19.5 us
    pallas_call x17, Pallas kernels, call(): pl.pallas_call(kernel, in_specs=[SCALARS] * scalars + [HERE] * (len(opera...  19.1 us
    pallas_call x1, Pallas kernels, solve(): pl.pallas_call(solve_kernel, in_specs=[pl.BlockSpec(memory_space=pltpu.SM...  10.3 us
  transfers between devices with their start and end apart: 18, of which 11 were waited for; matrix products, arithmetic and copies ran while one was open for 4% of the time, Pallas kernels for 23%

profile of v4, /device:TPU:0, one launch (start us, length us, event | category | flops | bytes accessed | tf_op | source)
XLA Modules:
  0.0 73.8 jit_solution(10631813630371434505)
XLA Ops:
  1.1 1.1 %constant_dynamic-slice_fusion.7 = (f32[32,2048]{1,0:T(8,128)S(1)}, f32[32,2048]{1,0:T(8,128)S(1)}) fusion(f32[32,32768]{1,0:T(8,128)} %param.5, s32[]{:T(128)S(6)} %select_n.63, s32[]{:T(128)S(6)} %select_n.55), kind=kLoop, calls=%fused_computation.26 | loop fusion | bytes 1048584 | tf_op jit(solution)/shard_map/dynamic_slice | solution.py:398
  2.2 3.5 %collective-permute-start.22 = (f32[32,2048]{1,0:T(8,128)S(1)}, f32[32,2048]{1,0:T(8,128)S(1)}, u32[]{:S(2)}, u32[]{:S(2)}) collective-permute-start(f32[32,2048]{1,0:T(8,128)S(1)} %get-tuple-element.118), channel_id=1, source_target_pairs={{0,6},{1,7},{2,4},{3,5},{4,2},{5,3},{6,0},{7,1},{8,14},{9,15},{10,... | collective-permute-start | bytes 786440 | tf_op jit(solution)/shard_map/ppermute | solution.py:362
  5.8 2.6 %shard_map.54 = (s32[8,32,128]{2,1,0:T(8,128)S(1)}, s32[8,32,128]{2,1,0:T(8,128)S(1)}, f32[8,128]{1,0:T(8,128)S(1)}, f32[32,1536]{1,0:T(8,128)S(1)}) custom-call(s32[1]{0:T(128)} %bitcast.4.base_ref, f32[32,2048]{1,0:T(8,128)S(1)} %get-tuple-element.119.x_ref, s32[256,128]{1,0:T(8,128)} %bitcast.14, f32[256,128]{1,0:T(8,128)} %bitcast.24, ...), custom_call_target="tpu_custom_call" | custom-call | flops 2000000000 | bytes 7200000 | tf_op jit(solution)/shard_map/pallas_call | solution.py:127
  10.5 2.3 %collective-permute-start.24 = (f32[32,3072]{1,0:T(8,128)S(1)}, f32[32,3072]{1,0:T(8,128)S(1)}, u32[]{:S(2)}, u32[]{:S(2)}) collective-permute-start(f32[32,3072]{1,0:T(8,128)S(1)} %shard_map.55), channel_id=1, source_target_pairs={{0,7},{1,6},{2,5},{3,4},{4,3},{5,2},{6,1},{7,0},{8,15},{9,14},{10,... | collective-permute-start | bytes 1179656 | tf_op jit(solution)/shard_map/ppermute | solution.py:362
  14.0 3.4 %collective-permute-done.23 = f32[32,1536]{1,0:T(8,128)S(1)} collective-permute-done((f32[32,1536]{1,0:T(8,128)S(1)}, f32[32,1536]{1,0:T(8,128)S(1)}, u32[]{:S(2)}, u32[]{:S(2)}) %collective-permute-start.23) | collective-permute-done | bytes 196640 | tf_op jit(solution)/shard_map/ppermute | solution.py:362
  17.4 1.0 %shard_map.65.refs_6_ = f32[32,4096]{1,0:T(8,128)S(1)} custom-call(s32[1]{0:T(128)} %bitcast.2.me_ref, s32[8,32,128]{2,1,0:T(8,128)S(1)} %get-tuple-element.87.rank_ref, f32[32,3072]{1,0:T(8,128)S(1)} %pad_maximum_fusion.kept_ref.refs_6_), custom_call_target="tpu_custom_call" | custom-call | flops 1000000000 | bytes 3600000 | tf_op jit(solution)/shard_map/pallas_call | solution.py:127
  19.7 1.7 %collective-permute-start.18 = (f32[32,3072]{1,0:T(8,128)S(1)}, f32[32,3072]{1,0:T(8,128)S(1)}, u32[]{:S(2)}, u32[]{:S(2)}) collective-permute-start(f32[32,3072]{1,0:T(8,128)S(1)} %shard_map.58), channel_id=1, source_target_pairs={{0,2},{1,3},{2,0},{3,1},{4,6},{5,7},{6,4},{7,5},{8,10},{9,11},{10,... | collective-permute-start | bytes 1179656 | tf_op jit(solution)/shard_map/ppermute | solution.py:362
  22.4 1.6 %collective-permute-start.20 = (f32[32,3072]{1,0:T(8,128)S(1)}, f32[32,3072]{1,0:T(8,128)S(1)}, u32[]{:S(2)}, u32[]{:S(2)}) collective-permute-start(f32[32,3072]{1,0:T(8,128)S(1)} %shard_map.60), channel_id=1, source_target_pairs={{0,4},{1,5},{2,6},{3,7},{4,0},{5,1},{6,2},{7,3},{8,12},{9,13},{10,... | collective-permute-start | bytes 1179656 | tf_op jit(solution)/shard_map/ppermute | solution.py:362
  26.6 1.0 %shard_map.66.refs_7_ = f32[32,4096]{1,0:T(8,128)S(1)} custom-call(s32[1]{0:T(128)} %bitcast.2.me_ref, s32[8,32,128]{2,1,0:T(8,128)S(1)} %get-tuple-element.87.rank_ref, f32[32,3072]{1,0:T(8,128)S(1)} %collective-permute-done.24.kept_ref.refs_7_), custom_call_target="tpu_custom_call" | custom-call | flops 1000000000 | bytes 3600000 | tf_op jit(solution)/shard_map/pallas_call | solution.py:127
  29.5 5.0 %collective-permute-done.20.kept_ref.refs_4_ = f32[32,3072]{1,0:T(8,128)S(1)} collective-permute-done((f32[32,3072]{1,0:T(8,128)S(1)}, f32[32,3072]{1,0:T(8,128)S(1)}, u32[]{:S(2)}, u32[]{:S(2)}) %collective-permute-start.20) | collective-permute-done | bytes 393248 | tf_op jit(solution)/shard_map/ppermute | solution.py:362
  34.5 1.0 %shard_map.63.refs_4_ = f32[32,4096]{1,0:T(8,128)S(1)} custom-call(s32[1]{0:T(128)} %bitcast.2.me_ref, s32[8,32,128]{2,1,0:T(8,128)S(1)} %get-tuple-element.87.rank_ref, f32[32,3072]{1,0:T(8,128)S(1)} %collective-permute-done.20.kept_ref.refs_4_), custom_call_target="tpu_custom_call" | custom-call | flops 1000000000 | bytes 3600000 | tf_op jit(solution)/shard_map/pallas_call | solution.py:127
  35.5 1.0 %shard_map.62.refs_2_ = f32[32,4096]{1,0:T(8,128)S(1)} custom-call(s32[1]{0:T(128)} %bitcast.2.me_ref, s32[8,32,128]{2,1,0:T(8,128)S(1)} %get-tuple-element.87.rank_ref, f32[32,3072]{1,0:T(8,128)S(1)} %collective-permute-done.18.kept_ref.refs_2_), custom_call_target="tpu_custom_call" | custom-call | flops 1000000000 | bytes 3600000 | tf_op jit(solution)/shard_map/pallas_call | solution.py:127
  36.5 4.9 %collective-permute-done.21.refs_5_.kept_ref = f32[32,3072]{1,0:T(8,128)S(1)} collective-permute-done((f32[32,3072]{1,0:T(8,128)S(1)}, f32[32,3072]{1,0:T(8,128)S(1)}, u32[]{:S(2)}, u32[]{:S(2)}) %collective-permute-start.21) | collective-permute-done | bytes 393248 | tf_op jit(solution)/shard_map/ppermute | solution.py:362
  42.0 1.9 %shard_map.67 = (f32[136,128]{1,0:T(8,128)S(1)}, f32[136,128]{1,0:T(8,128)S(1)}) custom-call(s32[1]{0:T(128)} %bitcast.2.me_ref, f32[32,3072]{1,0:T(8,128)S(1)} %shard_map.56.refs_0_, f32[32,3072]{1,0:T(8,128)S(1)} %shard_map.57.refs_1_, f32[32,3072]{1,0:T(8,128)S(1)} %collective-permute-done.18.kept_ref.refs_2_, ...), custom_call_target="tpu_custom_call" | custom-call | flops 2000000000 | bytes 7200000 | tf_op jit(solution)/shard_map/pallas_call | solution.py:127
  44.2 1.0 %collective-permute-done.25 = f32[136,128]{1,0:T(8,128)S(1)} collective-permute-done((f32[136,128]{1,0:T(8,128)S(1)}, f32[136,128]{1,0:T(8,128)S(1)}, u32[]{:S(2)}, u32[]{:S(2)}) %collective-permute-start.25) | collective-permute-done | bytes 69664 | tf_op jit(solution)/shard_map/ppermute | solution.py:362
  45.2 2.8 %collective-permute-start.28 = (f32[136,128]{1,0:T(8,128)S(1)}, f32[136,128]{1,0:T(8,128)S(1)}, u32[]{:S(2)}, u32[]{:S(2)}) collective-permute-start(f32[136,128]{1,0:T(8,128)S(1)} %add.116), channel_id=1, source_target_pairs={{0,6},{1,7},{2,4},{3,5},{4,2},{5,3},{6,0},{7,1},{8,14},{9,15},{10,... | collective-permute-start | bytes 208904 | tf_op jit(solution)/shard_map/ppermute | solution.py:362
  48.8 1.2 %shard_map.68.refs_3_ = f32[32,4096]{1,0:T(8,128)S(1)} custom-call(s32[1]{0:T(128)} %bitcast.2.me_ref, s32[8,32,128]{2,1,0:T(8,128)S(1)} %get-tuple-element.87.rank_ref, f32[32,3072]{1,0:T(8,128)S(1)} %collective-permute-done.19.refs_3_.kept_ref), custom_call_target="tpu_custom_call" | custom-call | flops 1000000000 | bytes 3600000 | tf_op jit(solution)/shard_map/pallas_call | solution.py:127
  50.6 1.8 %collective-permute-done.27 = f32[136,128]{1,0:T(8,128)S(1)} collective-permute-done((f32[136,128]{1,0:T(8,128)S(1)}, f32[136,128]{1,0:T(8,128)S(1)}, u32[]{:S(2)}, u32[]{:S(2)}) %collective-permute-start.27) | collective-permute-done | bytes 69664 | tf_op jit(solution)/shard_map/ppermute | solution.py:362
  52.9 3.7 %collective-permute-start.31 = (f32[136,128]{1,0:T(8,128)S(1)}, f32[136,128]{1,0:T(8,128)S(1)}, u32[]{:S(2)}, u32[]{:S(2)}) collective-permute-start(f32[136,128]{1,0:T(8,128)S(1)} %add_add_fusion.3), channel_id=1, source_target_pairs={{0,24},{8,16},{16,8},{24,0},{1,25},{9,17},{17,9},{25,1},{2,26},{10... | collective-permute-start | bytes 208904 | tf_op jit(solution)/shard_map/ppermute | solution.py:362
  57.3 1.0 %shard_map.69.refs_5_ = f32[32,4096]{1,0:T(8,128)S(1)} custom-call(s32[1]{0:T(128)} %bitcast.2.me_ref, s32[8,32,128]{2,1,0:T(8,128)S(1)} %get-tuple-element.87.rank_ref, f32[32,3072]{1,0:T(8,128)S(1)} %collective-permute-done.21.refs_5_.kept_ref), custom_call_target="tpu_custom_call" | custom-call | flops 1000000000 | bytes 3600000 | tf_op jit(solution)/shard_map/pallas_call | solution.py:127
  58.3 1.3 %shard_map.70 = (bf16[256,4096]{1,0:T(8,128)(2,1)S(1)}, bf16[256,4096]{1,0:T(8,128)(2,1)S(1)}) custom-call(s32[1]{0:T(128)} %bitcast.2.me_ref, f32[32,4096]{1,0:T(8,128)S(1)} %get-tuple-element.83.refs_0_, f32[32,4096]{1,0:T(8,128)S(1)} %get-tuple-element.84.refs_1_, f32[32,4096]{1,0:T(8,128)S(1)} %shard_map.62.refs_2_, f32[32,4096]{1,0:T(8,128)S(1)} %shard_map.68.refs_3_, ...), custom_call_target="tpu_custom_call" | custom-call | flops 1000000000 | bytes 3600000 | tf_op jit(solution)/shard_map/pallas_call | solution.py:127
  59.6 2.1 %collective-permute-done.30 = f32[136,128]{1,0:T(8,128)S(1)} collective-permute-done((f32[136,128]{1,0:T(8,128)S(1)}, f32[136,128]{1,0:T(8,128)S(1)}, u32[]{:S(2)}, u32[]{:S(2)}) %collective-permute-start.30) | collective-permute-done | bytes 69664 | tf_op jit(solution)/shard_map/ppermute | solution.py:362
  63.1 10.5 %conditional.1 = ((f32[256,256]{1,0:T(8,128)}, f32[256,4096]{1,0:T(8,128)})) conditional(s32[]{:T(128)} %bitcast.13, (s32[]{:T(128)}, f32[136,128]{1,0:T(8,128)S(1)}, f32[136,128]{1,0:T(8,128)S(1)}, bf16[256,4096]{1,0:T(8,128)(2,1)S(1)}, bf16[256,4096]{1,0:T(8,128)(2,1)S(1)}) %tuple.25, (s32[]{:T(128)}, f32[32,32768]{1,0:T(8,128)}, ...), branch_computations={%region_1.0_spmd, %region_2.0_spmd} | conditional | flops 3001178624 | bytes 44425160 | solution.py:441
  63.1 10.3 %branch_0_fun.1 = (f32[256,256]{1,0:T(8,128)}, f32[256,4096]{1,0:T(8,128)}) custom-call(s32[1]{0:T(128)} %bitcast.me_ref, f32[136,128]{1,0:T(8,128)S(1)} %get-tuple-element.23.mine_ref, f32[136,128]{1,0:T(8,128)S(1)} %get-tuple-element.24.other_ref, bf16[256,4096]{1,0:T(8,128)(2,1)S(1)} %get-tuple-element.25.refs_0_, ...), custom_call_target="tpu_custom_call" | custom-call | tf_op jit(solution)/shard_map/cond/branch_0_fun/pallas_call | solution.py:349
  (46 shorter events, 15.0 us)
Async XLA Ops:
  0.6 5.1 %collective-permute-start.15 = (f32[256,128]{1,0:T(8,128)}, f32[256,128]{1,0:T(8,128)S(1)}, u32[]{:S(2)}, u32[]{:S(2)}) collective-permute-start(f32[256,128]{1,0:T(8,128)} %bitcast.23), channel_id=1, source_target_pairs={{0,1},{1,0},{2,3},{3,2},{4,5},{5,4},{6,7},{7,6},{8,9},{9,8},{10,11... | collective-permute-start | bytes 393224 | tf_op jit(solution)/shard_map/ppermute | solution.py:362
  2.2 11.2 %collective-permute-start.22 = (f32[32,2048]{1,0:T(8,128)S(1)}, f32[32,2048]{1,0:T(8,128)S(1)}, u32[]{:S(2)}, u32[]{:S(2)}) collective-permute-start(f32[32,2048]{1,0:T(8,128)S(1)} %get-tuple-element.118), channel_id=1, source_target_pairs={{0,6},{1,7},{2,4},{3,5},{4,2},{5,3},{6,0},{7,1},{8,14},{9,15},{10,... | collective-permute-start | bytes 786440 | tf_op jit(solution)/shard_map/ppermute | solution.py:362
  5.8 3.2 %copy-start = (f32[32,32768]{1,0:T(8,128)S(1)}, f32[32,32768]{1,0:T(8,128)}, u32[]{:S(2)}) copy-start(f32[32,32768]{1,0:T(8,128)} %param.5) | copy-start | bytes 12582916
  5.8 3.8 %copy-start.1 = (s32[32768]{0:T(1024)S(1)}, s32[32768]{0:T(1024)}, u32[]{:S(2)}) copy-start(s32[32768]{0:T(1024)} %param.6) | copy-start | bytes 393220
  5.8 3.8 %copy-start.2 = (f32[32768]{0:T(1024)S(1)}, f32[32768]{0:T(1024)}, u32[]{:S(2)}) copy-start(f32[32768]{0:T(1024)} %param.7) | copy-start | bytes 393220
  8.4 1.2 %collective-permute-start.16 = (f32[8,128]{1,0:T(8,128)S(1)}, f32[8,128]{1,0:T(8,128)S(1)}, u32[]{:S(2)}, u32[]{:S(2)}) collective-permute-start(f32[8,128]{1,0:T(8,128)S(1)} %get-tuple-element.70.refs_9_), channel_id=1, source_target_pairs={{0,1},{1,0},{2,3},{3,2},{4,5},{5,4},{6,7},{7,6},{8,9},{9,8},{10,11... | collective-permute-start | bytes 12296 | tf_op jit(solution)/shard_map/ppermute | solution.py:362
  8.6 8.7 %collective-permute-start.23 = (f32[32,1536]{1,0:T(8,128)S(1)}, f32[32,1536]{1,0:T(8,128)S(1)}, u32[]{:S(2)}, u32[]{:S(2)}) collective-permute-start(f32[32,1536]{1,0:T(8,128)S(1)} %get-tuple-element.76), channel_id=1, source_target_pairs={{0,6},{1,7},{2,4},{3,5},{4,2},{5,3},{6,0},{7,1},{8,14},{9,15},{10,... | collective-permute-start | bytes 589832 | tf_op jit(solution)/shard_map/ppermute | solution.py:362
  9.1 9.3 %collective-permute-start.17 = (f32[32,4096]{1,0:T(8,128)S(1)}, f32[32,4096]{1,0:T(8,128)S(1)}, u32[]{:S(2)}, u32[]{:S(2)}) collective-permute-start(f32[32,4096]{1,0:T(8,128)S(1)} %get-tuple-element.126), channel_id=1, source_target_pairs={{0,1},{1,0},{2,3},{3,2},{4,5},{5,4},{6,7},{7,6},{8,9},{9,8},{10,11... | collective-permute-start | bytes 1572872 | tf_op jit(solution)/shard_map/ppermute | solution.py:362
  10.5 16.1 %collective-permute-start.24 = (f32[32,3072]{1,0:T(8,128)S(1)}, f32[32,3072]{1,0:T(8,128)S(1)}, u32[]{:S(2)}, u32[]{:S(2)}) collective-permute-start(f32[32,3072]{1,0:T(8,128)S(1)} %shard_map.55), channel_id=1, source_target_pairs={{0,7},{1,6},{2,5},{3,4},{4,3},{5,2},{6,1},{7,0},{8,15},{9,14},{10,... | collective-permute-start | bytes 1179656 | tf_op jit(solution)/shard_map/ppermute | solution.py:362
  19.7 15.8 %collective-permute-start.18 = (f32[32,3072]{1,0:T(8,128)S(1)}, f32[32,3072]{1,0:T(8,128)S(1)}, u32[]{:S(2)}, u32[]{:S(2)}) collective-permute-start(f32[32,3072]{1,0:T(8,128)S(1)} %shard_map.58), channel_id=1, source_target_pairs={{0,2},{1,3},{2,0},{3,1},{4,6},{5,7},{6,4},{7,5},{8,10},{9,11},{10,... | collective-permute-start | bytes 1179656 | tf_op jit(solution)/shard_map/ppermute | solution.py:362
  22.4 12.1 %collective-permute-start.20 = (f32[32,3072]{1,0:T(8,128)S(1)}, f32[32,3072]{1,0:T(8,128)S(1)}, u32[]{:S(2)}, u32[]{:S(2)}) collective-permute-start(f32[32,3072]{1,0:T(8,128)S(1)} %shard_map.60), channel_id=1, source_target_pairs={{0,4},{1,5},{2,6},{3,7},{4,0},{5,1},{6,2},{7,3},{8,12},{9,13},{10,... | collective-permute-start | bytes 1179656 | tf_op jit(solution)/shard_map/ppermute | solution.py:362
  24.9 17.1 %collective-permute-start.19 = (f32[32,3072]{1,0:T(8,128)S(1)}, f32[32,3072]{1,0:T(8,128)S(1)}, u32[]{:S(2)}, u32[]{:S(2)}) collective-permute-start(f32[32,3072]{1,0:T(8,128)S(1)} %shard_map.59), channel_id=1, source_target_pairs={{0,3},{1,2},{2,1},{3,0},{4,7},{5,6},{6,5},{7,4},{8,11},{9,10},{10,... | collective-permute-start | bytes 1179656 | tf_op jit(solution)/shard_map/ppermute | solution.py:362
  26.0 15.4 %collective-permute-start.21 = (f32[32,3072]{1,0:T(8,128)S(1)}, f32[32,3072]{1,0:T(8,128)S(1)}, u32[]{:S(2)}, u32[]{:S(2)}) collective-permute-start(f32[32,3072]{1,0:T(8,128)S(1)} %shard_map.61), channel_id=1, source_target_pairs={{0,5},{1,4},{2,7},{3,6},{4,1},{5,0},{6,3},{7,2},{8,13},{9,12},{10,... | collective-permute-start | bytes 1179656 | tf_op jit(solution)/shard_map/ppermute | solution.py:362
  43.9 1.3 %collective-permute-start.25 = (f32[136,128]{1,0:T(8,128)S(1)}, f32[136,128]{1,0:T(8,128)S(1)}, u32[]{:S(2)}, u32[]{:S(2)}) collective-permute-start(f32[136,128]{1,0:T(8,128)S(1)} %get-tuple-element.79), channel_id=1, source_target_pairs={{0,1},{1,0},{2,3},{3,2},{4,5},{5,4},{6,7},{7,6},{8,9},{9,8},{10,11... | collective-permute-start | bytes 208904 | tf_op jit(solution)/shard_map/ppermute | solution.py:362
  45.2 5.3 %collective-permute-start.28 = (f32[136,128]{1,0:T(8,128)S(1)}, f32[136,128]{1,0:T(8,128)S(1)}, u32[]{:S(2)}, u32[]{:S(2)}) collective-permute-start(f32[136,128]{1,0:T(8,128)S(1)} %add.116), channel_id=1, source_target_pairs={{0,6},{1,7},{2,4},{3,5},{4,2},{5,3},{6,0},{7,1},{8,14},{9,15},{10,... | collective-permute-start | bytes 208904 | tf_op jit(solution)/shard_map/ppermute | solution.py:362
  48.0 4.3 %collective-permute-start.27 = (f32[136,128]{1,0:T(8,128)S(1)}, f32[136,128]{1,0:T(8,128)S(1)}, u32[]{:S(2)}, u32[]{:S(2)}) collective-permute-start(f32[136,128]{1,0:T(8,128)S(1)} %add.116), channel_id=1, source_target_pairs={{0,4},{1,5},{2,6},{3,7},{4,0},{5,1},{6,2},{7,3},{8,12},{9,13},{10,... | collective-permute-start | bytes 208904 | tf_op jit(solution)/shard_map/ppermute | solution.py:362
  48.5 4.3 %collective-permute-start.26 = (f32[136,128]{1,0:T(8,128)S(1)}, f32[136,128]{1,0:T(8,128)S(1)}, u32[]{:S(2)}, u32[]{:S(2)}) collective-permute-start(f32[136,128]{1,0:T(8,128)S(1)} %add.116), channel_id=1, source_target_pairs={{0,2},{1,3},{2,0},{3,1},{4,6},{5,7},{6,4},{7,5},{8,10},{9,11},{10,... | collective-permute-start | bytes 208904 | tf_op jit(solution)/shard_map/ppermute | solution.py:362
  52.9 6.7 %collective-permute-start.31 = (f32[136,128]{1,0:T(8,128)S(1)}, f32[136,128]{1,0:T(8,128)S(1)}, u32[]{:S(2)}, u32[]{:S(2)}) collective-permute-start(f32[136,128]{1,0:T(8,128)S(1)} %add_add_fusion.3), channel_id=1, source_target_pairs={{0,24},{8,16},{16,8},{24,0},{1,25},{9,17},{17,9},{25,1},{2,26},{10... | collective-permute-start | bytes 208904 | tf_op jit(solution)/shard_map/ppermute | solution.py:362
  56.5 5.2 %collective-permute-start.30 = (f32[136,128]{1,0:T(8,128)S(1)}, f32[136,128]{1,0:T(8,128)S(1)}, u32[]{:S(2)}, u32[]{:S(2)}) collective-permute-start(f32[136,128]{1,0:T(8,128)S(1)} %add_add_fusion.3), channel_id=1, source_target_pairs={{0,16},{8,24},{16,0},{24,8},{1,17},{9,25},{17,1},{25,9},{2,18},{10... | collective-permute-start | bytes 208904 | tf_op jit(solution)/shard_map/ppermute | solution.py:362
  56.5 5.2 %collective-permute-start.29 = (f32[136,128]{1,0:T(8,128)S(1)}, f32[136,128]{1,0:T(8,128)S(1)}, u32[]{:S(2)}, u32[]{:S(2)}) collective-permute-start(f32[136,128]{1,0:T(8,128)S(1)} %add_add_fusion.3), channel_id=1, source_target_pairs={{0,8},{8,0},{16,24},{24,16},{1,9},{9,1},{17,25},{25,17},{2,10},{10... | collective-permute-start | bytes 208904 | tf_op jit(solution)/shard_map/ppermute | solution.py:362
  61.8 1.3 %collective-permute-start.32 = (f32[136,128]{1,0:T(8,128)S(1)}, f32[136,128]{1,0:T(8,128)S(1)}, u32[]{:S(2)}, u32[]{:S(2)}) collective-permute-start(f32[136,128]{1,0:T(8,128)S(1)} %add_add_fusion.2), channel_id=1, source_target_pairs={{0,1},{1,0},{2,3},{3,2},{4,5},{5,4},{6,7},{7,6},{8,9},{9,8},{10,11... | collective-permute-start | bytes 208904 | tf_op jit(solution)/shard_map/ppermute | solution.py:362

commit v5 on v4

--- a/solution.py
+++ b/solution.py
@@ -87,36 +87,50 @@
     return tiles
 
 
-def cholesky_and_inverse(a_ref, inverse_ref, upper_ref, lower_ref):
+def cholesky_and_inverse(a_ref, inverse_ref, upper_ref):
     order = a_ref.shape[0]
+    count = order // PANEL
     inverse_ref[...] = jnp.zeros((order, order), F32)
     upper_ref[...] = jnp.zeros((order, order), F32)
     lane = lax.broadcasted_iota(jnp.int32, (SUB, PANEL), 1)
     sub = lax.broadcasted_iota(jnp.int32, (SUB, PANEL), 0)
     block_row = lax.broadcasted_iota(jnp.int32, (PANEL, PANEL), 0)
     block_col = lax.broadcasted_iota(jnp.int32, (PANEL, PANEL), 1)
-    for first in range(0, order, PANEL):
-        end = first + PANEL
-        column = a_ref[first:, first:end]
-        if first:
-            done = split3(lower_ref[first:, :first])
-            column = column - product(done, tuple(term[:PANEL] for term in done), NT)
+    block = lambda i: slice(i * PANEL, (i + 1) * PANEL)
+    rows_of = lambda terms, first, end: tuple(term[first * PANEL : end * PANEL] for term in terms)
+    columns = [a_ref[j * PANEL :, block(j)] for j in range(count)]
+    left = [[] for _ in range(count)]
+    diag = columns[0][:PANEL]
+    for p in range(count):
         tiles = []
         for t in range(PANEL // SUB):
             eye = jnp.where(lane == sub + SUB * t, 1.0, 0.0)
-            tiles.append(jnp.concatenate([column[SUB * t : SUB * t + SUB], eye], 1))
+            tiles.append(jnp.concatenate([diag[SUB * t : SUB * t + SUB], eye], 1))
         both = jnp.concatenate(factor_panel(tiles, 0), 0)
-        upper_ref[first:end, first:end] = jnp.where(block_col >= block_row, both[:, :PANEL], 0.0)
+        upper_ref[block(p), block(p)] = jnp.where(block_col >= block_row, both[:, :PANEL], 0.0)
         own = both[:, PANEL:]
         own_terms = split3(own)
-        if end < order:
-            lower = product(split3(column[PANEL:]), own_terms, NT)
-            lower_ref[end:, first:end] = lower
-            upper_ref[first:end, end:] = lower.T
-        if first:
-            behind = product(tuple(term[:PANEL] for term in done), split3(inverse_ref[:first, :first]), NN)
-            inverse_ref[first:end, :first] = -product(own_terms, split3(behind), NN)
-        inverse_ref[first:end, first:end] = own
+        below = count - p - 1
+        if below:
+            lower = product(split3(columns[p][PANEL : 2 * PANEL]), own_terms, NT)
+            terms = split3(lower)
+            diag = columns[p + 1][:PANEL] - product(terms, terms, NT)
+        if below > 1:
+            more = product(split3(columns[p][2 * PANEL :]), own_terms, NT)
+            lower = jnp.concatenate([lower, more], 0)
+            terms = tuple(jnp.concatenate(pair, 0) for pair in zip(terms, split3(more)))
+            rest = columns[p + 1][PANEL:] - product(rows_of(terms, 1, below), rows_of(terms, 0, 1), NT)
+            columns[p + 1] = jnp.concatenate([columns[p + 1][:PANEL], rest], 0)
+            for i in range(1, below):
+                columns[p + 1 + i] = columns[p + 1 + i] - product(rows_of(terms, i, below), rows_of(terms, i, i + 1), NT)
+        if below:
+            upper_ref[block(p), (p + 1) * PANEL :] = lower.T
+            for i in range(below):
+                left[p + 1 + i].append(lower[block(i)])
+        if p:
+            behind = product(split3(jnp.concatenate(left[p], 1)), split3(inverse_ref[: p * PANEL, : p * PANEL]), NN)
+            inverse_ref[block(p), : p * PANEL] = -product(own_terms, split3(behind), NN)
+        inverse_ref[block(p), block(p)] = own
 
 
 HERE = pl.BlockSpec(memory_space=pltpu.VMEM)
@@ -312,7 +326,7 @@
 
 
 def solve_kernel(me_ref, mine_ref, other_ref, *refs):
-    term_refs, (upper_ref, scores_ref, out_ref, a_ref, inverse_ref, lower_ref, sems) = refs[:-7], refs[-7:]
+    term_refs, (upper_ref, scores_ref, out_ref, a_ref, inverse_ref, sems) = refs[:-6], refs[-6:]
     half = mine_ref.shape[1]
     first_core = (me_ref[0] & 1) == 0
     mine, other = mine_ref[...], other_ref[...]
@@ -326,7 +340,7 @@
     a_ref[:half, :half] = jnp.where(row >= col, both, turned) * scale
     a_ref[half:, half:] = jnp.where(row < col, both, jnp.where(row > col, turned, corner)) * scale
     a_ref[half:, :half] = off * scale
-    cholesky_and_inverse(a_ref, inverse_ref, upper_ref, lower_ref)
+    cholesky_and_inverse(a_ref, inverse_ref, upper_ref)
     high, low = split2(inverse_ref[...])
     copies, at = [], 0
     for high_ref, low_ref in zip(term_refs[::2], term_refs[1::2]):
@@ -352,7 +366,7 @@
         out_specs=[here, pl.BlockSpec(memory_space=pl.ANY)],
         out_shape=[jax.ShapeDtypeStruct(square, F32), jax.ShapeDtypeStruct((order, sum(cells)), F32)],
         scratch_shapes=[pltpu.VMEM((order, sum(cells)), F32)]
-        + [pltpu.VMEM(square, F32)] * 3
+        + [pltpu.VMEM(square, F32)] * 2
         + [pltpu.SemaphoreType.DMA((sum(-(-c // STEP) for c in cells),))],
         compiler_params=pltpu.CompilerParams(vmem_limit_bytes=VMEM_LIMIT),
     )(me[None], mine, other, *terms)
@@ -366,7 +380,7 @@
     size = lax.axis_size(axis)
     while first < size:
         if 2 * first < size:
-            near, far, both = swap(x, axis, first), swap(x, axis, 2 * first), swap(x, axis, 3 * first)
+            both, far, near = swap(x, axis, 3 * first), swap(x, axis, 2 * first), swap(x, axis, first)
             x = op(op(x, near), op(far, both))
         else:
             x = op(x, swap(x, axis, first))

time: 73.9 us -> 73.8 us (level)
  no operation moved by 1% of the time
where the time goes in v5:
time: 73.8 us; the launch traced here: 73.6 us
  Pallas kernels  29.2 us (40%)
  waiting for transfers between devices  20.4 us (28%)
  starting transfers between devices  19.5 us (26%)
  local copies, waits for them, and re-layouts  1.66 us (2%)
  between operations  1.57 us (2%)
  other arithmetic  1.08 us (1%)
    ppermute x18, waiting for transfers between devices, swap(): lax.ppermute(x, axis, [(i, i ^ mask) for i in range(lax.axis_size(axis))])  20.4 us
    ppermute x18, starting transfers between devices, swap(): lax.ppermute(x, axis, [(i, i ^ mask) for i in range(lax.axis_size(axis))])  19.5 us
    pallas_call x17, Pallas kernels, call(): pl.pallas_call(kernel, in_specs=[SCALARS] * scalars + [HERE] * (len(opera...  19.1 us
    pallas_call x1, Pallas kernels, solve(): pl.pallas_call(solve_kernel, in_specs=[pl.BlockSpec(memory_space=pltpu.SM...  10.1 us
  transfers between devices with their start and end apart: 18, of which 11 were waited for; matrix products, arithmetic and copies ran while one was open for 4% of the time, Pallas kernels for 23%

profile of v5, /device:TPU:0, one launch (start us, length us, event | category | flops | bytes accessed | tf_op | source)
XLA Modules:
  0.0 73.6 jit_solution(12593780226531972461)
XLA Ops:
  1.1 1.1 %constant_dynamic-slice_fusion.7 = (f32[32,2048]{1,0:T(8,128)S(1)}, f32[32,2048]{1,0:T(8,128)S(1)}) fusion(f32[32,32768]{1,0:T(8,128)} %param.5, s32[]{:T(128)S(6)} %select_n.63, s32[]{:T(128)S(6)} %select_n.55), kind=kLoop, calls=%fused_computation.26 | loop fusion | bytes 1048584 | tf_op jit(solution)/shard_map/dynamic_slice | solution.py:412
  2.2 3.5 %collective-permute-start.22 = (f32[32,2048]{1,0:T(8,128)S(1)}, f32[32,2048]{1,0:T(8,128)S(1)}, u32[]{:S(2)}, u32[]{:S(2)}) collective-permute-start(f32[32,2048]{1,0:T(8,128)S(1)} %get-tuple-element.118), channel_id=1, source_target_pairs={{0,6},{1,7},{2,4},{3,5},{4,2},{5,3},{6,0},{7,1},{8,14},{9,15},{10,... | collective-permute-start | bytes 786440 | tf_op jit(solution)/shard_map/ppermute | solution.py:376
  5.8 2.6 %shard_map.54 = (s32[8,32,128]{2,1,0:T(8,128)S(1)}, s32[8,32,128]{2,1,0:T(8,128)S(1)}, f32[8,128]{1,0:T(8,128)S(1)}, f32[32,1536]{1,0:T(8,128)S(1)}) custom-call(s32[1]{0:T(128)} %bitcast.4.base_ref, f32[32,2048]{1,0:T(8,128)S(1)} %get-tuple-element.119.x_ref, s32[256,128]{1,0:T(8,128)} %bitcast.14, f32[256,128]{1,0:T(8,128)} %bitcast.24, ...), custom_call_target="tpu_custom_call" | custom-call | flops 2000000000 | bytes 7200000 | tf_op jit(solution)/shard_map/pallas_call | solution.py:141
  10.5 2.3 %collective-permute-start.24 = (f32[32,3072]{1,0:T(8,128)S(1)}, f32[32,3072]{1,0:T(8,128)S(1)}, u32[]{:S(2)}, u32[]{:S(2)}) collective-permute-start(f32[32,3072]{1,0:T(8,128)S(1)} %shard_map.55), channel_id=1, source_target_pairs={{0,7},{1,6},{2,5},{3,4},{4,3},{5,2},{6,1},{7,0},{8,15},{9,14},{10,... | collective-permute-start | bytes 1179656 | tf_op jit(solution)/shard_map/ppermute | solution.py:376
  14.0 3.4 %collective-permute-done.23 = f32[32,1536]{1,0:T(8,128)S(1)} collective-permute-done((f32[32,1536]{1,0:T(8,128)S(1)}, f32[32,1536]{1,0:T(8,128)S(1)}, u32[]{:S(2)}, u32[]{:S(2)}) %collective-permute-start.23) | collective-permute-done | bytes 196640 | tf_op jit(solution)/shard_map/ppermute | solution.py:376
  17.4 1.0 %shard_map.65.refs_6_ = f32[32,4096]{1,0:T(8,128)S(1)} custom-call(s32[1]{0:T(128)} %bitcast.2.me_ref, s32[8,32,128]{2,1,0:T(8,128)S(1)} %get-tuple-element.87.rank_ref, f32[32,3072]{1,0:T(8,128)S(1)} %pad_maximum_fusion.kept_ref.refs_6_), custom_call_target="tpu_custom_call" | custom-call | flops 1000000000 | bytes 3600000 | tf_op jit(solution)/shard_map/pallas_call | solution.py:141
  19.7 1.7 %collective-permute-start.18 = (f32[32,3072]{1,0:T(8,128)S(1)}, f32[32,3072]{1,0:T(8,128)S(1)}, u32[]{:S(2)}, u32[]{:S(2)}) collective-permute-start(f32[32,3072]{1,0:T(8,128)S(1)} %shard_map.58), channel_id=1, source_target_pairs={{0,2},{1,3},{2,0},{3,1},{4,6},{5,7},{6,4},{7,5},{8,10},{9,11},{10,... | collective-permute-start | bytes 1179656 | tf_op jit(solution)/shard_map/ppermute | solution.py:376
  22.4 1.6 %collective-permute-start.20 = (f32[32,3072]{1,0:T(8,128)S(1)}, f32[32,3072]{1,0:T(8,128)S(1)}, u32[]{:S(2)}, u32[]{:S(2)}) collective-permute-start(f32[32,3072]{1,0:T(8,128)S(1)} %shard_map.60), channel_id=1, source_target_pairs={{0,4},{1,5},{2,6},{3,7},{4,0},{5,1},{6,2},{7,3},{8,12},{9,13},{10,... | collective-permute-start | bytes 1179656 | tf_op jit(solution)/shard_map/ppermute | solution.py:376
  26.6 1.0 %shard_map.66.refs_7_ = f32[32,4096]{1,0:T(8,128)S(1)} custom-call(s32[1]{0:T(128)} %bitcast.2.me_ref, s32[8,32,128]{2,1,0:T(8,128)S(1)} %get-tuple-element.87.rank_ref, f32[32,3072]{1,0:T(8,128)S(1)} %collective-permute-done.24.kept_ref.refs_7_), custom_call_target="tpu_custom_call" | custom-call | flops 1000000000 | bytes 3600000 | tf_op jit(solution)/shard_map/pallas_call | solution.py:141
  29.5 5.0 %collective-permute-done.20.kept_ref.refs_4_ = f32[32,3072]{1,0:T(8,128)S(1)} collective-permute-done((f32[32,3072]{1,0:T(8,128)S(1)}, f32[32,3072]{1,0:T(8,128)S(1)}, u32[]{:S(2)}, u32[]{:S(2)}) %collective-permute-start.20) | collective-permute-done | bytes 393248 | tf_op jit(solution)/shard_map/ppermute | solution.py:376
  34.5 1.0 %shard_map.63.refs_4_ = f32[32,4096]{1,0:T(8,128)S(1)} custom-call(s32[1]{0:T(128)} %bitcast.2.me_ref, s32[8,32,128]{2,1,0:T(8,128)S(1)} %get-tuple-element.87.rank_ref, f32[32,3072]{1,0:T(8,128)S(1)} %collective-permute-done.20.kept_ref.refs_4_), custom_call_target="tpu_custom_call" | custom-call | flops 1000000000 | bytes 3600000 | tf_op jit(solution)/shard_map/pallas_call | solution.py:141
  35.5 1.0 %shard_map.62.refs_2_ = f32[32,4096]{1,0:T(8,128)S(1)} custom-call(s32[1]{0:T(128)} %bitcast.2.me_ref, s32[8,32,128]{2,1,0:T(8,128)S(1)} %get-tuple-element.87.rank_ref, f32[32,3072]{1,0:T(8,128)S(1)} %collective-permute-done.18.kept_ref.refs_2_), custom_call_target="tpu_custom_call" | custom-call | flops 1000000000 | bytes 3600000 | tf_op jit(solution)/shard_map/pallas_call | solution.py:141
  36.5 4.9 %collective-permute-done.21.refs_5_.kept_ref = f32[32,3072]{1,0:T(8,128)S(1)} collective-permute-done((f32[32,3072]{1,0:T(8,128)S(1)}, f32[32,3072]{1,0:T(8,128)S(1)}, u32[]{:S(2)}, u32[]{:S(2)}) %collective-permute-start.21) | collective-permute-done | bytes 393248 | tf_op jit(solution)/shard_map/ppermute | solution.py:376
  42.0 1.9 %shard_map.67 = (f32[136,128]{1,0:T(8,128)S(1)}, f32[136,128]{1,0:T(8,128)S(1)}) custom-call(s32[1]{0:T(128)} %bitcast.2.me_ref, f32[32,3072]{1,0:T(8,128)S(1)} %shard_map.56.refs_0_, f32[32,3072]{1,0:T(8,128)S(1)} %shard_map.57.refs_1_, f32[32,3072]{1,0:T(8,128)S(1)} %collective-permute-done.18.kept_ref.refs_2_, ...), custom_call_target="tpu_custom_call" | custom-call | flops 2000000000 | bytes 7200000 | tf_op jit(solution)/shard_map/pallas_call | solution.py:141
  44.2 1.0 %collective-permute-done.25 = f32[136,128]{1,0:T(8,128)S(1)} collective-permute-done((f32[136,128]{1,0:T(8,128)S(1)}, f32[136,128]{1,0:T(8,128)S(1)}, u32[]{:S(2)}, u32[]{:S(2)}) %collective-permute-start.25) | collective-permute-done | bytes 69664 | tf_op jit(solution)/shard_map/ppermute | solution.py:376
  45.2 2.8 %collective-permute-start.28 = (f32[136,128]{1,0:T(8,128)S(1)}, f32[136,128]{1,0:T(8,128)S(1)}, u32[]{:S(2)}, u32[]{:S(2)}) collective-permute-start(f32[136,128]{1,0:T(8,128)S(1)} %add.116), channel_id=1, source_target_pairs={{0,6},{1,7},{2,4},{3,5},{4,2},{5,3},{6,0},{7,1},{8,14},{9,15},{10,... | collective-permute-start | bytes 208904 | tf_op jit(solution)/shard_map/ppermute | solution.py:376
  48.8 1.2 %shard_map.68.refs_3_ = f32[32,4096]{1,0:T(8,128)S(1)} custom-call(s32[1]{0:T(128)} %bitcast.2.me_ref, s32[8,32,128]{2,1,0:T(8,128)S(1)} %get-tuple-element.87.rank_ref, f32[32,3072]{1,0:T(8,128)S(1)} %collective-permute-done.19.refs_3_.kept_ref), custom_call_target="tpu_custom_call" | custom-call | flops 1000000000 | bytes 3600000 | tf_op jit(solution)/shard_map/pallas_call | solution.py:141
  50.6 1.8 %collective-permute-done.27 = f32[136,128]{1,0:T(8,128)S(1)} collective-permute-done((f32[136,128]{1,0:T(8,128)S(1)}, f32[136,128]{1,0:T(8,128)S(1)}, u32[]{:S(2)}, u32[]{:S(2)}) %collective-permute-start.27) | collective-permute-done | bytes 69664 | tf_op jit(solution)/shard_map/ppermute | solution.py:376
  52.9 3.7 %collective-permute-start.31 = (f32[136,128]{1,0:T(8,128)S(1)}, f32[136,128]{1,0:T(8,128)S(1)}, u32[]{:S(2)}, u32[]{:S(2)}) collective-permute-start(f32[136,128]{1,0:T(8,128)S(1)} %add_add_fusion.3), channel_id=1, source_target_pairs={{0,24},{8,16},{16,8},{24,0},{1,25},{9,17},{17,9},{25,1},{2,26},{10... | collective-permute-start | bytes 208904 | tf_op jit(solution)/shard_map/ppermute | solution.py:376
  57.3 1.0 %shard_map.69.refs_5_ = f32[32,4096]{1,0:T(8,128)S(1)} custom-call(s32[1]{0:T(128)} %bitcast.2.me_ref, s32[8,32,128]{2,1,0:T(8,128)S(1)} %get-tuple-element.87.rank_ref, f32[32,3072]{1,0:T(8,128)S(1)} %collective-permute-done.21.refs_5_.kept_ref), custom_call_target="tpu_custom_call" | custom-call | flops 1000000000 | bytes 3600000 | tf_op jit(solution)/shard_map/pallas_call | solution.py:141
  58.3 1.3 %shard_map.70 = (bf16[256,4096]{1,0:T(8,128)(2,1)S(1)}, bf16[256,4096]{1,0:T(8,128)(2,1)S(1)}) custom-call(s32[1]{0:T(128)} %bitcast.2.me_ref, f32[32,4096]{1,0:T(8,128)S(1)} %get-tuple-element.83.refs_0_, f32[32,4096]{1,0:T(8,128)S(1)} %get-tuple-element.84.refs_1_, f32[32,4096]{1,0:T(8,128)S(1)} %shard_map.62.refs_2_, f32[32,4096]{1,0:T(8,128)S(1)} %shard_map.68.refs_3_, ...), custom_call_target="tpu_custom_call" | custom-call | flops 1000000000 | bytes 3600000 | tf_op jit(solution)/shard_map/pallas_call | solution.py:141
  59.6 2.1 %collective-permute-done.30 = f32[136,128]{1,0:T(8,128)S(1)} collective-permute-done((f32[136,128]{1,0:T(8,128)S(1)}, f32[136,128]{1,0:T(8,128)S(1)}, u32[]{:S(2)}, u32[]{:S(2)}) %collective-permute-start.30) | collective-permute-done | bytes 69664 | tf_op jit(solution)/shard_map/ppermute | solution.py:376
  63.1 10.3 %conditional.1 = ((f32[256,256]{1,0:T(8,128)}, f32[256,4096]{1,0:T(8,128)})) conditional(s32[]{:T(128)} %bitcast.13, (s32[]{:T(128)}, f32[136,128]{1,0:T(8,128)S(1)}, f32[136,128]{1,0:T(8,128)S(1)}, bf16[256,4096]{1,0:T(8,128)(2,1)S(1)}, bf16[256,4096]{1,0:T(8,128)(2,1)S(1)}) %tuple.25, (s32[]{:T(128)}, f32[32,32768]{1,0:T(8,128)}, ...), branch_computations={%region_1.0_spmd, %region_2.0_spmd} | conditional | flops 3001178624 | bytes 44425160 | solution.py:455
  63.1 10.1 %branch_0_fun.1 = (f32[256,256]{1,0:T(8,128)}, f32[256,4096]{1,0:T(8,128)}) custom-call(s32[1]{0:T(128)} %bitcast.me_ref, f32[136,128]{1,0:T(8,128)S(1)} %get-tuple-element.23.mine_ref, f32[136,128]{1,0:T(8,128)S(1)} %get-tuple-element.24.other_ref, bf16[256,4096]{1,0:T(8,128)(2,1)S(1)} %get-tuple-element.25.refs_0_, ...), custom_call_target="tpu_custom_call" | custom-call | tf_op jit(solution)/shard_map/cond/branch_0_fun/pallas_call | solution.py:363
  (46 shorter events, 15.0 us)
Async XLA Ops:
  0.6 5.1 %collective-permute-start.15 = (f32[256,128]{1,0:T(8,128)}, f32[256,128]{1,0:T(8,128)S(1)}, u32[]{:S(2)}, u32[]{:S(2)}) collective-permute-start(f32[256,128]{1,0:T(8,128)} %bitcast.23), channel_id=1, source_target_pairs={{0,1},{1,0},{2,3},{3,2},{4,5},{5,4},{6,7},{7,6},{8,9},{9,8},{10,11... | collective-permute-start | bytes 393224 | tf_op jit(solution)/shard_map/ppermute | solution.py:376
  2.2 11.2 %collective-permute-start.22 = (f32[32,2048]{1,0:T(8,128)S(1)}, f32[32,2048]{1,0:T(8,128)S(1)}, u32[]{:S(2)}, u32[]{:S(2)}) collective-permute-start(f32[32,2048]{1,0:T(8,128)S(1)} %get-tuple-element.118), channel_id=1, source_target_pairs={{0,6},{1,7},{2,4},{3,5},{4,2},{5,3},{6,0},{7,1},{8,14},{9,15},{10,... | collective-permute-start | bytes 786440 | tf_op jit(solution)/shard_map/ppermute | solution.py:376
  5.8 3.2 %copy-start = (f32[32,32768]{1,0:T(8,128)S(1)}, f32[32,32768]{1,0:T(8,128)}, u32[]{:S(2)}) copy-start(f32[32,32768]{1,0:T(8,128)} %param.5) | copy-start | bytes 12582916
  5.8 3.8 %copy-start.1 = (s32[32768]{0:T(1024)S(1)}, s32[32768]{0:T(1024)}, u32[]{:S(2)}) copy-start(s32[32768]{0:T(1024)} %param.6) | copy-start | bytes 393220
  5.8 3.8 %copy-start.2 = (f32[32768]{0:T(1024)S(1)}, f32[32768]{0:T(1024)}, u32[]{:S(2)}) copy-start(f32[32768]{0:T(1024)} %param.7) | copy-start | bytes 393220
  8.4 1.2 %collective-permute-start.16 = (f32[8,128]{1,0:T(8,128)S(1)}, f32[8,128]{1,0:T(8,128)S(1)}, u32[]{:S(2)}, u32[]{:S(2)}) collective-permute-start(f32[8,128]{1,0:T(8,128)S(1)} %get-tuple-element.70.refs_9_), channel_id=1, source_target_pairs={{0,1},{1,0},{2,3},{3,2},{4,5},{5,4},{6,7},{7,6},{8,9},{9,8},{10,11... | collective-permute-start | bytes 12296 | tf_op jit(solution)/shard_map/ppermute | solution.py:376
  8.6 8.7 %collective-permute-start.23 = (f32[32,1536]{1,0:T(8,128)S(1)}, f32[32,1536]{1,0:T(8,128)S(1)}, u32[]{:S(2)}, u32[]{:S(2)}) collective-permute-start(f32[32,1536]{1,0:T(8,128)S(1)} %get-tuple-element.76), channel_id=1, source_target_pairs={{0,6},{1,7},{2,4},{3,5},{4,2},{5,3},{6,0},{7,1},{8,14},{9,15},{10,... | collective-permute-start | bytes 589832 | tf_op jit(solution)/shard_map/ppermute | solution.py:376
  9.1 9.3 %collective-permute-start.17 = (f32[32,4096]{1,0:T(8,128)S(1)}, f32[32,4096]{1,0:T(8,128)S(1)}, u32[]{:S(2)}, u32[]{:S(2)}) collective-permute-start(f32[32,4096]{1,0:T(8,128)S(1)} %get-tuple-element.126), channel_id=1, source_target_pairs={{0,1},{1,0},{2,3},{3,2},{4,5},{5,4},{6,7},{7,6},{8,9},{9,8},{10,11... | collective-permute-start | bytes 1572872 | tf_op jit(solution)/shard_map/ppermute | solution.py:376
  10.5 16.1 %collective-permute-start.24 = (f32[32,3072]{1,0:T(8,128)S(1)}, f32[32,3072]{1,0:T(8,128)S(1)}, u32[]{:S(2)}, u32[]{:S(2)}) collective-permute-start(f32[32,3072]{1,0:T(8,128)S(1)} %shard_map.55), channel_id=1, source_target_pairs={{0,7},{1,6},{2,5},{3,4},{4,3},{5,2},{6,1},{7,0},{8,15},{9,14},{10,... | collective-permute-start | bytes 1179656 | tf_op jit(solution)/shard_map/ppermute | solution.py:376
  19.7 15.8 %collective-permute-start.18 = (f32[32,3072]{1,0:T(8,128)S(1)}, f32[32,3072]{1,0:T(8,128)S(1)}, u32[]{:S(2)}, u32[]{:S(2)}) collective-permute-start(f32[32,3072]{1,0:T(8,128)S(1)} %shard_map.58), channel_id=1, source_target_pairs={{0,2},{1,3},{2,0},{3,1},{4,6},{5,7},{6,4},{7,5},{8,10},{9,11},{10,... | collective-permute-start | bytes 1179656 | tf_op jit(solution)/shard_map/ppermute | solution.py:376
  22.4 12.1 %collective-permute-start.20 = (f32[32,3072]{1,0:T(8,128)S(1)}, f32[32,3072]{1,0:T(8,128)S(1)}, u32[]{:S(2)}, u32[]{:S(2)}) collective-permute-start(f32[32,3072]{1,0:T(8,128)S(1)} %shard_map.60), channel_id=1, source_target_pairs={{0,4},{1,5},{2,6},{3,7},{4,0},{5,1},{6,2},{7,3},{8,12},{9,13},{10,... | collective-permute-start | bytes 1179656 | tf_op jit(solution)/shard_map/ppermute | solution.py:376
  24.9 17.1 %collective-permute-start.19 = (f32[32,3072]{1,0:T(8,128)S(1)}, f32[32,3072]{1,0:T(8,128)S(1)}, u32[]{:S(2)}, u32[]{:S(2)}) collective-permute-start(f32[32,3072]{1,0:T(8,128)S(1)} %shard_map.59), channel_id=1, source_target_pairs={{0,3},{1,2},{2,1},{3,0},{4,7},{5,6},{6,5},{7,4},{8,11},{9,10},{10,... | collective-permute-start | bytes 1179656 | tf_op jit(solution)/shard_map/ppermute | solution.py:376
  26.0 15.4 %collective-permute-start.21 = (f32[32,3072]{1,0:T(8,128)S(1)}, f32[32,3072]{1,0:T(8,128)S(1)}, u32[]{:S(2)}, u32[]{:S(2)}) collective-permute-start(f32[32,3072]{1,0:T(8,128)S(1)} %shard_map.61), channel_id=1, source_target_pairs={{0,5},{1,4},{2,7},{3,6},{4,1},{5,0},{6,3},{7,2},{8,13},{9,12},{10,... | collective-permute-start | bytes 1179656 | tf_op jit(solution)/shard_map/ppermute | solution.py:376
  43.9 1.3 %collective-permute-start.25 = (f32[136,128]{1,0:T(8,128)S(1)}, f32[136,128]{1,0:T(8,128)S(1)}, u32[]{:S(2)}, u32[]{:S(2)}) collective-permute-start(f32[136,128]{1,0:T(8,128)S(1)} %get-tuple-element.79), channel_id=1, source_target_pairs={{0,1},{1,0},{2,3},{3,2},{4,5},{5,4},{6,7},{7,6},{8,9},{9,8},{10,11... | collective-permute-start | bytes 208904 | tf_op jit(solution)/shard_map/ppermute | solution.py:376
  45.2 5.3 %collective-permute-start.28 = (f32[136,128]{1,0:T(8,128)S(1)}, f32[136,128]{1,0:T(8,128)S(1)}, u32[]{:S(2)}, u32[]{:S(2)}) collective-permute-start(f32[136,128]{1,0:T(8,128)S(1)} %add.116), channel_id=1, source_target_pairs={{0,6},{1,7},{2,4},{3,5},{4,2},{5,3},{6,0},{7,1},{8,14},{9,15},{10,... | collective-permute-start | bytes 208904 | tf_op jit(solution)/shard_map/ppermute | solution.py:376
  48.0 4.3 %collective-permute-start.27 = (f32[136,128]{1,0:T(8,128)S(1)}, f32[136,128]{1,0:T(8,128)S(1)}, u32[]{:S(2)}, u32[]{:S(2)}) collective-permute-start(f32[136,128]{1,0:T(8,128)S(1)} %add.116), channel_id=1, source_target_pairs={{0,4},{1,5},{2,6},{3,7},{4,0},{5,1},{6,2},{7,3},{8,12},{9,13},{10,... | collective-permute-start | bytes 208904 | tf_op jit(solution)/shard_map/ppermute | solution.py:376
  48.5 4.3 %collective-permute-start.26 = (f32[136,128]{1,0:T(8,128)S(1)}, f32[136,128]{1,0:T(8,128)S(1)}, u32[]{:S(2)}, u32[]{:S(2)}) collective-permute-start(f32[136,128]{1,0:T(8,128)S(1)} %add.116), channel_id=1, source_target_pairs={{0,2},{1,3},{2,0},{3,1},{4,6},{5,7},{6,4},{7,5},{8,10},{9,11},{10,... | collective-permute-start | bytes 208904 | tf_op jit(solution)/shard_map/ppermute | solution.py:376
  52.9 6.7 %collective-permute-start.31 = (f32[136,128]{1,0:T(8,128)S(1)}, f32[136,128]{1,0:T(8,128)S(1)}, u32[]{:S(2)}, u32[]{:S(2)}) collective-permute-start(f32[136,128]{1,0:T(8,128)S(1)} %add_add_fusion.3), channel_id=1, source_target_pairs={{0,24},{8,16},{16,8},{24,0},{1,25},{9,17},{17,9},{25,1},{2,26},{10... | collective-permute-start | bytes 208904 | tf_op jit(solution)/shard_map/ppermute | solution.py:376
  56.5 5.2 %collective-permute-start.30 = (f32[136,128]{1,0:T(8,128)S(1)}, f32[136,128]{1,0:T(8,128)S(1)}, u32[]{:S(2)}, u32[]{:S(2)}) collective-permute-start(f32[136,128]{1,0:T(8,128)S(1)} %add_add_fusion.3), channel_id=1, source_target_pairs={{0,16},{8,24},{16,0},{24,8},{1,17},{9,25},{17,1},{25,9},{2,18},{10... | collective-permute-start | bytes 208904 | tf_op jit(solution)/shard_map/ppermute | solution.py:376
  56.5 5.2 %collective-permute-start.29 = (f32[136,128]{1,0:T(8,128)S(1)}, f32[136,128]{1,0:T(8,128)S(1)}, u32[]{:S(2)}, u32[]{:S(2)}) collective-permute-start(f32[136,128]{1,0:T(8,128)S(1)} %add_add_fusion.3), channel_id=1, source_target_pairs={{0,8},{8,0},{16,24},{24,16},{1,9},{9,1},{17,25},{25,17},{2,10},{10... | collective-permute-start | bytes 208904 | tf_op jit(solution)/shard_map/ppermute | solution.py:376
  61.8 1.3 %collective-permute-start.32 = (f32[136,128]{1,0:T(8,128)S(1)}, f32[136,128]{1,0:T(8,128)S(1)}, u32[]{:S(2)}, u32[]{:S(2)}) collective-permute-start(f32[136,128]{1,0:T(8,128)S(1)} %add_add_fusion.2), channel_id=1, source_target_pairs={{0,1},{1,0},{2,3},{3,2},{4,5},{5,4},{6,7},{7,6},{8,9},{9,8},{10,11... | collective-permute-start | bytes 208904 | tf_op jit(solution)/shard_map/ppermute | solution.py:376

commit v6 on v5

--- a/solution.py
+++ b/solution.py
@@ -87,7 +87,7 @@
     return tiles
 
 
-def cholesky_and_inverse(a_ref, inverse_ref, upper_ref):
+def cholesky_and_inverse(a_ref, inverse_ref, upper_ref, after):
     order = a_ref.shape[0]
     count = order // PANEL
     inverse_ref[...] = jnp.zeros((order, order), F32)
@@ -131,6 +131,7 @@
             behind = product(split3(jnp.concatenate(left[p], 1)), split3(inverse_ref[: p * PANEL, : p * PANEL]), NN)
             inverse_ref[block(p), : p * PANEL] = -product(own_terms, split3(behind), NN)
         inverse_ref[block(p), block(p)] = own
+        after((p + 1) * PANEL)
 
 
 HERE = pl.BlockSpec(memory_space=pltpu.VMEM)
@@ -340,18 +341,21 @@
     a_ref[:half, :half] = jnp.where(row >= col, both, turned) * scale
     a_ref[half:, half:] = jnp.where(row < col, both, jnp.where(row > col, turned, corner)) * scale
     a_ref[half:, :half] = off * scale
-    cholesky_and_inverse(a_ref, inverse_ref, upper_ref)
-    high, low = split2(inverse_ref[...])
-    copies, at = [], 0
-    for high_ref, low_ref in zip(term_refs[::2], term_refs[1::2]):
+    high_ref, low_ref = term_refs
+    copies = []
+
+    def form_scores(rows):
+        if rows % half:
+            return
+        high, low = split2(inverse_ref[rows - half : rows, :rows])
         for first in range(0, high_ref.shape[1], STEP):
-            here = slice(first, min(first + STEP, high_ref.shape[1]))
-            there = slice(at + here.start, at + here.stop)
-            high_term = high_ref[:, here]
-            out_ref[:, there] = dot(high, high_term, NN) + (dot(high, low_ref[:, here], NN) + dot(low, high_term, NN))
-            copies.append(pltpu.make_async_copy(out_ref.at[:, there], scores_ref.at[:, there], sems.at[len(copies)]))
+            at = (slice(rows - half, rows), slice(first, min(first + STEP, high_ref.shape[1])))
+            high_term, low_term = high_ref[:rows, at[1]], low_ref[:rows, at[1]]
+            out_ref[at] = dot(high, high_term, NN) + (dot(high, low_term, NN) + dot(low, high_term, NN))
+            copies.append(pltpu.make_async_copy(out_ref.at[at], scores_ref.at[at], sems.at[len(copies)]))
             copies[-1].start()
-        at += high_ref.shape[1]
+
+    cholesky_and_inverse(a_ref, inverse_ref, upper_ref, form_scores)
     for copy in copies:
         copy.wait()
 
@@ -367,7 +371,7 @@
         out_shape=[jax.ShapeDtypeStruct(square, F32), jax.ShapeDtypeStruct((order, sum(cells)), F32)],
         scratch_shapes=[pltpu.VMEM((order, sum(cells)), F32)]
         + [pltpu.VMEM(square, F32)] * 2
-        + [pltpu.SemaphoreType.DMA((sum(-(-c // STEP) for c in cells),))],
+        + [pltpu.SemaphoreType.DMA((2 * sum(-(-c // STEP) for c in cells),))],
         compiler_params=pltpu.CompilerParams(vmem_limit_bytes=VMEM_LIMIT),
     )(me[None], mine, other, *terms)
 

time: 73.8 us -> 73 us (0.989)
  transfers between devices with their start and end apart: 18 -> 18, of which waited for: 11 -> 11; matrix products, arithmetic and copies ran while one was open for 4% -> 4% of each run, Pallas kernels for 23% -> 24%
where the time goes in v6:
time: 73 us; the launch traced here: 72.9 us
  Pallas kernels  28.5 us (39%)
  waiting for transfers between devices  20.4 us (28%)
  starting transfers between devices  19.5 us (27%)
  local copies, waits for them, and re-layouts  1.66 us (2%)
  between operations  1.57 us (2%)
  other arithmetic  1.08 us (1%)
    ppermute x18, waiting for transfers between devices, swap(): lax.ppermute(x, axis, [(i, i ^ mask) for i in range(lax.axis_size(axis))])  20.4 us
    ppermute x18, starting transfers between devices, swap(): lax.ppermute(x, axis, [(i, i ^ mask) for i in range(lax.axis_size(axis))])  19.5 us
    pallas_call x17, Pallas kernels, call(): pl.pallas_call(kernel, in_specs=[SCALARS] * scalars + [HERE] * (len(opera...  19.1 us
    pallas_call x1, Pallas kernels, solve(): pl.pallas_call(solve_kernel, in_specs=[pl.BlockSpec(memory_space=pltpu.SM...  9.38 us
  transfers between devices with their start and end apart: 18, of which 11 were waited for; matrix products, arithmetic and copies ran while one was open for 4% of the time, Pallas kernels for 24%

profile of v6, /device:TPU:0, one launch (start us, length us, event | category | flops | bytes accessed | tf_op | source)
XLA Modules:
  0.0 72.9 jit_solution(2302268674476714401)
XLA Ops:
  1.1 1.1 %constant_dynamic-slice_fusion.7 = (f32[32,2048]{1,0:T(8,128)S(1)}, f32[32,2048]{1,0:T(8,128)S(1)}) fusion(f32[32,32768]{1,0:T(8,128)} %param.5, s32[]{:T(128)S(6)} %select_n.63, s32[]{:T(128)S(6)} %select_n.55), kind=kLoop, calls=%fused_computation.26 | loop fusion | bytes 1048584 | tf_op jit(solution)/shard_map/dynamic_slice | solution.py:416
  2.2 3.5 %collective-permute-start.22 = (f32[32,2048]{1,0:T(8,128)S(1)}, f32[32,2048]{1,0:T(8,128)S(1)}, u32[]{:S(2)}, u32[]{:S(2)}) collective-permute-start(f32[32,2048]{1,0:T(8,128)S(1)} %get-tuple-element.118), channel_id=1, source_target_pairs={{0,6},{1,7},{2,4},{3,5},{4,2},{5,3},{6,0},{7,1},{8,14},{9,15},{10,... | collective-permute-start | bytes 786440 | tf_op jit(solution)/shard_map/ppermute | solution.py:380
  5.8 2.6 %shard_map.54 = (s32[8,32,128]{2,1,0:T(8,128)S(1)}, s32[8,32,128]{2,1,0:T(8,128)S(1)}, f32[8,128]{1,0:T(8,128)S(1)}, f32[32,1536]{1,0:T(8,128)S(1)}) custom-call(s32[1]{0:T(128)} %bitcast.4.base_ref, f32[32,2048]{1,0:T(8,128)S(1)} %get-tuple-element.119.x_ref, s32[256,128]{1,0:T(8,128)} %bitcast.14, f32[256,128]{1,0:T(8,128)} %bitcast.24, ...), custom_call_target="tpu_custom_call" | custom-call | flops 2000000000 | bytes 7200000 | tf_op jit(solution)/shard_map/pallas_call | solution.py:142
  10.5 2.3 %collective-permute-start.24 = (f32[32,3072]{1,0:T(8,128)S(1)}, f32[32,3072]{1,0:T(8,128)S(1)}, u32[]{:S(2)}, u32[]{:S(2)}) collective-permute-start(f32[32,3072]{1,0:T(8,128)S(1)} %shard_map.55), channel_id=1, source_target_pairs={{0,7},{1,6},{2,5},{3,4},{4,3},{5,2},{6,1},{7,0},{8,15},{9,14},{10,... | collective-permute-start | bytes 1179656 | tf_op jit(solution)/shard_map/ppermute | solution.py:380
  14.0 3.4 %collective-permute-done.23 = f32[32,1536]{1,0:T(8,128)S(1)} collective-permute-done((f32[32,1536]{1,0:T(8,128)S(1)}, f32[32,1536]{1,0:T(8,128)S(1)}, u32[]{:S(2)}, u32[]{:S(2)}) %collective-permute-start.23) | collective-permute-done | bytes 196640 | tf_op jit(solution)/shard_map/ppermute | solution.py:380
  17.4 1.0 %shard_map.65.refs_6_ = f32[32,4096]{1,0:T(8,128)S(1)} custom-call(s32[1]{0:T(128)} %bitcast.2.me_ref, s32[8,32,128]{2,1,0:T(8,128)S(1)} %get-tuple-element.87.rank_ref, f32[32,3072]{1,0:T(8,128)S(1)} %pad_maximum_fusion.kept_ref.refs_6_), custom_call_target="tpu_custom_call" | custom-call | flops 1000000000 | bytes 3600000 | tf_op jit(solution)/shard_map/pallas_call | solution.py:142
  19.7 1.7 %collective-permute-start.18 = (f32[32,3072]{1,0:T(8,128)S(1)}, f32[32,3072]{1,0:T(8,128)S(1)}, u32[]{:S(2)}, u32[]{:S(2)}) collective-permute-start(f32[32,3072]{1,0:T(8,128)S(1)} %shard_map.58), channel_id=1, source_target_pairs={{0,2},{1,3},{2,0},{3,1},{4,6},{5,7},{6,4},{7,5},{8,10},{9,11},{10,... | collective-permute-start | bytes 1179656 | tf_op jit(solution)/shard_map/ppermute | solution.py:380
  22.4 1.6 %collective-permute-start.20 = (f32[32,3072]{1,0:T(8,128)S(1)}, f32[32,3072]{1,0:T(8,128)S(1)}, u32[]{:S(2)}, u32[]{:S(2)}) collective-permute-start(f32[32,3072]{1,0:T(8,128)S(1)} %shard_map.60), channel_id=1, source_target_pairs={{0,4},{1,5},{2,6},{3,7},{4,0},{5,1},{6,2},{7,3},{8,12},{9,13},{10,... | collective-permute-start | bytes 1179656 | tf_op jit(solution)/shard_map/ppermute | solution.py:380
  26.6 1.0 %shard_map.66.refs_7_ = f32[32,4096]{1,0:T(8,128)S(1)} custom-call(s32[1]{0:T(128)} %bitcast.2.me_ref, s32[8,32,128]{2,1,0:T(8,128)S(1)} %get-tuple-element.87.rank_ref, f32[32,3072]{1,0:T(8,128)S(1)} %collective-permute-done.24.kept_ref.refs_7_), custom_call_target="tpu_custom_call" | custom-call | flops 1000000000 | bytes 3600000 | tf_op jit(solution)/shard_map/pallas_call | solution.py:142
  29.5 5.0 %collective-permute-done.20.kept_ref.refs_4_ = f32[32,3072]{1,0:T(8,128)S(1)} collective-permute-done((f32[32,3072]{1,0:T(8,128)S(1)}, f32[32,3072]{1,0:T(8,128)S(1)}, u32[]{:S(2)}, u32[]{:S(2)}) %collective-permute-start.20) | collective-permute-done | bytes 393248 | tf_op jit(solution)/shard_map/ppermute | solution.py:380
  34.5 1.0 %shard_map.63.refs_4_ = f32[32,4096]{1,0:T(8,128)S(1)} custom-call(s32[1]{0:T(128)} %bitcast.2.me_ref, s32[8,32,128]{2,1,0:T(8,128)S(1)} %get-tuple-element.87.rank_ref, f32[32,3072]{1,0:T(8,128)S(1)} %collective-permute-done.20.kept_ref.refs_4_), custom_call_target="tpu_custom_call" | custom-call | flops 1000000000 | bytes 3600000 | tf_op jit(solution)/shard_map/pallas_call | solution.py:142
  35.5 1.0 %shard_map.62.refs_2_ = f32[32,4096]{1,0:T(8,128)S(1)} custom-call(s32[1]{0:T(128)} %bitcast.2.me_ref, s32[8,32,128]{2,1,0:T(8,128)S(1)} %get-tuple-element.87.rank_ref, f32[32,3072]{1,0:T(8,128)S(1)} %collective-permute-done.18.kept_ref.refs_2_), custom_call_target="tpu_custom_call" | custom-call | flops 1000000000 | bytes 3600000 | tf_op jit(solution)/shard_map/pallas_call | solution.py:142
  36.5 4.9 %collective-permute-done.21.refs_5_.kept_ref = f32[32,3072]{1,0:T(8,128)S(1)} collective-permute-done((f32[32,3072]{1,0:T(8,128)S(1)}, f32[32,3072]{1,0:T(8,128)S(1)}, u32[]{:S(2)}, u32[]{:S(2)}) %collective-permute-start.21) | collective-permute-done | bytes 393248 | tf_op jit(solution)/shard_map/ppermute | solution.py:380
  42.0 1.9 %shard_map.67 = (f32[136,128]{1,0:T(8,128)S(1)}, f32[136,128]{1,0:T(8,128)S(1)}) custom-call(s32[1]{0:T(128)} %bitcast.2.me_ref, f32[32,3072]{1,0:T(8,128)S(1)} %shard_map.56.refs_0_, f32[32,3072]{1,0:T(8,128)S(1)} %shard_map.57.refs_1_, f32[32,3072]{1,0:T(8,128)S(1)} %collective-permute-done.18.kept_ref.refs_2_, ...), custom_call_target="tpu_custom_call" | custom-call | flops 2000000000 | bytes 7200000 | tf_op jit(solution)/shard_map/pallas_call | solution.py:142
  44.2 1.0 %collective-permute-done.25 = f32[136,128]{1,0:T(8,128)S(1)} collective-permute-done((f32[136,128]{1,0:T(8,128)S(1)}, f32[136,128]{1,0:T(8,128)S(1)}, u32[]{:S(2)}, u32[]{:S(2)}) %collective-permute-start.25) | collective-permute-done | bytes 69664 | tf_op jit(solution)/shard_map/ppermute | solution.py:380
  45.2 2.8 %collective-permute-start.28 = (f32[136,128]{1,0:T(8,128)S(1)}, f32[136,128]{1,0:T(8,128)S(1)}, u32[]{:S(2)}, u32[]{:S(2)}) collective-permute-start(f32[136,128]{1,0:T(8,128)S(1)} %add.116), channel_id=1, source_target_pairs={{0,6},{1,7},{2,4},{3,5},{4,2},{5,3},{6,0},{7,1},{8,14},{9,15},{10,... | collective-permute-start | bytes 208904 | tf_op jit(solution)/shard_map/ppermute | solution.py:380
  48.8 1.2 %shard_map.68.refs_3_ = f32[32,4096]{1,0:T(8,128)S(1)} custom-call(s32[1]{0:T(128)} %bitcast.2.me_ref, s32[8,32,128]{2,1,0:T(8,128)S(1)} %get-tuple-element.87.rank_ref, f32[32,3072]{1,0:T(8,128)S(1)} %collective-permute-done.19.refs_3_.kept_ref), custom_call_target="tpu_custom_call" | custom-call | flops 1000000000 | bytes 3600000 | tf_op jit(solution)/shard_map/pallas_call | solution.py:142
  50.6 1.8 %collective-permute-done.27 = f32[136,128]{1,0:T(8,128)S(1)} collective-permute-done((f32[136,128]{1,0:T(8,128)S(1)}, f32[136,128]{1,0:T(8,128)S(1)}, u32[]{:S(2)}, u32[]{:S(2)}) %collective-permute-start.27) | collective-permute-done | bytes 69664 | tf_op jit(solution)/shard_map/ppermute | solution.py:380
  52.9 3.7 %collective-permute-start.31 = (f32[136,128]{1,0:T(8,128)S(1)}, f32[136,128]{1,0:T(8,128)S(1)}, u32[]{:S(2)}, u32[]{:S(2)}) collective-permute-start(f32[136,128]{1,0:T(8,128)S(1)} %add_add_fusion.3), channel_id=1, source_target_pairs={{0,24},{8,16},{16,8},{24,0},{1,25},{9,17},{17,9},{25,1},{2,26},{10... | collective-permute-start | bytes 208904 | tf_op jit(solution)/shard_map/ppermute | solution.py:380
  57.3 1.0 %shard_map.69.refs_5_ = f32[32,4096]{1,0:T(8,128)S(1)} custom-call(s32[1]{0:T(128)} %bitcast.2.me_ref, s32[8,32,128]{2,1,0:T(8,128)S(1)} %get-tuple-element.87.rank_ref, f32[32,3072]{1,0:T(8,128)S(1)} %collective-permute-done.21.refs_5_.kept_ref), custom_call_target="tpu_custom_call" | custom-call | flops 1000000000 | bytes 3600000 | tf_op jit(solution)/shard_map/pallas_call | solution.py:142
  58.3 1.3 %shard_map.70 = (bf16[256,4096]{1,0:T(8,128)(2,1)S(1)}, bf16[256,4096]{1,0:T(8,128)(2,1)S(1)}) custom-call(s32[1]{0:T(128)} %bitcast.2.me_ref, f32[32,4096]{1,0:T(8,128)S(1)} %get-tuple-element.83.refs_0_, f32[32,4096]{1,0:T(8,128)S(1)} %get-tuple-element.84.refs_1_, f32[32,4096]{1,0:T(8,128)S(1)} %shard_map.62.refs_2_, f32[32,4096]{1,0:T(8,128)S(1)} %shard_map.68.refs_3_, ...), custom_call_target="tpu_custom_call" | custom-call | flops 1000000000 | bytes 3600000 | tf_op jit(solution)/shard_map/pallas_call | solution.py:142
  59.6 2.1 %collective-permute-done.30 = f32[136,128]{1,0:T(8,128)S(1)} collective-permute-done((f32[136,128]{1,0:T(8,128)S(1)}, f32[136,128]{1,0:T(8,128)S(1)}, u32[]{:S(2)}, u32[]{:S(2)}) %collective-permute-start.30) | collective-permute-done | bytes 69664 | tf_op jit(solution)/shard_map/ppermute | solution.py:380
  63.1 9.6 %conditional.1 = ((f32[256,256]{1,0:T(8,128)}, f32[256,4096]{1,0:T(8,128)})) conditional(s32[]{:T(128)} %bitcast.13, (s32[]{:T(128)}, f32[136,128]{1,0:T(8,128)S(1)}, f32[136,128]{1,0:T(8,128)S(1)}, bf16[256,4096]{1,0:T(8,128)(2,1)S(1)}, bf16[256,4096]{1,0:T(8,128)(2,1)S(1)}) %tuple.25, (s32[]{:T(128)}, f32[32,32768]{1,0:T(8,128)}, ...), branch_computations={%region_1.0_spmd, %region_2.0_spmd} | conditional | flops 3001178624 | bytes 44425160 | solution.py:459
  63.1 9.4 %branch_0_fun.1 = (f32[256,256]{1,0:T(8,128)}, f32[256,4096]{1,0:T(8,128)}) custom-call(s32[1]{0:T(128)} %bitcast.me_ref, f32[136,128]{1,0:T(8,128)S(1)} %get-tuple-element.23.mine_ref, f32[136,128]{1,0:T(8,128)S(1)} %get-tuple-element.24.other_ref, bf16[256,4096]{1,0:T(8,128)(2,1)S(1)} %get-tuple-element.25.refs_0_, ...), custom_call_target="tpu_custom_call" | custom-call | tf_op jit(solution)/shard_map/cond/branch_0_fun/pallas_call | solution.py:367
  (46 shorter events, 15.0 us)
Async XLA Ops:
  0.6 5.1 %collective-permute-start.15 = (f32[256,128]{1,0:T(8,128)}, f32[256,128]{1,0:T(8,128)S(1)}, u32[]{:S(2)}, u32[]{:S(2)}) collective-permute-start(f32[256,128]{1,0:T(8,128)} %bitcast.23), channel_id=1, source_target_pairs={{0,1},{1,0},{2,3},{3,2},{4,5},{5,4},{6,7},{7,6},{8,9},{9,8},{10,11... | collective-permute-start | bytes 393224 | tf_op jit(solution)/shard_map/ppermute | solution.py:380
  2.2 11.2 %collective-permute-start.22 = (f32[32,2048]{1,0:T(8,128)S(1)}, f32[32,2048]{1,0:T(8,128)S(1)}, u32[]{:S(2)}, u32[]{:S(2)}) collective-permute-start(f32[32,2048]{1,0:T(8,128)S(1)} %get-tuple-element.118), channel_id=1, source_target_pairs={{0,6},{1,7},{2,4},{3,5},{4,2},{5,3},{6,0},{7,1},{8,14},{9,15},{10,... | collective-permute-start | bytes 786440 | tf_op jit(solution)/shard_map/ppermute | solution.py:380
  5.8 3.2 %copy-start = (f32[32,32768]{1,0:T(8,128)S(1)}, f32[32,32768]{1,0:T(8,128)}, u32[]{:S(2)}) copy-start(f32[32,32768]{1,0:T(8,128)} %param.5) | copy-start | bytes 12582916
  5.8 3.8 %copy-start.1 = (s32[32768]{0:T(1024)S(1)}, s32[32768]{0:T(1024)}, u32[]{:S(2)}) copy-start(s32[32768]{0:T(1024)} %param.6) | copy-start | bytes 393220
  5.8 3.8 %copy-start.2 = (f32[32768]{0:T(1024)S(1)}, f32[32768]{0:T(1024)}, u32[]{:S(2)}) copy-start(f32[32768]{0:T(1024)} %param.7) | copy-start | bytes 393220
  8.4 1.2 %collective-permute-start.16 = (f32[8,128]{1,0:T(8,128)S(1)}, f32[8,128]{1,0:T(8,128)S(1)}, u32[]{:S(2)}, u32[]{:S(2)}) collective-permute-start(f32[8,128]{1,0:T(8,128)S(1)} %get-tuple-element.70.refs_9_), channel_id=1, source_target_pairs={{0,1},{1,0},{2,3},{3,2},{4,5},{5,4},{6,7},{7,6},{8,9},{9,8},{10,11... | collective-permute-start | bytes 12296 | tf_op jit(solution)/shard_map/ppermute | solution.py:380
  8.6 8.7 %collective-permute-start.23 = (f32[32,1536]{1,0:T(8,128)S(1)}, f32[32,1536]{1,0:T(8,128)S(1)}, u32[]{:S(2)}, u32[]{:S(2)}) collective-permute-start(f32[32,1536]{1,0:T(8,128)S(1)} %get-tuple-element.76), channel_id=1, source_target_pairs={{0,6},{1,7},{2,4},{3,5},{4,2},{5,3},{6,0},{7,1},{8,14},{9,15},{10,... | collective-permute-start | bytes 589832 | tf_op jit(solution)/shard_map/ppermute | solution.py:380
  9.1 9.3 %collective-permute-start.17 = (f32[32,4096]{1,0:T(8,128)S(1)}, f32[32,4096]{1,0:T(8,128)S(1)}, u32[]{:S(2)}, u32[]{:S(2)}) collective-permute-start(f32[32,4096]{1,0:T(8,128)S(1)} %get-tuple-element.126), channel_id=1, source_target_pairs={{0,1},{1,0},{2,3},{3,2},{4,5},{5,4},{6,7},{7,6},{8,9},{9,8},{10,11... | collective-permute-start | bytes 1572872 | tf_op jit(solution)/shard_map/ppermute | solution.py:380
  10.5 16.1 %collective-permute-start.24 = (f32[32,3072]{1,0:T(8,128)S(1)}, f32[32,3072]{1,0:T(8,128)S(1)}, u32[]{:S(2)}, u32[]{:S(2)}) collective-permute-start(f32[32,3072]{1,0:T(8,128)S(1)} %shard_map.55), channel_id=1, source_target_pairs={{0,7},{1,6},{2,5},{3,4},{4,3},{5,2},{6,1},{7,0},{8,15},{9,14},{10,... | collective-permute-start | bytes 1179656 | tf_op jit(solution)/shard_map/ppermute | solution.py:380
  19.7 15.8 %collective-permute-start.18 = (f32[32,3072]{1,0:T(8,128)S(1)}, f32[32,3072]{1,0:T(8,128)S(1)}, u32[]{:S(2)}, u32[]{:S(2)}) collective-permute-start(f32[32,3072]{1,0:T(8,128)S(1)} %shard_map.58), channel_id=1, source_target_pairs={{0,2},{1,3},{2,0},{3,1},{4,6},{5,7},{6,4},{7,5},{8,10},{9,11},{10,... | collective-permute-start | bytes 1179656 | tf_op jit(solution)/shard_map/ppermute | solution.py:380
  22.4 12.1 %collective-permute-start.20 = (f32[32,3072]{1,0:T(8,128)S(1)}, f32[32,3072]{1,0:T(8,128)S(1)}, u32[]{:S(2)}, u32[]{:S(2)}) collective-permute-start(f32[32,3072]{1,0:T(8,128)S(1)} %shard_map.60), channel_id=1, source_target_pairs={{0,4},{1,5},{2,6},{3,7},{4,0},{5,1},{6,2},{7,3},{8,12},{9,13},{10,... | collective-permute-start | bytes 1179656 | tf_op jit(solution)/shard_map/ppermute | solution.py:380
  24.9 17.1 %collective-permute-start.19 = (f32[32,3072]{1,0:T(8,128)S(1)}, f32[32,3072]{1,0:T(8,128)S(1)}, u32[]{:S(2)}, u32[]{:S(2)}) collective-permute-start(f32[32,3072]{1,0:T(8,128)S(1)} %shard_map.59), channel_id=1, source_target_pairs={{0,3},{1,2},{2,1},{3,0},{4,7},{5,6},{6,5},{7,4},{8,11},{9,10},{10,... | collective-permute-start | bytes 1179656 | tf_op jit(solution)/shard_map/ppermute | solution.py:380
  26.0 15.4 %collective-permute-start.21 = (f32[32,3072]{1,0:T(8,128)S(1)}, f32[32,3072]{1,0:T(8,128)S(1)}, u32[]{:S(2)}, u32[]{:S(2)}) collective-permute-start(f32[32,3072]{1,0:T(8,128)S(1)} %shard_map.61), channel_id=1, source_target_pairs={{0,5},{1,4},{2,7},{3,6},{4,1},{5,0},{6,3},{7,2},{8,13},{9,12},{10,... | collective-permute-start | bytes 1179656 | tf_op jit(solution)/shard_map/ppermute | solution.py:380
  43.9 1.3 %collective-permute-start.25 = (f32[136,128]{1,0:T(8,128)S(1)}, f32[136,128]{1,0:T(8,128)S(1)}, u32[]{:S(2)}, u32[]{:S(2)}) collective-permute-start(f32[136,128]{1,0:T(8,128)S(1)} %get-tuple-element.79), channel_id=1, source_target_pairs={{0,1},{1,0},{2,3},{3,2},{4,5},{5,4},{6,7},{7,6},{8,9},{9,8},{10,11... | collective-permute-start | bytes 208904 | tf_op jit(solution)/shard_map/ppermute | solution.py:380
  45.2 5.3 %collective-permute-start.28 = (f32[136,128]{1,0:T(8,128)S(1)}, f32[136,128]{1,0:T(8,128)S(1)}, u32[]{:S(2)}, u32[]{:S(2)}) collective-permute-start(f32[136,128]{1,0:T(8,128)S(1)} %add.116), channel_id=1, source_target_pairs={{0,6},{1,7},{2,4},{3,5},{4,2},{5,3},{6,0},{7,1},{8,14},{9,15},{10,... | collective-permute-start | bytes 208904 | tf_op jit(solution)/shard_map/ppermute | solution.py:380
  48.0 4.3 %collective-permute-start.27 = (f32[136,128]{1,0:T(8,128)S(1)}, f32[136,128]{1,0:T(8,128)S(1)}, u32[]{:S(2)}, u32[]{:S(2)}) collective-permute-start(f32[136,128]{1,0:T(8,128)S(1)} %add.116), channel_id=1, source_target_pairs={{0,4},{1,5},{2,6},{3,7},{4,0},{5,1},{6,2},{7,3},{8,12},{9,13},{10,... | collective-permute-start | bytes 208904 | tf_op jit(solution)/shard_map/ppermute | solution.py:380
  48.5 4.3 %collective-permute-start.26 = (f32[136,128]{1,0:T(8,128)S(1)}, f32[136,128]{1,0:T(8,128)S(1)}, u32[]{:S(2)}, u32[]{:S(2)}) collective-permute-start(f32[136,128]{1,0:T(8,128)S(1)} %add.116), channel_id=1, source_target_pairs={{0,2},{1,3},{2,0},{3,1},{4,6},{5,7},{6,4},{7,5},{8,10},{9,11},{10,... | collective-permute-start | bytes 208904 | tf_op jit(solution)/shard_map/ppermute | solution.py:380
  52.9 6.7 %collective-permute-start.31 = (f32[136,128]{1,0:T(8,128)S(1)}, f32[136,128]{1,0:T(8,128)S(1)}, u32[]{:S(2)}, u32[]{:S(2)}) collective-permute-start(f32[136,128]{1,0:T(8,128)S(1)} %add_add_fusion.3), channel_id=1, source_target_pairs={{0,24},{8,16},{16,8},{24,0},{1,25},{9,17},{17,9},{25,1},{2,26},{10... | collective-permute-start | bytes 208904 | tf_op jit(solution)/shard_map/ppermute | solution.py:380
  56.5 5.2 %collective-permute-start.30 = (f32[136,128]{1,0:T(8,128)S(1)}, f32[136,128]{1,0:T(8,128)S(1)}, u32[]{:S(2)}, u32[]{:S(2)}) collective-permute-start(f32[136,128]{1,0:T(8,128)S(1)} %add_add_fusion.3), channel_id=1, source_target_pairs={{0,16},{8,24},{16,0},{24,8},{1,17},{9,25},{17,1},{25,9},{2,18},{10... | collective-permute-start | bytes 208904 | tf_op jit(solution)/shard_map/ppermute | solution.py:380
  56.5 5.2 %collective-permute-start.29 = (f32[136,128]{1,0:T(8,128)S(1)}, f32[136,128]{1,0:T(8,128)S(1)}, u32[]{:S(2)}, u32[]{:S(2)}) collective-permute-start(f32[136,128]{1,0:T(8,128)S(1)} %add_add_fusion.3), channel_id=1, source_target_pairs={{0,8},{8,0},{16,24},{24,16},{1,9},{9,1},{17,25},{25,17},{2,10},{10... | collective-permute-start | bytes 208904 | tf_op jit(solution)/shard_map/ppermute | solution.py:380
  61.8 1.3 %collective-permute-start.32 = (f32[136,128]{1,0:T(8,128)S(1)}, f32[136,128]{1,0:T(8,128)S(1)}, u32[]{:S(2)}, u32[]{:S(2)}) collective-permute-start(f32[136,128]{1,0:T(8,128)S(1)} %add_add_fusion.2), channel_id=1, source_target_pairs={{0,1},{1,0},{2,3},{3,2},{4,5},{5,4},{6,7},{7,6},{8,9},{9,8},{10,11... | collective-permute-start | bytes 208904 | tf_op jit(solution)/shard_map/ppermute | solution.py:380
